TPU v7x, 128 devices: a whole 4x4x4 slice. The times are simulated.
128 devices in a mesh: dp: 4 (over y), ep: 8 (over x, core), tp: 4 (over z).
Axes of the slice: x: 4, y: 4, z: 4, core: 2. Of those that a mesh axis runs over, the one named last changes fastest.
Arguments:
- inputs: bfloat16 [8, 1024, 768], P('dp', 'ep'), may hold values from -6 to 6
- lengths: int32 [8], P('dp'), may hold values from 256 to 1024, as said below
- expert_ids: int32 [2, 8, 1024, 2], P(None, 'dp', 'ep'), may hold values from 0 to 15, as said below
- slot_ids: int32 [2, 8, 1024, 2], P(None, 'dp', 'ep'), may hold values from 0 to 32, as said below
- attn_gain: bfloat16 [2, 768], P(None, ('dp', 'ep')), may hold values from 0.5 to 1.5
- query_weight: bfloat16 [2, 768, 768], P(None, ('dp', 'ep'), 'tp'), may hold values from -0.21875 to 0.21875
- key_weight: bfloat16 [2, 768, 768], P(None, ('dp', 'ep'), 'tp'), may hold values from -0.21875 to 0.21875
- value_weight: bfloat16 [2, 768, 768], P(None, ('dp', 'ep'), 'tp'), may hold values from -0.21875 to 0.21875
- out_weight: bfloat16 [2, 768, 768], P(None, ('dp', 'ep'), 'tp'), may hold values from -1.75 to 1.75
- ffn_gain: bfloat16 [2, 768], P(None, ('dp', 'ep')), may hold values from 0.5 to 1.5
- router_weight: bfloat16 [2, 768, 16], P(None, ('dp', 'ep')), may hold values from -0.15625 to 0.15625
- dense_gate: bfloat16 [2, 768, 2048], P(None, ('dp', 'ep'), 'tp'), may hold values from -0.21875 to 0.21875
- dense_up: bfloat16 [2, 768, 2048], P(None, ('dp', 'ep'), 'tp'), may hold values from -0.21875 to 0.21875
- dense_down: bfloat16 [2, 768, 2048], P(None, ('dp', 'ep'), 'tp'), may hold values from -0.125 to 0.125
- expert_gate: bfloat16 [2, 16, 768, 2048], P(None, 'ep', None, 'tp'), may hold values from -0.21875 to 0.21875
- expert_up: bfloat16 [2, 16, 768, 2048], P(None, 'ep', None, 'tp'), may hold values from -0.21875 to 0.21875
- expert_down: bfloat16 [2, 16, 2048, 768], P(None, 'ep', 'tp'), may hold values from -0.125 to 0.125
- cotangent: bfloat16 [8, 1024, 768], P('dp', 'ep'), may hold values from -6 to 6
Outputs:
- outputs: float32 [8, 1024, 768], P('dp', 'ep')
- input_grad: float32 [8, 1024, 768], P('dp', 'ep')
- attn_gain_grad: float32 [2, 768], P(None, ('dp', 'ep'))
- query_grad: float32 [2, 768, 768], P(None, ('dp', 'ep'), 'tp')
- key_grad: float32 [2, 768, 768], P(None, ('dp', 'ep'), 'tp')
- value_grad: float32 [2, 768, 768], P(None, ('dp', 'ep'), 'tp')
- out_grad: float32 [2, 768, 768], P(None, ('dp', 'ep'), 'tp')
- ffn_gain_grad: float32 [2, 768], P(None, ('dp', 'ep'))
- router_grad: float32 [2, 768, 16], P(None, ('dp', 'ep'))
- dense_gate_grad: float32 [2, 768, 2048], P(None, ('dp', 'ep'), 'tp')
- dense_up_grad: float32 [2, 768, 2048], P(None, ('dp', 'ep'), 'tp')
- dense_down_grad: float32 [2, 768, 2048], P(None, ('dp', 'ep'), 'tp')
- expert_gate_grad: float32 [2, 16, 768, 2048], P(None, 'ep', None, 'tp')
- expert_up_grad: float32 [2, 16, 768, 2048], P(None, 'ep', None, 'tp')
- expert_down_grad: float32 [2, 16, 2048, 768], P(None, 'ep', 'tp')
Inputs may be any that keep to these rules, and one draw needn't show every extreme that they name: `lengths`: in each group of 2 sequences of one dp index, one sequence, drawn, has length 1024. `expert_ids`: each token names two different experts in each block. `slot_ids`: within one block and one row block (the 256 tokens of one dp and ep index), the pairs (token, choice) of one expert, in order of tokens and then choices, get slots 0, 1, 2 and so on; a pair that finds all 32 slots taken gets 32 and is dropped. In every draw and block some expert fills all 32 slots of every row block of its dp index.
All inputs are finite; a program needn't handle non-finite values.
Results may differ from a plain program's by a relative error of at most 0.038.
Values may be sent and summed in bfloat16 or wider, within the bound.
A program may use at most 256 MiB of HBM per device.

v0:
```python
import jax
import jax.numpy as jnp
from jax import lax
from jax.sharding import PartitionSpec as P

HD = 64


epsilon = 1e-06


def normalize(values, gain):
    return values * lax.rsqrt(jnp.mean(values * values, axis=-1, keepdims=True) + epsilon) * gain


def rotate(values, positions, turn_sign):
    half_dim = values.shape[-1] // 2
    frequency = jnp.exp(-jnp.log(10000.0) * jnp.arange(half_dim).astype(jnp.float32) / half_dim)
    angles = positions[:, None] * frequency[None, :]
    cosine = jnp.cos(angles)[:, None, :]
    sine_part = turn_sign * jnp.sin(angles)[:, None, :]
    front_half = values[..., :half_dim]
    back_half = values[..., half_dim:]
    return jnp.concatenate(
        [front_half * cosine - back_half * sine_part, back_half * cosine + front_half * sine_part],
        axis=-1,
    )


def swish_product(gate_pre, up_pre):
    return jax.nn.silu(gate_pre) * up_pre


def padded_rows(slots):
    flat_rows = slots.reshape(slots.shape[0] * slots.shape[1], slots.shape[2])
    return jnp.concatenate([flat_rows, jnp.zeros((1, slots.shape[2]), slots.dtype)], axis=0)


def shards(
    inputs,
    lengths,
    expert_ids,
    slot_ids,
    attn_gain,
    query_weight,
    key_weight,
    value_weight,
    out_weight,
    ffn_gain,
    router_weight,
    dense_gate,
    dense_up,
    dense_down,
    expert_gate,
    expert_up,
    expert_down,
    cotangent,
):
    seq_count, span, width = inputs.shape
    rows = seq_count * span
    depth_count = attn_gain.shape[0]
    ep_count = lax.axis_size("ep")
    experts_all = expert_gate.shape[1] * ep_count
    capacity = 2 * rows // experts_all
    full_len = span * ep_count
    query_places = lax.axis_index("ep") * span + jnp.arange(span)
    query_pos = query_places.astype(jnp.float32)
    key_places = jnp.arange(full_len)
    allowed = (key_places[None, None, :] <= query_places[None, :, None]) & (
        key_places[None, None, :] < lengths[:, None, None]
    )
    scale = HD ** (-0.5)
    expert_range = jnp.arange(experts_all)
    slot_range = jnp.arange(capacity)

    def masked_scores(queries, key_heads):
        scores = (
            jnp.einsum("sqhd,skhd->shqk", queries, key_heads, preferred_element_type=jnp.float32)
            * scale
        )
        return jnp.where(allowed[:, None], scores, -1e30)

    gathered = (
        lax.all_gather(attn_gain, ("dp", "ep"), axis=1, tiled=True),
        lax.all_gather(query_weight, ("dp", "ep"), axis=1, tiled=True),
        lax.all_gather(key_weight, ("dp", "ep"), axis=1, tiled=True),
        lax.all_gather(value_weight, ("dp", "ep"), axis=1, tiled=True),
        lax.all_gather(out_weight, ("dp", "ep"), axis=1, tiled=True),
        lax.all_gather(ffn_gain, ("dp", "ep"), axis=1, tiled=True),
        lax.all_gather(router_weight, ("dp", "ep"), axis=1, tiled=True),
        lax.all_gather(dense_gate, ("dp", "ep"), axis=1, tiled=True),
        lax.all_gather(dense_up, ("dp", "ep"), axis=1, tiled=True),
        lax.all_gather(dense_down, ("dp", "ep"), axis=1, tiled=True),
    )
    stream = inputs.astype(jnp.float32).reshape(rows, width)
    saved = []
    for depth in range(depth_count):
        norm_one, w_query, w_key, w_value, w_out, norm_two, w_router, w_dgate, w_dup, w_ddown = [
            weight[depth] for weight in gathered
        ]
        normed = normalize(stream, norm_one.astype(jnp.float32)).astype(jnp.bfloat16)
        query_lin = jnp.dot(normed, w_query, preferred_element_type=jnp.float32)
        key_lin = jnp.dot(normed, w_key, preferred_element_type=jnp.float32)
        value_lin = jnp.dot(normed, w_value, preferred_element_type=jnp.float32)
        heads_here = query_lin.shape[1] // HD
        queries = rotate(query_lin.reshape(seq_count, span, heads_here, HD), query_pos, 1.0).astype(
            jnp.bfloat16
        )
        keys_rot = rotate(key_lin.reshape(seq_count, span, heads_here, HD), query_pos, 1.0).astype(
            jnp.bfloat16
        )
        values_low = value_lin.reshape(seq_count, span, heads_here * HD).astype(jnp.bfloat16)
        keys_all, values_all = (
            lax.all_gather(
                keys_rot.reshape(seq_count, span, heads_here * HD), "ep", axis=1, tiled=True
            ),
            lax.all_gather(values_low, "ep", axis=1, tiled=True),
        )
        key_heads = keys_all.reshape(seq_count, full_len, heads_here, HD)
        value_heads = values_all.reshape(seq_count, full_len, heads_here, HD)
        scores = masked_scores(queries, key_heads)
        row_max = jnp.max(scores, axis=-1, keepdims=True)
        expd = jnp.exp(scores - row_max)
        total = jnp.sum(expd, axis=-1, keepdims=True)
        probs = expd / total
        log_total = row_max + jnp.log(total)
        attended = jnp.einsum(
            "shqk,skhd->sqhd",
            probs.astype(jnp.bfloat16),
            value_heads,
            preferred_element_type=jnp.float32,
        )
        attended_low = attended.reshape(rows, heads_here * HD).astype(jnp.bfloat16)
        attn_part = jnp.einsum("rh,dh->rd", attended_low, w_out, preferred_element_type=jnp.float32)
        middle = stream + lax.psum(attn_part.astype(jnp.bfloat16), "tp").astype(jnp.float32)
        ffn_in = normalize(middle, norm_two.astype(jnp.float32)).astype(jnp.bfloat16)
        logits = jnp.dot(ffn_in, w_router, preferred_element_type=jnp.float32)
        gate_dense = jnp.dot(ffn_in, w_dgate, preferred_element_type=jnp.float32)
        up_dense = jnp.dot(ffn_in, w_dup, preferred_element_type=jnp.float32)
        hidden_dense = swish_product(gate_dense, up_dense).astype(jnp.bfloat16)
        dense_part = jnp.einsum(
            "rf,df->rd", hidden_dense, w_ddown, preferred_element_type=jnp.float32
        )
        route_now = expert_ids[depth].reshape(rows, 2)
        slot_now = slot_ids[depth].reshape(rows, 2)
        pair_index = jnp.where(
            slot_now < capacity, route_now * capacity + slot_now, experts_all * capacity
        )
        pick_expert = (route_now[:, :, None] == expert_range).astype(jnp.float32)
        pick_slot = (slot_now[:, :, None] == slot_range).astype(jnp.bfloat16)
        placed = jnp.sum(
            pick_expert.astype(jnp.bfloat16)[:, :, :, None] * pick_slot[:, :, None, :], axis=1
        )
        chosen = jnp.sum(pick_expert * logits[:, None, :], axis=-1)
        shares = jax.nn.softmax(chosen, axis=-1)
        sent = jnp.einsum("rec,rd->ecd", placed, ffn_in, preferred_element_type=jnp.float32).astype(
            jnp.bfloat16
        )
        arrived = lax.all_to_all(sent, "ep", split_axis=0, concat_axis=1, tiled=True)
        gate_exp = jnp.einsum(
            "ecd,edf->ecf", arrived, expert_gate[depth], preferred_element_type=jnp.float32
        )
        up_exp = jnp.einsum(
            "ecd,edf->ecf", arrived, expert_up[depth], preferred_element_type=jnp.float32
        )
        hidden_exp = swish_product(gate_exp, up_exp).astype(jnp.bfloat16)
        out_exp = jnp.einsum(
            "ecf,efd->ecd", hidden_exp, expert_down[depth], preferred_element_type=jnp.float32
        )
        returned = lax.all_to_all(
            out_exp.astype(jnp.bfloat16), "ep", split_axis=1, concat_axis=0, tiled=True
        ).astype(out_exp.dtype)
        picked_rows = padded_rows(returned)[pair_index]
        moe_part = jnp.sum(shares[:, :, None] * picked_rows, axis=1)
        ffn_sum = lax.psum((dense_part + moe_part).astype(jnp.bfloat16), "tp").astype(jnp.float32)
        saved.append(
            (
                stream,
                normed,
                queries,
                key_heads,
                value_heads,
                log_total,
                attended_low,
                middle,
                ffn_in,
                gate_dense,
                up_dense,
                hidden_dense,
                pick_expert,
                pair_index,
                shares,
                arrived,
                gate_exp,
                up_exp,
                hidden_exp,
                picked_rows,
            )
        )
        stream = middle + ffn_sum
    outputs = stream
    shared_parts = [[None] * depth_count for column in range(10)]
    expert_parts = [[None] * depth_count for column in range(3)]
    grad_stream = cotangent.astype(jnp.float32).reshape(rows, width)
    for depth in reversed(range(depth_count)):
        norm_one, w_query, w_key, w_value, w_out, norm_two, w_router, w_dgate, w_dup, w_ddown = [
            weight[depth] for weight in gathered
        ]
        (
            stream_in,
            normed,
            queries,
            key_heads,
            value_heads,
            log_total,
            attended_low,
            middle,
            ffn_in,
            gate_dense,
            up_dense,
            hidden_dense,
            pick_expert,
            pair_index,
            shares,
            arrived,
            gate_exp,
            up_exp,
            hidden_exp,
            picked_rows,
        ) = saved[depth]
        heads_here = queries.shape[2]
        ffn_grad = grad_stream.astype(jnp.bfloat16)
        ffn_grad_wide = ffn_grad.astype(jnp.float32)
        hidden_dense_grad = jnp.einsum(
            "rd,df->rf", ffn_grad, w_ddown, preferred_element_type=jnp.float32
        )
        gate_dense_grad, up_dense_grad = jax.vjp(swish_product, gate_dense, up_dense)[1](
            hidden_dense_grad
        )
        gate_dense_grad = gate_dense_grad.astype(jnp.bfloat16)
        up_dense_grad = up_dense_grad.astype(jnp.bfloat16)
        shared_parts[9][depth] = jnp.einsum(
            "rd,rf->df", ffn_grad, hidden_dense, preferred_element_type=jnp.float32
        )
        shared_parts[7][depth] = jnp.einsum(
            "rd,rf->df", ffn_in, gate_dense_grad, preferred_element_type=jnp.float32
        )
        shared_parts[8][depth] = jnp.einsum(
            "rd,rf->df", ffn_in, up_dense_grad, preferred_element_type=jnp.float32
        )
        dense_input = jnp.einsum(
            "rf,df->rd", gate_dense_grad, w_dgate, preferred_element_type=jnp.float32
        )
        dense_input = dense_input + jnp.einsum(
            "rf,df->rd", up_dense_grad, w_dup, preferred_element_type=jnp.float32
        )
        weighted = shares[:, :, None] * ffn_grad_wide[:, None, :]
        slot_flat = (
            jnp.zeros((experts_all * capacity + 1, width), jnp.float32)
            .at[pair_index.reshape(rows * 2)]
            .add(weighted.reshape(rows * 2, width))
        )
        slot_grad = (
            slot_flat[: experts_all * capacity]
            .reshape(experts_all, capacity, width)
            .astype(jnp.bfloat16)
        )
        share_part = jnp.sum(ffn_grad_wide[:, None, :] * picked_rows, axis=-1)
        back_arrived = lax.all_to_all(slot_grad, "ep", split_axis=0, concat_axis=1, tiled=True)
        hidden_exp_grad = jnp.einsum(
            "ecd,efd->ecf", back_arrived, expert_down[depth], preferred_element_type=jnp.float32
        )
        gate_exp_grad, up_exp_grad = jax.vjp(swish_product, gate_exp, up_exp)[1](hidden_exp_grad)
        gate_exp_grad = gate_exp_grad.astype(jnp.bfloat16)
        up_exp_grad = up_exp_grad.astype(jnp.bfloat16)
        down_part = jnp.einsum(
            "ecf,ecd->efd", hidden_exp, back_arrived, preferred_element_type=jnp.float32
        )
        gate_part = jnp.einsum(
            "ecd,ecf->edf", arrived, gate_exp_grad, preferred_element_type=jnp.float32
        )
        up_part = jnp.einsum(
            "ecd,ecf->edf", arrived, up_exp_grad, preferred_element_type=jnp.float32
        )
        expert_parts[0][depth] = gate_part
        expert_parts[1][depth] = up_part
        expert_parts[2][depth] = down_part
        arrived_grad = jnp.einsum(
            "ecf,edf->ecd", gate_exp_grad, expert_gate[depth], preferred_element_type=jnp.float32
        )
        arrived_grad = arrived_grad + jnp.einsum(
            "ecf,edf->ecd", up_exp_grad, expert_up[depth], preferred_element_type=jnp.float32
        )
        sent_grad = lax.all_to_all(
            arrived_grad.astype(jnp.bfloat16), "ep", split_axis=1, concat_axis=0, tiled=True
        ).astype(arrived_grad.dtype)
        moe_input = jnp.sum(padded_rows(sent_grad)[pair_index], axis=1)
        input_sum, share_grad = (
            lax.psum((dense_input + moe_input).astype(jnp.bfloat16), "tp").astype(jnp.float32),
            lax.psum(share_part.astype(jnp.bfloat16), "tp").astype(jnp.float32),
        )
        chosen_grad = shares * (share_grad - jnp.sum(shares * share_grad, axis=-1, keepdims=True))
        logit_grad = jnp.sum(chosen_grad[:, :, None] * pick_expert, axis=1).astype(jnp.bfloat16)
        shared_parts[6][depth] = jnp.einsum(
            "rd,re->de", ffn_in, logit_grad, preferred_element_type=jnp.float32
        )
        ffn_in_grad = input_sum + jnp.einsum(
            "re,de->rd", logit_grad, w_router, preferred_element_type=jnp.float32
        )
        middle_norm_grad, gain_two_grad = jax.vjp(normalize, middle, norm_two.astype(jnp.float32))[
            1
        ](ffn_in_grad)
        shared_parts[5][depth] = gain_two_grad
        middle_grad = grad_stream + middle_norm_grad
        attn_grad = middle_grad.astype(jnp.bfloat16)
        shared_parts[4][depth] = jnp.einsum(
            "rd,rh->dh", attn_grad, attended_low, preferred_element_type=jnp.float32
        )
        attended_grad = jnp.einsum(
            "rd,dh->rh", attn_grad, w_out, preferred_element_type=jnp.float32
        ).astype(jnp.bfloat16)
        attended_grad = attended_grad.reshape(seq_count, span, heads_here, HD)
        probs = jnp.exp(masked_scores(queries, key_heads) - log_total)
        probs_grad = jnp.einsum(
            "sqhd,skhd->shqk", attended_grad, value_heads, preferred_element_type=jnp.float32
        )
        score_grad = (
            probs * (probs_grad - jnp.sum(probs * probs_grad, axis=-1, keepdims=True))
        ).astype(jnp.bfloat16)
        queries_grad = (
            jnp.einsum("shqk,skhd->sqhd", score_grad, key_heads, preferred_element_type=jnp.float32)
            * scale
        )
        keys_grad_all = (
            jnp.einsum("shqk,sqhd->skhd", score_grad, queries, preferred_element_type=jnp.float32)
            * scale
        )
        values_grad_all = jnp.einsum(
            "shqk,sqhd->skhd",
            probs.astype(jnp.bfloat16),
            attended_grad,
            preferred_element_type=jnp.float32,
        )
        keys_grad, values_grad = (
            lax.psum_scatter(
                keys_grad_all.reshape(seq_count, full_len, heads_here * HD).astype(jnp.bfloat16),
                "ep",
                scatter_dimension=1,
                tiled=True,
            ).astype(jnp.float32),
            lax.psum_scatter(
                values_grad_all.reshape(seq_count, full_len, heads_here * HD).astype(jnp.bfloat16),
                "ep",
                scatter_dimension=1,
                tiled=True,
            ).astype(jnp.float32),
        )
        query_lin_grad = (
            rotate(queries_grad, query_pos, -1.0)
            .reshape(rows, heads_here * HD)
            .astype(jnp.bfloat16)
        )
        key_lin_grad = (
            rotate(keys_grad.reshape(seq_count, span, heads_here, HD), query_pos, -1.0)
            .reshape(rows, heads_here * HD)
            .astype(jnp.bfloat16)
        )
        value_lin_grad = values_grad.reshape(rows, heads_here * HD).astype(jnp.bfloat16)
        shared_parts[1][depth] = jnp.einsum(
            "rd,rh->dh", normed, query_lin_grad, preferred_element_type=jnp.float32
        )
        shared_parts[2][depth] = jnp.einsum(
            "rd,rh->dh", normed, key_lin_grad, preferred_element_type=jnp.float32
        )
        shared_parts[3][depth] = jnp.einsum(
            "rd,rh->dh", normed, value_lin_grad, preferred_element_type=jnp.float32
        )
        normed_part = jnp.einsum(
            "rh,dh->rd", query_lin_grad, w_query, preferred_element_type=jnp.float32
        )
        normed_part = normed_part + jnp.einsum(
            "rh,dh->rd", key_lin_grad, w_key, preferred_element_type=jnp.float32
        )
        normed_part = normed_part + jnp.einsum(
            "rh,dh->rd", value_lin_grad, w_value, preferred_element_type=jnp.float32
        )
        normed_grad = lax.psum(normed_part.astype(jnp.bfloat16), "tp").astype(jnp.float32)
        stream_norm_grad, gain_one_grad = jax.vjp(
            normalize, stream_in, norm_one.astype(jnp.float32)
        )[1](normed_grad)
        shared_parts[0][depth] = gain_one_grad
        grad_stream = middle_grad + stream_norm_grad
    stacked = [jnp.stack(column) for column in shared_parts]
    summed = (
        lax.psum_scatter(
            stacked[0].astype(jnp.bfloat16), ("dp", "ep"), scatter_dimension=1, tiled=True
        ).astype(jnp.float32),
        lax.psum_scatter(
            stacked[1].astype(jnp.bfloat16), ("dp", "ep"), scatter_dimension=1, tiled=True
        ).astype(jnp.float32),
        lax.psum_scatter(
            stacked[2].astype(jnp.bfloat16), ("dp", "ep"), scatter_dimension=1, tiled=True
        ).astype(jnp.float32),
        lax.psum_scatter(
            stacked[3].astype(jnp.bfloat16), ("dp", "ep"), scatter_dimension=1, tiled=True
        ).astype(jnp.float32),
        lax.psum_scatter(
            stacked[4].astype(jnp.bfloat16), ("dp", "ep"), scatter_dimension=1, tiled=True
        ).astype(jnp.float32),
        lax.psum_scatter(
            stacked[5].astype(jnp.bfloat16), ("dp", "ep"), scatter_dimension=1, tiled=True
        ).astype(jnp.float32),
        lax.psum_scatter(
            stacked[6].astype(jnp.bfloat16), ("dp", "ep"), scatter_dimension=1, tiled=True
        ).astype(jnp.float32),
        lax.psum_scatter(
            stacked[7].astype(jnp.bfloat16), ("dp", "ep"), scatter_dimension=1, tiled=True
        ).astype(jnp.float32),
        lax.psum_scatter(
            stacked[8].astype(jnp.bfloat16), ("dp", "ep"), scatter_dimension=1, tiled=True
        ).astype(jnp.float32),
        lax.psum_scatter(
            stacked[9].astype(jnp.bfloat16), ("dp", "ep"), scatter_dimension=1, tiled=True
        ).astype(jnp.float32),
    )
    expert_sums = (
        lax.psum(jnp.stack(expert_parts[0]).astype(jnp.bfloat16), "dp").astype(jnp.float32),
        lax.psum(jnp.stack(expert_parts[1]).astype(jnp.bfloat16), "dp").astype(jnp.float32),
        lax.psum(jnp.stack(expert_parts[2]).astype(jnp.bfloat16), "dp").astype(jnp.float32),
    )
    outputs = outputs.reshape(seq_count, span, width)
    input_grad = grad_stream.reshape(seq_count, span, width)
    return (
        outputs,
        input_grad,
        summed[0],
        summed[1],
        summed[2],
        summed[3],
        summed[4],
        summed[5],
        summed[6],
        summed[7],
        summed[8],
        summed[9],
        expert_sums[0],
        expert_sums[1],
        expert_sums[2],
    )


def solution(mesh):
    return jax.shard_map(
        shards,
        mesh=mesh,
        in_specs=(
            P("dp", "ep", None),
            P("dp"),
            P(None, "dp", "ep", None),
            P(None, "dp", "ep", None),
            P(None, ("dp", "ep")),
            P(None, ("dp", "ep"), "tp"),
            P(None, ("dp", "ep"), "tp"),
            P(None, ("dp", "ep"), "tp"),
            P(None, ("dp", "ep"), "tp"),
            P(None, ("dp", "ep")),
            P(None, ("dp", "ep"), None),
            P(None, ("dp", "ep"), "tp"),
            P(None, ("dp", "ep"), "tp"),
            P(None, ("dp", "ep"), "tp"),
            P(None, "ep", None, "tp"),
            P(None, "ep", None, "tp"),
            P(None, "ep", "tp", None),
            P("dp", "ep", None),
        ),
        out_specs=(
            P("dp", "ep", None),
            P("dp", "ep", None),
            P(None, ("dp", "ep")),
            P(None, ("dp", "ep"), "tp"),
            P(None, ("dp", "ep"), "tp"),
            P(None, ("dp", "ep"), "tp"),
            P(None, ("dp", "ep"), "tp"),
            P(None, ("dp", "ep")),
            P(None, ("dp", "ep"), None),
            P(None, ("dp", "ep"), "tp"),
            P(None, ("dp", "ep"), "tp"),
            P(None, ("dp", "ep"), "tp"),
            P(None, "ep", None, "tp"),
            P(None, "ep", None, "tp"),
            P(None, "ep", "tp", None),
        ),
        check_vma=False,
    )
```

profile of v0, /device:TPU:1, one launch (start us, length us, event | category | flops | bytes accessed | tf_op | source)
XLA Modules:
  0.0 1704.1 jit_solution(4424376036920871792)
XLA Ops:
  8.1 26.6 %all_gather.48 = bf16[2,768,192]{2,1,0:T(8,128)(2,1)S(1)} all-gather(bf16[2,24,192]{2,1,0:T(8,128)(2,1)} %param.26), channel_id=1, replica_groups=mesh['dp'=4,'ep'=8,'tp'=4] {'dp','ep'}, dimensions={1}, use_global_device_ids=true | all-gather | bytes 608256 | tf_op jit(solution)/shard_map/all_gather | solution.py:88
  34.7 20.5 %all-gather = bf16[32,24,2]{1,2,0:T(2,128)(2,1)S(1)} all-gather(bf16[1,24,2]{1,2,0:T(2,128)(2,1)} %bitcast.623), channel_id=1, replica_groups=mesh['dp'=4,'ep'=8,'tp'=4] {'dp','ep'}, dimensions={0}, use_global_device_ids=true | all-gather | bytes 3168 | tf_op jit(solution)/shard_map/all_gather | solution.py:84
  57.3 22.8 %all_gather.43 = bf16[2,768,192]{2,0,1:T(2,128)(2,1)S(1)} all-gather(bf16[2,24,192]{2,0,1:T(2,128)(2,1)S(1)} %copy.293), channel_id=1, replica_groups=mesh['dp'=4,'ep'=8,'tp'=4] {'dp','ep'}, dimensions={1}, use_global_device_ids=true | all-gather | bytes 608256 | tf_op jit(solution)/shard_map/all_gather | solution.py:87
  83.1 13.0 all_gather.44
  96.1 25.0 %all_gather.45 = bf16[2,768,192]{2,1,0:T(8,128)(2,1)S(1)} all-gather(bf16[2,24,192]{2,1,0:T(8,128)(2,1)S(1)} %copy-done.171), channel_id=1, replica_groups=mesh['dp'=4,'ep'=8,'tp'=4] {'dp','ep'}, dimensions={1}, use_global_device_ids=true | all-gather | bytes 608256 | tf_op jit(solution)/shard_map/all_gather | solution.py:85
  124.2 22.7 %all_gather.46 = bf16[2,768,192]{2,1,0:T(8,128)(2,1)S(1)} all-gather(bf16[2,24,192]{2,1,0:T(8,128)(2,1)S(1)} %copy-done.172), channel_id=1, replica_groups=mesh['dp'=4,'ep'=8,'tp'=4] {'dp','ep'}, dimensions={1}, use_global_device_ids=true | all-gather | bytes 608256 | tf_op jit(solution)/shard_map/all_gather | solution.py:86
  151.2 13.6 all_gather.47
  171.0 21.4 %all-gather.1 = bf16[32,24,2]{1,2,0:T(2,128)(2,1)S(1)} all-gather(bf16[1,24,2]{1,2,0:T(2,128)(2,1)S(1)} %bitcast.624), channel_id=1, replica_groups=mesh['dp'=4,'ep'=8,'tp'=4] {'dp','ep'}, dimensions={0}, use_global_device_ids=true | all-gather | bytes 3168 | tf_op jit(solution)/shard_map/all_gather | solution.py:89
  193.4 18.4 %all-reduce.25.cloned.1.call-done = bf16[256,768]{1,0:T(8,128)(2,1)} async-done(((bf16[256,768]{1,0:T(8,128)(2,1)}), bf16[256,768]{1,0:T(8,128)(2,1)}) %all-reduce.25.cloned.1.call-update) | async-done | bytes 393232 | tf_op jit(solution)/shard_map/psum | solution.py:135
  215.5 6.9 all-to-all-start
  223.9 28.7 %all_gather.53 = bf16[2,768,16]{2,0,1:T(2,128)(2,1)S(1)} all-gather(bf16[2,24,16]{2,0,1:T(2,128)(2,1)S(1)} %copy.299), channel_id=1, replica_groups=mesh['dp'=4,'ep'=8,'tp'=4] {'dp','ep'}, dimensions={1}, use_global_device_ids=true | all-gather | bytes 50688 | tf_op jit(solution)/shard_map/all_gather | solution.py:90
  261.7 4.1 all-to-all-start.1
  267.6 10.6 all-to-all-done.1
  283.3 2.8 multiply_reduce_fusion.5
  290.9 17.1 %all-gather.10.cloned.1.call-done = bf16[2,768,512]{2,1,0:T(8,128)(2,1)} async-done(((bf16[2,24,512]{2,1,0:T(8,128)(2,1)}), bf16[2,768,512]{2,1,0:T(8,128)(2,1)}) %all-gather.10.cloned.1.call-update) | async-done | bytes 1572880 | tf_op jit(solution)/shard_map/all_gather | solution.py:93
  320.2 29.6 %all-reduce.27.cloned.1.call-done = bf16[256,768]{1,0:T(8,128)(2,1)} async-done(((bf16[256,768]{1,0:T(8,128)(2,1)}), bf16[256,768]{1,0:T(8,128)(2,1)}) %all-reduce.27.cloned.1.call-update) | async-done | bytes 393232 | tf_op jit(solution)/shard_map/psum | solution.py:175
  351.9 16.8 all_gather.54
  369.5 13.6 all_gather.55
  387.8 40.2 %all-reduce.29.cloned.1.call-done = bf16[256,768]{1,0:T(8,128)(2,1)} async-done(((bf16[256,768]{1,0:T(8,128)(2,1)}), bf16[256,768]{1,0:T(8,128)(2,1)}) %all-reduce.29.cloned.1.call-update) | async-done | bytes 393232 | tf_op jit(solution)/shard_map/psum | solution.py:135
  430.0 6.1 scatter_custom_fusion
  438.5 7.1 all-to-all-start.4
  447.5 10.3 all-to-all-done.4
  457.8 5.0 all-to-all-start.2
  470.1 5.1 all-to-all-done.2
  483.3 5.4 all-to-all-start.3
  488.8 2.8 multiply_convert_fusion.12
  495.9 5.2 all-to-all-done.3
  501.1 5.0 all-to-all-start.5
  513.6 4.9 multiply_reduce_fusion.3
  518.6 7.4 psum.96
  532.2 2.9 reduce_sum.356
  535.1 2.8 fusion.84
  538.2 41.0 %all-reduce.31.cloned.1.call-done = bf16[256,768]{1,0:T(8,128)(2,1)} async-done(((bf16[256,768]{1,0:T(8,128)(2,1)}), bf16[256,768]{1,0:T(8,128)(2,1)}) %all-reduce.31.cloned.1.call-update) | async-done | bytes 393232 | tf_op jit(solution)/shard_map/psum | solution.py:299
  591.6 3.6 copy.363
  595.2 3.5 reshape.924
  601.3 36.3 %copy.365 = bf16[2,1024,192]{0,2,1:T(8,128)(2,1)} copy(bf16[2,1024,192]{1,2,0:T(8,128)(2,1)} %bitcast.587) | data formatting | bytes 1572864
  637.7 68.6 %reshape.926 = bf16[1024,384]{1,0:T(8,128)(2,1)} reshape(bf16[1024,192,2]{2,1,0:T(8,128)(2,1)} %bitcast.534) | data formatting | bytes 1572864
  709.2 28.3 %reduce-scatter.27.cloned.1.call-done = bf16[128,384]{1,0:T(8,128)(2,1)} async-done(((bf16[1024,384]{1,0:T(8,128)(2,1)}), bf16[128,384]{1,0:T(8,128)(2,1)}) %reduce-scatter.27.cloned.1.call-update) | async-done | bytes 98320
  737.6 14.8 reshape.927
  752.4 6.5 copy.366
  762.6 40.4 %all-reduce.33.cloned.1.call-done = bf16[256,768]{1,0:T(8,128)(2,1)} async-done(((bf16[256,768]{1,0:T(8,128)(2,1)}), bf16[256,768]{1,0:T(8,128)(2,1)}) %all-reduce.33.cloned.1.call-update) | async-done | bytes 393232 | tf_op jit(solution)/shard_map/psum | solution.py:387
  810.2 5.3 scatter_custom_fusion.1
  817.9 7.5 all-to-all-start.6
  826.0 11.6 all-to-all-done.6
  846.5 5.0 all-to-all-start.7
  853.9 8.3 psum.99
  862.3 2.8 multiply_convert_fusion.11
  872.5 2.9 reduce_sum.363
  878.5 40.6 %all-reduce.35.cloned.1.call-done = bf16[256,768]{1,0:T(8,128)(2,1)} async-done(((bf16[256,768]{1,0:T(8,128)(2,1)}), bf16[256,768]{1,0:T(8,128)(2,1)}) %all-reduce.35.cloned.1.call-update) | async-done | bytes 393232 | tf_op jit(solution)/shard_map/psum | solution.py:299
  928.4 36.3 %copy.369 = bf16[2,1024,192]{0,2,1:T(8,128)(2,1)} copy(bf16[2,1024,192]{1,2,0:T(8,128)(2,1)} %bitcast.588) | data formatting | bytes 1572864
  964.8 68.4 %reshape.930 = bf16[1024,384]{1,0:T(8,128)(2,1)} reshape(bf16[1024,192,2]{2,1,0:T(8,128)(2,1)} %bitcast.535) | data formatting | bytes 1572864
  1065.5 3.0 copy.342
  1069.8 14.8 reshape.931
  1084.7 7.0 copy.370
  1091.7 7.0 copy.340
  1124.0 54.6 %reduce-scatter.33.cloned.1.call-done = bf16[24,1024]{1,0:T(8,128)(2,1)} async-done(((bf16[768,1024]{1,0:T(8,128)(2,1)}), bf16[24,1024]{1,0:T(8,128)(2,1)}) %reduce-scatter.33.cloned.1.call-update) | async-done | bytes 49168
  1179.4 80.0 %reduce-scatter.35.cloned.1.call-done = bf16[24,1024]{1,0:T(8,128)(2,1)} async-done(((bf16[768,1024]{1,0:T(8,128)(2,1)}), bf16[24,1024]{1,0:T(8,128)(2,1)}) %reduce-scatter.35.cloned.1.call-update) | async-done | bytes 49168
  1260.2 80.2 %reduce-scatter.37.cloned.1.call-done = bf16[24,1024]{1,0:T(8,128)(2,1)} async-done(((bf16[768,1024]{1,0:T(8,128)(2,1)}), bf16[24,1024]{1,0:T(8,128)(2,1)}) %reduce-scatter.37.cloned.1.call-update) | async-done | bytes 49168
  1343.2 44.2 %all-reduce.39.cloned.1.call-done = (bf16[256,768]{1,0:T(8,128)(2,1)}, bf16[256,768]{1,0:T(8,128)(2,1)}) async-done(((bf16[256,768]{1,0:T(8,128)(2,1)}, bf16[256,768]{1,0:T(8,128)(2,1)}), (bf16[256,768]{1,0:T(8,128)(2,1)}, bf16[256,768]{1,0:T(8,128)(2,1)})) %all-reduce.39.cloned.1.call-update) | async-done | bytes 786448 | tf_op jit(solution)/shard_map/psum | solution.py:175
  1388.8 123.7 %all-reduce.11 = (bf16[2,768]{1,0:T(2,128)(2,1)S(1)}, bf16[2,768]{1,0:T(2,128)(2,1)S(1)}, bf16[2,768,16]{1,2,0:T(8,128)(2,1)S(1)}) all-reduce(bf16[2,768]{1,0:T(2,128)(2,1)S(1)} %pad_maximum_fusion.21, bf16[2,768]{1,0:T(2,128)(2,1)S(1)} %pad_maximum_fusion.22, ...), channel_id=6, replica_groups=mesh['dp'=4,'ep'=8,'tp'=4] {'dp','ep'}, use_global_device_ids=true, to_apply=%region_50.51.clone | all-reduce | flops 27648 | bytes 110592
  1523.2 160.7 %all-reduce.41.cloned.1.call-done = (bf16[2,2,768,512]{3,2,1,0:T(8,128)(2,1)}, bf16[2,2,768,512]{3,2,1,0:T(8,128)(2,1)}, bf16[2,2,512,768]{3,2,1,0:T(8,128)(2,1)}) async-done(((bf16[2,2,768,512]{3,2,1,0:T(8,128)(2,1)}, bf16[2,2,768,512]{3,2,1,0:T(8,128)(2,1)}, bf16[2,2,512,768]{3,2,1,0:T(8,128)(2,1)}), (bf16[2,2,768,512]{3,2,1,0:T(8,128)(2,1)}, bf16[2,2,768,512]{3,2,1,0:T(8,128)(2,1)}, ...) | async-done | bytes 9437200 | tf_op jit(solution)/shard_map/psum | solution.py:427
  1683.8 5.6 convert_element_type.638
  1689.5 3.6 convert_element_type.639
  1693.0 3.2 convert_element_type.640
  (735 shorter events, 240.7 us)
Async XLA Ops:
  8.0 203.7 %all-reduce.25.cloned.1.call-start = ((), (), s32[]{:S(2)}) async-start(), calls=%async_computation.15 | async-start | bytes 786432 | tf_op jit(solution)/shard_map/psum | solution.py:135
  34.7 352.0 %copy-start.31 = (bf16[2,768,192]{2,1,0:T(8,128)(2,1)}, bf16[2,768,192]{2,1,0:T(8,128)(2,1)S(1)}, u32[]{:S(2)}) copy-start(bf16[2,768,192]{2,1,0:T(8,128)(2,1)S(1)} %all_gather.48) | copy-start | bytes 1769476
  55.3 295.8 %copy-start.157 = (f32[768]{0:T(1024)}, f32[768]{0:T(1024)S(1)}, u32[]{:S(2)}) copy-start(f32[768]{0:T(1024)S(1)} %get-tuple-element.117) | copy-start | bytes 9220
  82.6 38.5 %copy-start.75 = (bf16[1,768,192]{1,2,0:T(8,128)(2,1)}, bf16[1,768,192]{1,2,0:T(8,128)(2,1)S(1)}, u32[]{:S(2)}) copy-start(bf16[1,768,192]{1,2,0:T(8,128)(2,1)S(1)} %copy.386) | copy-start | bytes 884740
  82.8 66.3 %copy-start.11 = (bf16[2,128,768]{2,1,0:T(8,128)(2,1)}, bf16[2,128,768]{2,1,0:T(8,128)(2,1)S(1)}, u32[]{:S(2)}) copy-start(bf16[2,128,768]{2,1,0:T(8,128)(2,1)S(1)} %fusion.129) | copy-start | bytes 1179652
  96.1 70.9 %copy-start.73 = (bf16[2,1024,192]{1,2,0:T(8,128)(2,1)}, bf16[2,1024,192]{1,2,0:T(8,128)(2,1)S(1)}, u32[]{:S(2)}) copy-start(bf16[2,1024,192]{1,2,0:T(8,128)(2,1)S(1)} %all_gather.44) | copy-start | bytes 2359300
  169.9 116.2 %all-gather.6.cloned.1.call-start = ((), (), s32[]{:S(2)}) async-start(), calls=%async_computation.16 | async-start | bytes 1622016 | tf_op jit(solution)/shard_map/all_gather | solution.py:91
  170.4 117.9 %all-gather.8.cloned.1.call-start = ((), (), s32[]{:S(2)}) async-start(), calls=%async_computation.17 | async-start | bytes 1622016 | tf_op jit(solution)/shard_map/all_gather | solution.py:92
  192.6 386.6 %copy-start.153 = (f32[768]{0:T(1024)}, f32[768]{0:T(1024)S(1)}, u32[]{:S(2)}) copy-start(f32[768]{0:T(1024)S(1)} %get-tuple-element.115) | copy-start | bytes 9220
  193.2 73.3 %copy-start.163 = (s32[256,2]{0,1:T(2,128)}, s32[256,2]{0,1:T(2,128)S(1)}, u32[]{:S(2)}) copy-start(s32[256,2]{0,1:T(2,128)S(1)} %get-tuple-element.186) | copy-start | bytes 6148
  193.2 236.4 %copy-start.165 = (s32[256,2]{0,1:T(2,128)}, s32[256,2]{0,1:T(2,128)S(1)}, u32[]{:S(2)}) copy-start(s32[256,2]{0,1:T(2,128)S(1)} %get-tuple-element.185) | copy-start | bytes 6148
  214.2 74.2 %copy-start.15 = (bf16[256,768]{1,0:T(8,128)(2,1)}, bf16[256,768]{1,0:T(8,128)(2,1)S(1)}, u32[]{:S(2)}) copy-start(bf16[256,768]{1,0:T(8,128)(2,1)S(1)} %multiply_convert_fusion.10) | copy-start | bytes 1179652
  215.5 38.4 %all-to-all-start = ((bf16[16,32,768]{2,1,0:T(8,128)(2,1)}), bf16[16,32,768]{2,1,0:T(8,128)(2,1)S(1)}, u32[]{:S(2)}, u32[]{:S(2)}) async-start(bf16[16,32,768]{2,1,0:T(8,128)(2,1)} %convolution_convert_fusion.13), calls=%async_computation | async-start | bytes 1572864 | tf_op jit(solution)/shard_map/all_to_all | solution.py:159
  222.4 85.6 %all-gather.10.cloned.1.call-start = ((), (), s32[]{:S(2)}) async-start(), calls=%async_computation.18 | async-start | bytes 1622016 | tf_op jit(solution)/shard_map/all_gather | solution.py:93
  261.7 16.4 all-to-all-start.1
  265.9 83.9 %all-reduce.27.cloned.1.call-start = ((), (), s32[]{:S(2)}) async-start(), calls=%async_computation.19 | async-start | bytes 786432 | tf_op jit(solution)/shard_map/psum | solution.py:175
  310.3 117.7 %all-reduce.29.cloned.1.call-start = ((), (), s32[]{:S(2)}) async-start(), calls=%async_computation.20 | async-start | bytes 786432 | tf_op jit(solution)/shard_map/psum | solution.py:135
  310.9 40.7 %copy-start.77 = (bf16[1,768,192]{1,2,0:T(8,128)(2,1)}, bf16[1,768,192]{1,2,0:T(8,128)(2,1)S(1)}, u32[]{:S(2)}) copy-start(bf16[1,768,192]{1,2,0:T(8,128)(2,1)S(1)} %copy.388) | copy-start | bytes 884740
  314.7 35.1 %copy-start.55 = (bf16[256,768]{1,0:T(8,128)(2,1)S(1)}, bf16[256,768]{1,0:T(8,128)(2,1)}, u32[]{:S(2)}) copy-start(bf16[256,768]{1,0:T(8,128)(2,1)} %all-reduce.25.cloned.1.call-done) | copy-start | bytes 1179652
  351.1 76.9 %copy-start.9 = (f32[256,768]{1,0:T(8,128)}, f32[256,768]{1,0:T(8,128)S(1)}, u32[]{:S(2)}) copy-start(f32[256,768]{1,0:T(8,128)S(1)} %get-tuple-element.138) | copy-start | bytes 2359300
  386.7 42.5 %copy-start.116 = (bf16[2,128,3,64]{1,0,3,2:T(2,128)(2,1)}, bf16[2,128,3,64]{1,0,3,2:T(2,128)(2,1)S(1)}, u32[]{:S(2)}) copy-start(bf16[2,128,3,64]{1,0,3,2:T(2,128)(2,1)S(1)} %copy.309) | copy-start | bytes 294916
  387.8 41.5 %copy-start.144 = (bf16[1,768,16]{1,2,0:T(8,128)(2,1)S(1)}, bf16[1,768,16]{1,2,0:T(8,128)(2,1)}, u32[]{:S(2)}) copy-start(bf16[1,768,16]{1,2,0:T(8,128)(2,1)} %copy.389) | copy-start | bytes 73732
  429.2 150.1 %copy-start.7 = (f32[256,768]{1,0:T(8,128)}, f32[256,768]{1,0:T(8,128)S(1)}, u32[]{:S(2)}) copy-start(f32[256,768]{1,0:T(8,128)S(1)} %get-tuple-element.136) | copy-start | bytes 2359300
  429.2 150.0 %copy-start.181 = (f32[256]{0:T(256)}, f32[256]{0:T(256)S(1)}, u32[]{:S(2)}) copy-start(f32[256]{0:T(256)S(1)} %fusion.234) | copy-start | bytes 3076
  429.4 35.7 %copy-start.5 = (bf16[256,768]{1,0:T(8,128)(2,1)}, bf16[256,768]{1,0:T(8,128)(2,1)S(1)}, u32[]{:S(2)}) copy-start(bf16[256,768]{1,0:T(8,128)(2,1)S(1)} %multiply_convert_fusion.8) | copy-start | bytes 1179652
  438.5 19.3 %all-to-all-start.4 = ((bf16[16,32,768]{2,1,0:T(8,128)(2,1)}), bf16[16,32,768]{2,1,0:T(8,128)(2,1)S(1)}, u32[]{:S(2)}, u32[]{:S(2)}) async-start(bf16[16,32,768]{2,1,0:T(8,128)(2,1)} %bitcast.571), calls=%async_computation.4 | async-start | bytes 1572864 | tf_op jit(solution)/shard_map/all_to_all | solution.py:269
  457.8 17.4 %all-to-all-start.2 = ((bf16[16,32,768]{2,1,0:T(8,128)(2,1)}), bf16[16,32,768]{2,1,0:T(8,128)(2,1)}, u32[]{:S(2)}, u32[]{:S(2)}) async-start(bf16[16,32,768]{2,1,0:T(8,128)(2,1)} %convolution_convert_fusion.12), calls=%async_computation.2 | async-start | bytes 1572864 | tf_op jit(solution)/shard_map/all_to_all | solution.py:159
  483.3 17.8 %all-to-all-start.3 = ((bf16[2,256,768]{2,0,1:T(2,128)(2,1)}), bf16[2,256,768]{2,0,1:T(2,128)(2,1)}, u32[]{:S(2)}, u32[]{:S(2)}) async-start(bf16[2,256,768]{2,0,1:T(2,128)(2,1)} %copy.313), calls=%async_computation.3 | async-start | bytes 1572864 | tf_op jit(solution)/shard_map/all_to_all | solution.py:170
  501.1 24.8 %all-to-all-start.5 = ((bf16[2,256,768]{2,0,1:T(2,128)(2,1)}), bf16[2,256,768]{2,0,1:T(2,128)(2,1)}, u32[]{:S(2)}, u32[]{:S(2)}) async-start(bf16[2,256,768]{2,0,1:T(2,128)(2,1)} %copy.319), calls=%async_computation.5 | async-start | bytes 1572864 | tf_op jit(solution)/shard_map/all_to_all | solution.py:294
  506.1 73.1 %all-reduce.31.cloned.1.call-start = ((), (), s32[]{:S(2)}) async-start(), calls=%async_computation.21 | async-start | bytes 786432 | tf_op jit(solution)/shard_map/psum | solution.py:299
  537.9 169.4 %reduce-scatter.25.cloned.1.call-start = ((), (), s32[]{:S(2)}) async-start(), calls=%async_computation.24 | async-start | bytes 884736
  598.8 138.8 %reduce-scatter.27.cloned.1.call-start = ((), (), s32[]{:S(2)}) async-start(), calls=%async_computation.25 | async-start | bytes 884736
  637.7 68.9 %copy-start.22 = (bf16[2,3,128,1024]{3,2,1,0:T(8,128)(2,1)S(1)}, bf16[2,3,128,1024]{3,2,1,0:T(8,128)(2,1)}, u32[]{:S(2)}) copy-start(bf16[2,3,128,1024]{3,2,1,0:T(8,128)(2,1)} %copy-done.21) | copy-start | bytes 4718596
  637.7 68.9 %copy-start.35 = (bf16[2,1024,192]{1,2,0:T(8,128)(2,1)S(1)}, bf16[2,1024,192]{1,2,0:T(8,128)(2,1)}, u32[]{:S(2)}) copy-start(bf16[2,1024,192]{1,2,0:T(8,128)(2,1)} %copy-done.34) | copy-start | bytes 2359300
  706.3 96.7 %all-reduce.33.cloned.1.call-start = ((), (), s32[]{:S(2)}) async-start(), calls=%async_computation.22 | async-start | bytes 786432 | tf_op jit(solution)/shard_map/psum | solution.py:387
  708.8 43.6 %copy-start.118 = (bf16[2,128,3,64]{1,0,3,2:T(2,128)(2,1)}, bf16[2,128,3,64]{1,0,3,2:T(2,128)(2,1)S(1)}, u32[]{:S(2)}) copy-start(bf16[2,128,3,64]{1,0,3,2:T(2,128)(2,1)S(1)} %copy.323) | copy-start | bytes 294916
  708.9 50.0 %copy-start.110 = (bf16[2,128,3,64]{1,0,3,2:T(2,128)(2,1)}, bf16[2,128,3,64]{1,0,3,2:T(2,128)(2,1)S(1)}, u32[]{:S(2)}) copy-start(bf16[2,128,3,64]{1,0,3,2:T(2,128)(2,1)S(1)} %copy.324) | copy-start | bytes 294916
  759.3 43.8 %copy-start.10 = (f32[256,768]{1,0:T(8,128)S(1)}, f32[256,768]{1,0:T(8,128)}, u32[]{:S(2)}) copy-start(f32[256,768]{1,0:T(8,128)} %copy-done.9) | copy-start | bytes 2359300
  759.3 43.8 %copy-start.158 = (f32[768]{0:T(1024)S(1)}, f32[768]{0:T(1024)}, u32[]{:S(2)}) copy-start(f32[768]{0:T(1024)} %copy-done.157) | copy-start | bytes 9220
  759.3 43.7 %copy-start.183 = (f32[256]{0:T(256)S(1)}, f32[256]{0:T(256)}, u32[]{:S(2)}) copy-start(f32[256]{0:T(256)} %copy-done.182) | copy-start | bytes 3076
  759.9 45.0 %copy-start.185 = (f32[256]{0:T(256)S(1)}, f32[256]{0:T(256)}, u32[]{:S(2)}) copy-start(f32[256]{0:T(256)} %copy-done.184) | copy-start | bytes 3076
  759.9 45.0 %copy-start.27 = (f32[256,768]{1,0:T(8,128)S(1)}, f32[256,768]{1,0:T(8,128)}, u32[]{:S(2)}) copy-start(f32[256,768]{1,0:T(8,128)} %copy-done.26) | copy-start | bytes 2359300
  806.1 56.1 %copy-start.46 = (f32[256,768]{1,0:T(8,128)}, f32[256,768]{1,0:T(8,128)S(1)}, u32[]{:S(2)}) copy-start(f32[256,768]{1,0:T(8,128)S(1)} %get-tuple-element.132) | copy-start | bytes 2359300
  817.9 19.7 %all-to-all-start.6 = ((bf16[16,32,768]{2,1,0:T(8,128)(2,1)}), bf16[16,32,768]{2,1,0:T(8,128)(2,1)S(1)}, u32[]{:S(2)}, u32[]{:S(2)}) async-start(bf16[16,32,768]{2,1,0:T(8,128)(2,1)} %bitcast.97), calls=%async_computation.6 | async-start | bytes 1572864 | tf_op jit(solution)/shard_map/all_to_all | solution.py:269
  846.5 19.8 %all-to-all-start.7 = ((bf16[2,256,768]{2,0,1:T(2,128)(2,1)}), bf16[2,256,768]{2,0,1:T(2,128)(2,1)}, u32[]{:S(2)}, u32[]{:S(2)}) async-start(bf16[2,256,768]{2,0,1:T(2,128)(2,1)} %copy.330), calls=%async_computation.7 | async-start | bytes 1572864 | tf_op jit(solution)/shard_map/all_to_all | solution.py:294
  851.5 67.7 %all-reduce.35.cloned.1.call-start = ((), (), s32[]{:S(2)}) async-start(), calls=%async_computation.23 | async-start | bytes 786432 | tf_op jit(solution)/shard_map/psum | solution.py:299
  875.5 43.7 %copy-start.56 = (bf16[256,768]{1,0:T(8,128)(2,1)S(1)}, bf16[256,768]{1,0:T(8,128)(2,1)}, u32[]{:S(2)}) copy-start(bf16[256,768]{1,0:T(8,128)(2,1)} %all-reduce.25.cloned.1.call-done) | copy-start | bytes 1179652
  875.5 43.7 %copy-start.150 = (bf16[1,768,16]{1,2,0:T(8,128)(2,1)S(1)}, bf16[1,768,16]{1,2,0:T(8,128)(2,1)}, u32[]{:S(2)}) copy-start(bf16[1,768,16]{1,2,0:T(8,128)(2,1)} %copy-done.149) | copy-start | bytes 73732
  875.5 43.7 %copy-start.160 = (f32[768]{0:T(1024)S(1)}, f32[768]{0:T(1024)}, u32[]{:S(2)}) copy-start(f32[768]{0:T(1024)} %copy-done.159) | copy-start | bytes 9220
  875.5 43.7 %copy-start.190 = (f32[256]{0:T(256)S(1)}, f32[256]{0:T(256)}, u32[]{:S(2)}) copy-start(f32[256]{0:T(256)} %copy-done.189) | copy-start | bytes 3076
  878.2 42.6 %copy-start.187 = (f32[256]{0:T(256)S(1)}, f32[256]{0:T(256)}, u32[]{:S(2)}) copy-start(f32[256]{0:T(256)} %copy-done.186) | copy-start | bytes 3076
  878.2 191.6 %reduce-scatter.31.cloned.1.call-start = ((), (), s32[]{:S(2)}) async-start(), calls=%async_computation.27 | async-start | bytes 884736
  878.5 42.3 %copy-start.167 = (bf16[256,16]{0,1:T(8,128)(2,1)}, bf16[256,16]{0,1:T(8,128)(2,1)S(1)}, u32[]{:S(2)}) copy-start(bf16[256,16]{0,1:T(8,128)(2,1)S(1)} %select_reduce_fusion) | copy-start | bytes 24580
  1033.2 65.5 %reduce-scatter.29.cloned.1.call-start = ((), (), s32[]{:S(2)}) async-start(), calls=%async_computation.26 | async-start | bytes 884736
  1040.0 138.5 %reduce-scatter.33.cloned.1.call-start = ((), (), s32[]{:S(2)}) async-start(), calls=%async_computation.28 | async-start | bytes 1622016
  1044.9 214.5 %reduce-scatter.35.cloned.1.call-start = ((), (), s32[]{:S(2)}) async-start(), calls=%async_computation.29 | async-start | bytes 1622016
  1050.0 290.4 %reduce-scatter.37.cloned.1.call-start = ((), (), s32[]{:S(2)}) async-start(), calls=%async_computation.30 | async-start | bytes 1622016
  1060.1 327.3 %all-reduce.39.cloned.1.call-start = ((), (), s32[]{:S(2)}) async-start(), calls=%async_computation.32 | async-start | bytes 1572864 | tf_op jit(solution)/shard_map/psum | solution.py:175
  1102.6 415.1 %all-reduce.37.cloned.1.call-start = ((), (), s32[]{:S(2)}) async-start(), calls=%async_computation.31 | async-start | bytes 6291456
  1109.6 574.2 %all-reduce.41.cloned.1.call-start = ((), (), s32[]{:S(2)}) async-start(), calls=%async_computation.33 | async-start | bytes 18874368 | tf_op jit(solution)/shard_map/psum | solution.py:427
  1121.6 265.8 %copy-start.152 = (f32[768]{0:T(1024)S(1)}, f32[768]{0:T(1024)}, u32[]{:S(2)}) copy-start(f32[768]{0:T(1024)} %copy-done.151) | copy-start | bytes 9220
  1121.6 392.8 %copy-start.8 = (f32[256,768]{1,0:T(8,128)S(1)}, f32[256,768]{1,0:T(8,128)}, u32[]{:S(2)}) copy-start(f32[256,768]{1,0:T(8,128)} %copy-done.7) | copy-start | bytes 2359300
  1341.9 174.6 %copy-start.25 = (f32[256,768]{1,0:T(8,128)S(1)}, f32[256,768]{1,0:T(8,128)}, u32[]{:S(2)}) copy-start(f32[256,768]{1,0:T(8,128)} %copy-done.23) | copy-start | bytes 2359300
  1387.4 129.1 %copy-start.92 = (bf16[256,768]{1,0:T(8,128)(2,1)S(1)}, bf16[256,768]{1,0:T(8,128)(2,1)}, u32[]{:S(2)}) copy-start(bf16[256,768]{1,0:T(8,128)(2,1)} %get-tuple-element.127) | copy-start | bytes 1179652
  (169 other events, 898.2 us)
Sparse Core Ops, SparseCore 0:
  170.0 41.7 all-reduce.24
  310.4 39.3 all-reduce.26
  387.9 40.0 all-reduce.28
  538.0 41.1 all-reduce.30
  598.9 31.0 reduce-scatter.24
  706.4 31.1 reduce-scatter.26
  761.1 41.8 all-reduce.32
  878.3 40.7 all-reduce.34
  1033.3 31.0 reduce-scatter.30
  1066.8 30.1 reduce-scatter.28
  1100.5 77.9 reduce-scatter.32
  1181.9 77.4 reduce-scatter.34
  1262.9 77.4 reduce-scatter.36
  1343.2 44.0 all-reduce.38
  1390.8 111.9 all-reduce.36
  1506.1 177.6 all-reduce.40
Sparse Core Ops, SparseCore 1:
  172.9 44.9 all-gather.5
  220.2 42.7 all-gather.7
  265.5 42.5 all-gather.9
where the time goes:
time: 1720 us; the launch traced here: 1700 us
  waiting for transfers between devices  720 us (42%)
  local copies, waits for them, and re-layouts  384 us (22%)
  blocking collectives  364 us (21%)
  matrix products  87.3 us (5%)
  other arithmetic  81.2 us (5%)
  starting transfers between devices  47.7 us (3%)
  between operations  19.5 us (1%)
    unnamed x450, local copies, waits for them, and re-layouts  309 us
    unnamed x27, waiting for transfers between devices  245 us
    psum x1, waiting for transfers between devices, shards(): lax.psum(jnp.stack(expert_parts[0]).astype(jnp.bfloat16), 'dp')  161 us
    unnamed x1, blocking collectives  124 us
    psum x2, waiting for transfers between devices, shards(): lax.psum((dense_input + moe_input).astype(jnp.bfloat16), 'tp')  81.6 us
    psum x2, waiting for transfers between devices, shards(): lax.psum((dense_part + moe_part).astype(jnp.bfloat16), 'tp')  73.9 us
    psum x2, waiting for transfers between devices, shards(): lax.psum(attn_part.astype(jnp.bfloat16), 'tp').astype(jnp.float32)  58.5 us
    psum x1, waiting for transfers between devices, shards(): lax.psum(normed_part.astype(jnp.bfloat16), 'tp').astype(jnp.float32)  40.4 us
  transfers between devices with their start and end apart: 27, of which 18 were waited for; matrix products, arithmetic and copies ran while one was open for 16% of the time, Pallas kernels for 0%

commit v1 on v0

--- a/solution.py
+++ b/solution.py
@@ -1,9 +1,360 @@
+import functools
+
 import jax
 import jax.numpy as jnp
 from jax import lax
+from jax.experimental import pallas as pl
+from jax.experimental.pallas import tpu as pltpu
 from jax.sharding import PartitionSpec as P
 
 HD = 64
+MESH = pl.DeviceIdType.MESH
+BF = jnp.bfloat16
+F32 = jnp.float32
+WIDE = 2432
+CHUNK = 48
+VM = pl.BlockSpec(memory_space=pltpu.VMEM)
+
+
+def place():
+    y = lax.axis_index("dp")
+    e = lax.axis_index("ep")
+    z = lax.axis_index("tp")
+    return y, e // 2, e % 2, z
+
+
+def device(y, x, c, z):
+    return (y, x * 2 + c, z)
+
+
+def meet(givers, takers):
+    barrier = pltpu.get_barrier_semaphore()
+    for who in givers:
+        pl.semaphore_signal(barrier, inc=1, device_id=who, device_id_type=MESH)
+    pl.semaphore_wait(barrier, takers)
+
+
+class Line:
+    def __init__(self, send_sems, recv_sems):
+        self.send_sems, self.recv_sems, self.used, self.open = send_sems, recv_sems, 0, []
+
+    def start(self, src, dst, who):
+        at = self.used
+        self.used += 1
+        copy = pltpu.make_async_remote_copy(
+            src_ref=src,
+            dst_ref=dst,
+            send_sem=self.send_sems.at[at],
+            recv_sem=self.recv_sems.at[at],
+            device_id=who,
+            device_id_type=MESH,
+        )
+        copy.start()
+        self.open.append(copy)
+        return copy
+
+    def finish(self):
+        for copy in self.open:
+            copy.wait_send()
+
+
+def gather_kernel(src, out, land, send_sems, recv_sems):
+    y, x, c, z = place()
+
+    def at(j, d, core=None):
+        yy = (y + j * c + d * (1 - c) + 8) % 4
+        xx = (x + j * (1 - c) + d * c + 8) % 4
+        return yy, xx
+
+    def who(j, d):
+        yy, xx = at(j, d)
+        return device(yy, xx, c, z)
+
+    def slot(j, d):
+        yy, xx = at(j, d)
+        return yy * 8 + xx * 2 + c
+
+    sibling = device(y, x, 1 - c, z)
+    near = [who(1, 0), who(-1, 0), who(0, 1), who(0, -1), sibling]
+    meet(near, 5)
+    line = Line(send_sems, recv_sems)
+    sib = []
+
+    def spread(ref, j):
+        plus = line.start(ref, land.at[slot(j, 0)], who(0, 1))
+        minus = line.start(ref, land.at[slot(j, 0)], who(0, -1))
+        sib.append(line.start(ref, land.at[slot(j, 0)], sibling))
+        return plus, minus
+
+    first_plus = line.start(src, land.at[slot(0, 0)], who(1, 0))
+    first_minus = line.start(src, land.at[slot(0, 0)], who(-1, 0))
+    second = {0: spread(src, 0)}
+    land[slot(0, 0)] = src[...]
+    first_plus.wait_recv()
+    below = land.at[slot(-1, 0)]
+    on_plus = line.start(below.at[pl.ds(0, 32)], below.at[pl.ds(0, 32)], who(1, 0))
+    second[-1] = spread(below, -1)
+    first_minus.wait_recv()
+    above = land.at[slot(1, 0)]
+    on_minus = line.start(above.at[pl.ds(32, 16)], above.at[pl.ds(32, 16)], who(-1, 0))
+    second[1] = spread(above, 1)
+    on_plus.wait_recv()
+    on_minus.wait_recv()
+    second[2] = spread(land.at[slot(2, 0)], 2)
+    far = []
+    for j in (0, -1, 1, 2):
+        plus, minus = second[j]
+        plus.wait_recv()
+        got = land.at[slot(j, -1)]
+        sib.append(line.start(got, got, sibling))
+        if j in (0, -1):
+            far.append((j, line.start(got, got, who(0, 1))))
+        minus.wait_recv()
+        got = land.at[slot(j, 1)]
+        sib.append(line.start(got, got, sibling))
+        if j in (1, 2):
+            far.append((j, line.start(got, got, who(0, -1))))
+    for j, copy in far:
+        copy.wait_recv()
+        got = land.at[slot(j, 2)]
+        sib.append(line.start(got, got, sibling))
+    for copy in sib:
+        copy.wait_recv()
+    line.finish()
+
+    def unpack(p, carry):
+        one = land[2 * p].astype(F32)
+        two = land[2 * p + 1].astype(F32)
+        rows = pl.ds(pl.multiple_of(p * CHUNK, CHUNK), CHUNK)
+        out[0, rows] = jnp.concatenate([one[:24], two[:24]], axis=0).astype(BF)
+        out[1, rows] = jnp.concatenate([one[24:], two[24:]], axis=0).astype(BF)
+        return carry
+
+    lax.fori_loop(0, 16, unpack, 0)
+
+
+def gather_weights(src):
+    return pl.pallas_call(
+        gather_kernel,
+        out_shape=jax.ShapeDtypeStruct((2, 768, WIDE), BF),
+        in_specs=[VM],
+        out_specs=VM,
+        scratch_shapes=[
+            pltpu.VMEM((32, CHUNK, WIDE), BF),
+            pltpu.SemaphoreType.DMA((32,)),
+            pltpu.SemaphoreType.DMA((32,)),
+        ],
+        compiler_params=pltpu.CompilerParams(
+            collective_id=0, has_side_effects=True, vmem_limit_bytes=48 * 2**20
+        ),
+        name="gather_weights",
+    )(src)
+
+
+PARTS = (256, 640, 512, 512, 512)
+
+
+def scatter_kernel(*refs):
+    ins, outs = refs[:10], refs[10:15]
+    chunks, sib_land, plus_far, minus_far, plus_near, minus_near, one_far, one_near, send_sems, recv_sems = refs[15:]
+    y, x, c, z = place()
+
+    def at(j, d):
+        yy = (y + j * c + d * (1 - c) + 8) % 4
+        xx = (x + j * (1 - c) + d * c + 8) % 4
+        return yy, xx
+
+    def who(j, d):
+        yy, xx = at(j, d)
+        return device(yy, xx, c, z)
+
+    def slot(j, d, core):
+        yy, xx = at(j, d)
+        return yy * 8 + xx * 2 + core
+
+    sibling = device(y, x, 1 - c, z)
+    meet([who(1, 0), who(-1, 0), who(0, 1), who(0, -1), sibling], 5)
+
+    def pack(p, carry):
+        rows = pl.ds(pl.multiple_of(p * CHUNK, CHUNK), CHUNK)
+        left = 0
+        for part, width in enumerate(PARTS):
+            one = ins[part][rows].astype(F32)
+            two = ins[5 + part][rows].astype(F32)
+            cols = slice(left, left + width)
+            chunks[2 * p, :, cols] = jnp.concatenate([one[:24], two[:24]], axis=0).astype(BF)
+            chunks[2 * p + 1, :, cols] = jnp.concatenate([one[24:], two[24:]], axis=0).astype(BF)
+            left += width
+        return carry
+
+    lax.fori_loop(0, 16, pack, 0)
+    line = Line(send_sems, recv_sems)
+    order = [(j, d) for d in (2, 1, -1, 0) for j in (0, -1, 1, 2)]
+    swapped = {}
+    for n, (j, d) in enumerate(order):
+        yy = (y + j * (1 - c) + d * c + 8) % 4
+        xx = (x + j * c + d * (1 - c) + 8) % 4
+        swapped[j, d] = line.start(chunks.at[yy * 8 + xx * 2 + 1 - c], sib_land.at[n], sibling)
+
+    def join(j, d):
+        n = order.index((j, d))
+        swapped[j, d].wait_recv()
+        mine = slot(j, d, c)
+        chunks[mine] = (chunks[mine].astype(F32) + sib_land[n].astype(F32)).astype(BF)
+        return chunks.at[mine]
+
+    plus_set, minus_set = (0, -1), (1, 2)
+    far = {}
+    for j in (0, -1, 1, 2):
+        ref = join(j, 2)
+        if j in plus_set:
+            far[j] = line.start(ref, plus_far.at[plus_set.index(j)], who(0, 1))
+        else:
+            far[j] = line.start(ref, minus_far.at[minus_set.index(j)], who(0, -1))
+    near = {}
+    for j in (1, 2):
+        near[j, 1] = line.start(join(j, 1), plus_near.at[j], who(0, 1))
+    for j in (0, -1):
+        near[j, -1] = line.start(join(j, -1), minus_near.at[j % 4], who(0, -1))
+    for j in plus_set:
+        ref = join(j, 1)
+        far[j].wait_recv()
+        ref[...] = (ref[...].astype(F32) + plus_far[plus_set.index(j)].astype(F32)).astype(BF)
+        near[j, 1] = line.start(ref, plus_near.at[j % 4], who(0, 1))
+    for j in minus_set:
+        ref = join(j, -1)
+        far[j].wait_recv()
+        ref[...] = (ref[...].astype(F32) + minus_far[minus_set.index(j)].astype(F32)).astype(BF)
+        near[j, -1] = line.start(ref, minus_near.at[j], who(0, -1))
+    held = {}
+    for j in (2, 1, -1, 0):
+        ref = join(j, 0)
+        near[j, 1].wait_recv()
+        near[j, -1].wait_recv()
+        total = ref[...].astype(F32) + plus_near[j % 4].astype(F32) + minus_near[j % 4].astype(F32)
+        ref[...] = total.astype(BF)
+        held[j] = ref
+        if j == 2:
+            a = line.start(ref.at[pl.ds(0, 32)], one_far.at[pl.ds(0, 32)], who(1, 0))
+            b = line.start(ref.at[pl.ds(32, 16)], one_far.at[pl.ds(32, 16)], who(-1, 0))
+    a.wait_recv()
+    up = held[1].at[pl.ds(0, 32)]
+    up[...] = (up[...].astype(F32) + one_far[:32].astype(F32)).astype(BF)
+    last_plus = line.start(held[1], one_near.at[0], who(1, 0))
+    b.wait_recv()
+    down = held[-1].at[pl.ds(32, 16)]
+    down[...] = (down[...].astype(F32) + one_far[32:].astype(F32)).astype(BF)
+    last_minus = line.start(held[-1], one_near.at[1], who(-1, 0))
+    last_plus.wait_recv()
+    last_minus.wait_recv()
+    left = 0
+    for part, width in enumerate(PARTS):
+        cols = slice(left, left + width)
+        total = held[0][:, cols].astype(F32) + one_near[0, :, cols].astype(F32) + one_near[1, :, cols].astype(F32)
+        outs[part][0] = total[:24]
+        outs[part][1] = total[24:]
+        left += width
+    line.finish()
+
+
+def scatter_grads(parts):
+    chunk = lambda n: pltpu.VMEM((n, CHUNK, WIDE), BF)
+    return pl.pallas_call(
+        scatter_kernel,
+        out_shape=[jax.ShapeDtypeStruct((2, 24, width), F32) for width in PARTS],
+        in_specs=[VM] * 10,
+        out_specs=[VM] * 5,
+        scratch_shapes=[
+            chunk(32),
+            chunk(16),
+            chunk(2),
+            chunk(2),
+            chunk(4),
+            chunk(4),
+            pltpu.VMEM((CHUNK, WIDE), BF),
+            chunk(2),
+            pltpu.SemaphoreType.DMA((32,)),
+            pltpu.SemaphoreType.DMA((32,)),
+        ],
+        compiler_params=pltpu.CompilerParams(
+            collective_id=1, has_side_effects=True, vmem_limit_bytes=56 * 2**20
+        ),
+        name="scatter_grads",
+    )(*parts)
+
+
+def rows_kernel(a0, a1, b0, b1, o0, o1, o2, o3, send_sems, recv_sems):
+    y, x, c, z = place()
+
+    def along(dy, dz):
+        return device((y + dy + 4) % 4, x, c, (z + dz + 4) % 4)
+
+    meet([along(1, 0), along(-1, 0), along(0, 1), along(0, -1)], 4)
+    line = Line(send_sems, recv_sems)
+
+    def quarter(k, first, count):
+        return pl.ds(pl.multiple_of(((z + k + 4) % 4) * 64 + first, 32), count)
+
+    work = list(zip((a0, a1, b0, b1), (o0, o1, o2, o3)))
+    near, half, full, spread = [], [], [], []
+    for src, out in work:
+        mine = src.at[0, quarter(0, 0, 64)]
+        near.append(
+            (
+                line.start(mine, out.at[0, 1, quarter(0, 0, 64)], along(1, 0)),
+                line.start(mine, out.at[0, 3, quarter(0, 0, 64)], along(-1, 0)),
+            )
+        )
+        full.append(
+            (
+                line.start(src.at[1], out.at[1, 1], along(1, 0)),
+                line.start(src.at[1], out.at[1, 3], along(-1, 0)),
+            )
+        )
+    for (src, out), (plus, minus) in zip(work, near):
+        plus.wait_recv()
+        p = line.start(out.at[0, 1, quarter(0, 0, 32)], out.at[0, 2, quarter(0, 0, 32)], along(1, 0))
+        minus.wait_recv()
+        m = line.start(out.at[0, 3, quarter(0, 32, 32)], out.at[0, 2, quarter(0, 32, 32)], along(-1, 0))
+        half.append((p, m))
+    for (src, out), (plus, minus) in zip(work, half):
+        plus.wait_recv()
+        minus.wait_recv()
+        got = out.at[0, pl.ds(1, 3), quarter(0, 0, 64)]
+        spread.append((line.start(got, got, along(0, 1)), line.start(got, got, along(0, -1))))
+    last = []
+    for (src, out), (plus, minus) in zip(work, full):
+        plus.wait_recv()
+        p = line.start(out.at[1, 1, pl.ds(0, 128)], out.at[1, 2, pl.ds(0, 128)], along(1, 0))
+        minus.wait_recv()
+        m = line.start(out.at[1, 3, pl.ds(128, 128)], out.at[1, 2, pl.ds(128, 128)], along(-1, 0))
+        last += [p, m]
+    for (src, out), (plus, minus) in zip(work, spread):
+        plus.wait_recv()
+        got = out.at[0, pl.ds(1, 3), quarter(-1, 0, 32)]
+        last.append(line.start(got, got, along(0, 1)))
+        minus.wait_recv()
+        got = out.at[0, pl.ds(1, 3), quarter(1, 32, 32)]
+        last.append(line.start(got, got, along(0, -1)))
+        out[:, 0] = src[...]
+    for copy in last:
+        copy.wait_recv()
+    line.finish()
+
+
+def gather_rows(arrays):
+    shape = jax.ShapeDtypeStruct((2, 4, 256, 768), BF)
+    return pl.pallas_call(
+        rows_kernel,
+        out_shape=[shape] * 4,
+        in_specs=[VM] * 4,
+        out_specs=[VM] * 4,
+        scratch_shapes=[pltpu.SemaphoreType.DMA((48,)), pltpu.SemaphoreType.DMA((48,))],
+        compiler_params=pltpu.CompilerParams(
+            collective_id=2, has_side_effects=True, vmem_limit_bytes=48 * 2**20
+        ),
+        name="gather_rows",
+    )(*arrays)
 
 
 epsilon = 1e-06
@@ -80,17 +431,26 @@
         )
         return jnp.where(allowed[:, None], scores, -1e30)
 
+    filler = jnp.zeros((depth_count, 24, 64), BF)
+    small = jnp.concatenate(
+        [router_weight, attn_gain[:, :, None], ffn_gain[:, :, None], filler[:, :, : 64 - 18]], axis=2
+    )
+    packed = jnp.concatenate(
+        [out_weight, small, query_weight, key_weight, value_weight, filler, dense_gate, dense_up, dense_down],
+        axis=2,
+    )
+    everything = gather_weights(packed.reshape(CHUNK, WIDE))
     gathered = (
-        lax.all_gather(attn_gain, ("dp", "ep"), axis=1, tiled=True),
-        lax.all_gather(query_weight, ("dp", "ep"), axis=1, tiled=True),
-        lax.all_gather(key_weight, ("dp", "ep"), axis=1, tiled=True),
-        lax.all_gather(value_weight, ("dp", "ep"), axis=1, tiled=True),
-        lax.all_gather(out_weight, ("dp", "ep"), axis=1, tiled=True),
-        lax.all_gather(ffn_gain, ("dp", "ep"), axis=1, tiled=True),
-        lax.all_gather(router_weight, ("dp", "ep"), axis=1, tiled=True),
-        lax.all_gather(dense_gate, ("dp", "ep"), axis=1, tiled=True),
-        lax.all_gather(dense_up, ("dp", "ep"), axis=1, tiled=True),
-        lax.all_gather(dense_down, ("dp", "ep"), axis=1, tiled=True),
+        everything[:, :, 208],
+        everything[:, :, 256:448],
+        everything[:, :, 448:640],
+        everything[:, :, 640:832],
+        everything[:, :, 0:192],
+        everything[:, :, 209],
+        everything[:, :, 192:208],
+        everything[:, :, 896:1408],
+        everything[:, :, 1408:1920],
+        everything[:, :, 1920:2432],
     )
     stream = inputs.astype(jnp.float32).reshape(rows, width)
     saved = []
@@ -200,7 +560,7 @@
         stream = middle + ffn_sum
     outputs = stream
     shared_parts = [[None] * depth_count for column in range(10)]
-    expert_parts = [[None] * depth_count for column in range(3)]
+    kept_rows = [None] * depth_count
     grad_stream = cotangent.astype(jnp.float32).reshape(rows, width)
     for depth in reversed(range(depth_count)):
         norm_one, w_query, w_key, w_value, w_out, norm_two, w_router, w_dgate, w_dup, w_ddown = [
@@ -273,18 +633,7 @@
         gate_exp_grad, up_exp_grad = jax.vjp(swish_product, gate_exp, up_exp)[1](hidden_exp_grad)
         gate_exp_grad = gate_exp_grad.astype(jnp.bfloat16)
         up_exp_grad = up_exp_grad.astype(jnp.bfloat16)
-        down_part = jnp.einsum(
-            "ecf,ecd->efd", hidden_exp, back_arrived, preferred_element_type=jnp.float32
-        )
-        gate_part = jnp.einsum(
-            "ecd,ecf->edf", arrived, gate_exp_grad, preferred_element_type=jnp.float32
-        )
-        up_part = jnp.einsum(
-            "ecd,ecf->edf", arrived, up_exp_grad, preferred_element_type=jnp.float32
-        )
-        expert_parts[0][depth] = gate_part
-        expert_parts[1][depth] = up_part
-        expert_parts[2][depth] = down_part
+        kept_rows[depth] = (arrived, back_arrived)
         arrived_grad = jnp.einsum(
             "ecf,edf->ecd", gate_exp_grad, expert_gate[depth], preferred_element_type=jnp.float32
         )
@@ -390,44 +739,47 @@
         )[1](normed_grad)
         shared_parts[0][depth] = gain_one_grad
         grad_stream = middle_grad + stream_norm_grad
-    stacked = [jnp.stack(column) for column in shared_parts]
+    parts = []
+    for depth in range(depth_count):
+        col = [column[depth] for column in shared_parts]
+        pad = jnp.zeros((width, 64), F32)
+        parts += [
+            jnp.concatenate([col[4], col[6], col[0][:, None], col[5][:, None], pad[:, : 64 - 18]], axis=1).astype(BF),
+            jnp.concatenate([col[1], col[2], col[3], pad], axis=1).astype(BF),
+            col[7].astype(BF),
+            col[8].astype(BF),
+            col[9].astype(BF),
+        ]
+    first, second, g_gate, g_up, g_down = scatter_grads(parts)
     summed = (
-        lax.psum_scatter(
-            stacked[0].astype(jnp.bfloat16), ("dp", "ep"), scatter_dimension=1, tiled=True
-        ).astype(jnp.float32),
-        lax.psum_scatter(
-            stacked[1].astype(jnp.bfloat16), ("dp", "ep"), scatter_dimension=1, tiled=True
-        ).astype(jnp.float32),
-        lax.psum_scatter(
-            stacked[2].astype(jnp.bfloat16), ("dp", "ep"), scatter_dimension=1, tiled=True
-        ).astype(jnp.float32),
-        lax.psum_scatter(
-            stacked[3].astype(jnp.bfloat16), ("dp", "ep"), scatter_dimension=1, tiled=True
-        ).astype(jnp.float32),
-        lax.psum_scatter(
-            stacked[4].astype(jnp.bfloat16), ("dp", "ep"), scatter_dimension=1, tiled=True
-        ).astype(jnp.float32),
-        lax.psum_scatter(
-            stacked[5].astype(jnp.bfloat16), ("dp", "ep"), scatter_dimension=1, tiled=True
-        ).astype(jnp.float32),
-        lax.psum_scatter(
-            stacked[6].astype(jnp.bfloat16), ("dp", "ep"), scatter_dimension=1, tiled=True
-        ).astype(jnp.float32),
-        lax.psum_scatter(
-            stacked[7].astype(jnp.bfloat16), ("dp", "ep"), scatter_dimension=1, tiled=True
-        ).astype(jnp.float32),
-        lax.psum_scatter(
-            stacked[8].astype(jnp.bfloat16), ("dp", "ep"), scatter_dimension=1, tiled=True
-        ).astype(jnp.float32),
-        lax.psum_scatter(
-            stacked[9].astype(jnp.bfloat16), ("dp", "ep"), scatter_dimension=1, tiled=True
-        ).astype(jnp.float32),
+        first[:, :, 208],
+        second[:, :, 0:192],
+        second[:, :, 192:384],
+        second[:, :, 384:576],
+        first[:, :, 0:192],
+        first[:, :, 209],
+        first[:, :, 192:208],
+        g_gate,
+        g_up,
+        g_down,
     )
-    expert_sums = (
-        lax.psum(jnp.stack(expert_parts[0]).astype(jnp.bfloat16), "dp").astype(jnp.float32),
-        lax.psum(jnp.stack(expert_parts[1]).astype(jnp.bfloat16), "dp").astype(jnp.float32),
-        lax.psum(jnp.stack(expert_parts[2]).astype(jnp.bfloat16), "dp").astype(jnp.float32),
+    rows0, rows1, back0, back1 = gather_rows(
+        [kept_rows[0][0], kept_rows[1][0], kept_rows[0][1], kept_rows[1][1]]
     )
+    expert_columns = ([], [], [])
+    for depth, (all_rows, all_back) in enumerate(((rows0, back0), (rows1, back1))):
+        all_rows = all_rows.reshape(2, 1024, width)
+        all_back = all_back.reshape(2, 1024, width)
+        gate_all = jnp.einsum("ecd,edf->ecf", all_rows, expert_gate[depth], preferred_element_type=F32)
+        up_all = jnp.einsum("ecd,edf->ecf", all_rows, expert_up[depth], preferred_element_type=F32)
+        hidden_all = swish_product(gate_all, up_all).astype(BF)
+        hidden_all_grad = jnp.einsum("ecd,efd->ecf", all_back, expert_down[depth], preferred_element_type=F32)
+        gate_all_grad, up_all_grad = jax.vjp(swish_product, gate_all, up_all)[1](hidden_all_grad)
+        gate_all_grad, up_all_grad = gate_all_grad.astype(BF), up_all_grad.astype(BF)
+        expert_columns[0].append(jnp.einsum("ecd,ecf->edf", all_rows, gate_all_grad, preferred_element_type=F32))
+        expert_columns[1].append(jnp.einsum("ecd,ecf->edf", all_rows, up_all_grad, preferred_element_type=F32))
+        expert_columns[2].append(jnp.einsum("ecf,ecd->efd", hidden_all, all_back, preferred_element_type=F32))
+    expert_sums = [jnp.stack(column) for column in expert_columns]
     outputs = outputs.reshape(seq_count, span, width)
     input_grad = grad_stream.reshape(seq_count, span, width)
     return (

time: 1720 us -> 1250 us (0.73)
  waiting for transfers between devices: 720 us -> 287 us
  blocking collectives: 364 us -> 73.5 us
  Pallas kernels: 0 us -> 165 us
  matrix products: 87.3 us -> 173 us
    unnamed x27 -> x15, waiting for transfers between devices: 245 us -> 18.4 us
    all_gather x7 -> x0, blocking collectives: 168 us -> none  [the longest x1 28.7 us: shards(): lax.all_gather(router_weight, ('dp', 'ep'), axis=1, tiled=True)]
    pallas_call x0 -> x3, Pallas kernels: none -> 165 us  [the longest x1 92.5 us: gather_rows(): pl.pallas_call(rows_kernel, out_shape=[shape] * 4, in_specs=[VM] * 4, out...]
    psum x1 -> x0, waiting for transfers between devices: 161 us -> none  [shards(): lax.psum(jnp.stack(expert_parts[0]).astype(jnp.bfloat16), 'dp')]
    unnamed x1 -> x0, blocking collectives: 124 us -> none
    dot_general x6 -> x12, matrix products: 6.02 us -> 57.1 us  [the longest x2 16 us: shards(): jnp.einsum('ecf,ecd->efd', hidden_all, all_back, preferred_element_type=F32)]
    unnamed x450 -> x318, local copies, waits for them, and re-layouts: 309 us -> 285 us
    convert_element_type x13 -> x1, other arithmetic: 19.4 us -> 1.83 us  [shards(): norm_two.astype(jnp.float32)]
  transfers between devices with their start and end apart: 27 -> 19, of which waited for: 18 -> 13; matrix products, arithmetic and copies ran while one was open for 16% -> 27% of each run, Pallas kernels for 0% -> 0%
where the time goes in v1:
time: 1250 us; the launch traced here: 1240 us
  local copies, waits for them, and re-layouts  389 us (31%)
  waiting for transfers between devices  287 us (23%)
  matrix products  173 us (14%)
  Pallas kernels  165 us (13%)
  other arithmetic  85.1 us (7%)
  blocking collectives  73.5 us (6%)
  starting transfers between devices  50.6 us (4%)
  between operations  16.5 us (1%)
    unnamed x318, local copies, waits for them, and re-layouts  285 us
    pallas_call x1, Pallas kernels, gather_rows(): pl.pallas_call(rows_kernel, out_shape=[shape] * 4, in_specs=[VM] * 4, out...  92.5 us
    psum x2, waiting for transfers between devices, shards(): lax.psum(attn_part.astype(jnp.bfloat16), 'tp').astype(jnp.float32)  71 us
    psum x2, waiting for transfers between devices, shards(): lax.psum((dense_part + moe_part).astype(jnp.bfloat16), 'tp')  69.8 us
    psum x2, waiting for transfers between devices, shards(): lax.psum((dense_input + moe_input).astype(jnp.bfloat16), 'tp')  68.8 us
    pallas_call x1, Pallas kernels, scatter_grads(): pl.pallas_call(scatter_kernel, out_shape=[jax.ShapeDtypeStruct((2, 24, wi...  37.8 us
    pallas_call x1, Pallas kernels, gather_weights(): pl.pallas_call(gather_kernel, out_shape=jax.ShapeDtypeStruct((2, 768, WID...  34.6 us
    psum x1, waiting for transfers between devices, shards(): lax.psum(normed_part.astype(jnp.bfloat16), 'tp').astype(jnp.float32)  32.8 us
  transfers between devices with their start and end apart: 19, of which 13 were waited for; matrix products, arithmetic and copies ran while one was open for 27% of the time, Pallas kernels for 0%

profile of v1, /device:TPU:1, one launch (start us, length us, event | category | flops | bytes accessed | tf_op | source)
XLA Modules:
  0.0 1239.6 jit_solution(13470082983729402737)
XLA Ops:
  10.6 34.6 %gather_weights.1 = bf16[2,768,2432]{2,1,0:T(8,128)(2,1)} custom-call(bf16[48,2432]{1,0:T(8,128)(2,1)S(1)} %concatenate.100.src), custom_call_target="tpu_custom_call" | custom-call | tf_op jit(solution)/shard_map/gather_weights/pallas_call | solution.py:137
  50.8 13.4 %all_gather.12 = bf16[2,1024,192]{1,2,0:T(8,128)(2,1)S(1)} all-gather(bf16[2,128,192]{1,2,0:T(8,128)(2,1)S(1)} %convolution_convert_fusion.20), channel_id=1, replica_groups=mesh['dp'=4,'ep'=8,'tp'=4] {'ep'}, dimensions={1}, use_global_device_ids=true | all-gather | bytes 884736 | tf_op jit(solution)/shard_map/all_gather | solution.py:477
  67.6 14.4 %all_gather.13 = bf16[2,1024,192]{1,2,0:T(8,128)(2,1)S(1)} all-gather(bf16[2,128,192]{1,2,0:T(8,128)(2,1)S(1)} %bitcast.561), channel_id=1, replica_groups=mesh['dp'=4,'ep'=8,'tp'=4] {'ep'}, dimensions={1}, use_global_device_ids=true | all-gather | bytes 884736 | tf_op jit(solution)/shard_map/all_gather | solution.py:474
  91.3 36.7 %all-reduce.13.cloned.1.call-done = bf16[256,768]{1,0:T(8,128)(2,1)} async-done(((bf16[256,768]{1,0:T(8,128)(2,1)}), bf16[256,768]{1,0:T(8,128)(2,1)}) %all-reduce.13.cloned.1.call-update) | async-done | bytes 393232 | tf_op jit(solution)/shard_map/psum | solution.py:495
  131.7 7.1 all-to-all-start
  140.8 10.2 all-to-all-done
  157.0 4.3 all-to-all-start.1
  167.4 6.2 all-to-all-done.1
  178.8 3.3 multiply_reduce_fusion.5
  185.7 37.9 %all-reduce.15.cloned.1.call-done = bf16[256,768]{1,0:T(8,128)(2,1)} async-done(((bf16[256,768]{1,0:T(8,128)(2,1)}), bf16[256,768]{1,0:T(8,128)(2,1)}) %all-reduce.15.cloned.1.call-update) | async-done | bytes 393232 | tf_op jit(solution)/shard_map/psum | solution.py:535
  226.7 16.8 %all_gather.14 = bf16[2,1024,192]{1,2,0:T(8,128)(2,1)S(1)} all-gather(bf16[2,128,192]{1,2,0:T(8,128)(2,1)S(1)} %convolution_convert_fusion.19), channel_id=1, replica_groups=mesh['dp'=4,'ep'=8,'tp'=4] {'ep'}, dimensions={1}, use_global_device_ids=true | all-gather | bytes 884736 | tf_op jit(solution)/shard_map/all_gather | solution.py:477
  244.2 13.4 %all_gather.15 = bf16[2,1024,192]{1,2,0:T(8,128)(2,1)S(1)} all-gather(bf16[2,128,192]{1,2,0:T(8,128)(2,1)S(1)} %bitcast.562), channel_id=1, replica_groups=mesh['dp'=4,'ep'=8,'tp'=4] {'ep'}, dimensions={1}, use_global_device_ids=true | all-gather | bytes 884736 | tf_op jit(solution)/shard_map/all_gather | solution.py:474
  269.4 34.3 %all-reduce.17.cloned.1.call-done = bf16[256,768]{1,0:T(8,128)(2,1)} async-done(((bf16[256,768]{1,0:T(8,128)(2,1)}), bf16[256,768]{1,0:T(8,128)(2,1)}) %all-reduce.17.cloned.1.call-update) | async-done | bytes 393232 | tf_op jit(solution)/shard_map/psum | solution.py:495
  311.2 7.2 all-to-all-start.2
  325.4 5.3 scatter_custom_fusion
  337.3 4.8 all-to-all-start.4
  348.8 5.5 all-to-all-done.4
  354.4 5.0 all-to-all-start.3
  367.5 4.2 all-to-all-done.3
  371.7 5.0 all-to-all-start.5
  381.9 4.6 gather_fusion.1
  389.6 5.1 multiply_reduce_fusion.3
  396.2 8.0 psum.75
  406.7 4.6 gather_fusion.2
  414.3 4.2 reduce_sum.356
  423.9 38.9 %all-reduce.19.cloned.1.call-done = bf16[256,768]{1,0:T(8,128)(2,1)} async-done(((bf16[256,768]{1,0:T(8,128)(2,1)}), bf16[256,768]{1,0:T(8,128)(2,1)}) %all-reduce.19.cloned.1.call-update) | async-done | bytes 393232 | tf_op jit(solution)/shard_map/psum | solution.py:648
  469.3 3.2 multiply_reduce_fusion.1
  476.8 3.6 reshape.978
  495.6 35.7 %copy.418 = bf16[2,1024,192]{0,2,1:T(8,128)(2,1)} copy(bf16[2,1024,192]{1,2,0:T(8,128)(2,1)S(1)} %bitcast.537) | data formatting | bytes 1572864
  531.3 68.4 %reshape.980 = bf16[1024,384]{1,0:T(8,128)(2,1)} reshape(bf16[1024,192,2]{2,1,0:T(8,128)(2,1)} %bitcast.502) | data formatting | bytes 1572864
  614.4 16.6 %reduce-scatter.15.cloned.1.call-done = bf16[128,384]{1,0:T(8,128)(2,1)} async-done(((bf16[1024,384]{1,0:T(8,128)(2,1)}), bf16[128,384]{1,0:T(8,128)(2,1)}) %reduce-scatter.15.cloned.1.call-update) | async-done | bytes 98320
  631.0 14.8 %reshape.981 = bf16[128,192,2]{2,1,0:T(8,128)(2,1)} reshape(bf16[128,384]{1,0:T(8,128)(2,1)} %reduce-scatter.15.cloned.1.call-done) | data formatting | bytes 196608
  645.8 7.0 copy.419
  667.9 32.8 %all-reduce.21.cloned.1.call-done = bf16[256,768]{1,0:T(8,128)(2,1)} async-done(((bf16[256,768]{1,0:T(8,128)(2,1)}), bf16[256,768]{1,0:T(8,128)(2,1)}) %all-reduce.21.cloned.1.call-update) | async-done | bytes 393232 | tf_op jit(solution)/shard_map/psum | solution.py:736
  707.6 7.5 psum.78
  721.7 6.1 scatter_custom_fusion.1
  730.2 9.2 all-to-all-start.6
  760.4 92.5 %gather_rows.1 = (bf16[2,4,256,768]{3,2,1,0:T(8,128)(2,1)}, bf16[2,4,256,768]{3,2,1,0:T(8,128)(2,1)}, bf16[2,4,256,768]{3,2,1,0:T(8,128)(2,1)}, bf16[2,4,256,768]{3,2,1,0:T(8,128)(2,1)}) custom-call(bf16[2,256,768]{2,1,0:T(8,128)(2,1)S(1)} %bitcast.494, bf16[2,256,768]{2,1,0:T(8,128)(2,1)S(1)} %bitcast.497, bf16[2,256,768]{2,1,0:T(8,128)(2,1)S(1)} %bitcast.501, ...), custom_call_target="tpu_custom_call" | custom-call | tf_op jit(solution)/shard_map/gather_rows/pallas_call | solution.py:347
  852.9 5.8 fusion.46
  858.8 3.8 fusion.40
  862.6 3.7 fusion.64
  866.3 3.7 fusion.58
  873.7 5.9 all-to-all-start.7
  880.0 4.3 fusion.34
  886.4 3.6 fusion.28
  890.0 6.5 fusion.23
  899.6 4.1 fusion.20
  903.7 3.7 fusion.29
  917.5 8.7 fusion.26
  926.2 29.9 %all-reduce.23.cloned.1.call-done = bf16[256,768]{1,0:T(8,128)(2,1)} async-done(((bf16[256,768]{1,0:T(8,128)(2,1)}), bf16[256,768]{1,0:T(8,128)(2,1)}) %all-reduce.23.cloned.1.call-update) | async-done | bytes 393232 | tf_op jit(solution)/shard_map/psum | solution.py:648
  962.7 35.7 %copy.422 = bf16[2,1024,192]{0,2,1:T(8,128)(2,1)} copy(bf16[2,1024,192]{1,2,0:T(8,128)(2,1)S(1)} %bitcast.538) | data formatting | bytes 1572864
  998.5 68.4 %reshape.984 = bf16[1024,384]{1,0:T(8,128)(2,1)} reshape(bf16[1024,192,2]{2,1,0:T(8,128)(2,1)} %bitcast.503) | data formatting | bytes 1572864
  1067.2 6.4 pad_maximum_fusion
  1073.6 3.4 pad_maximum_fusion.1
  1080.1 3.6 copy.420
  1083.8 3.5 reshape.982
  1087.4 7.2 fusion.27
  1094.6 3.2 pad_maximum_fusion.2
  1101.6 15.1 %reshape.985 = bf16[128,192,2]{2,1,0:T(8,128)(2,1)} reshape(bf16[128,384]{1,0:T(8,128)(2,1)} %reduce-scatter.19.cloned.1.call-done) | data formatting | bytes 196608
  1116.7 6.4 copy.423
  1123.2 6.4 copy.383
  1147.7 3.3 maximum_maximum_fusion.1
  1150.9 31.8 %all-reduce.25.cloned.1.call-done = (bf16[256,768]{1,0:T(8,128)(2,1)}, bf16[256,768]{1,0:T(8,128)(2,1)}) async-done(((bf16[256,768]{1,0:T(8,128)(2,1)}, bf16[256,768]{1,0:T(8,128)(2,1)}), (bf16[256,768]{1,0:T(8,128)(2,1)}, bf16[256,768]{1,0:T(8,128)(2,1)})) %all-reduce.25.cloned.1.call-update) | async-done | bytes 786448 | tf_op jit(solution)/shard_map/psum | solution.py:535
  1186.3 37.8 %scatter_grads.1 = (f32[2,24,256]{2,1,0:T(8,128)}, f32[2,24,640]{2,1,0:T(8,128)}, f32[2,24,512]{2,1,0:T(8,128)}, f32[2,24,512]{2,1,0:T(8,128)}, f32[2,24,512]{2,1,0:T(8,128)}) custom-call(bf16[768,256]{1,0:T(8,128)(2,1)} %concatenate.117.refs_0_, bf16[768,640]{1,0:T(8,128)(2,1)} %get-tuple-element.194.refs_1_, ...), custom_call_target="tpu_custom_call" | custom-call | tf_op jit(solution)/shard_map/scatter_grads/pallas_call | solution.py:262
  (571 shorter events, 274.3 us)
Async XLA Ops:
  7.2 120.8 %all-reduce.13.cloned.1.call-start = ((), (), s32[]{:S(2)}) async-start(), calls=%async_computation.12 | async-start | bytes 786432 | tf_op jit(solution)/shard_map/psum | solution.py:495
  47.1 82.2 %copy-start.89 = (f32[768]{0:T(1024)}, f32[768]{0:T(1024)S(1)}, u32[]{:S(2)}) copy-start(f32[768]{0:T(1024)S(1)} %get-tuple-element.125) | copy-start | bytes 9220
  47.1 177.9 %copy-start.88 = (f32[768]{0:T(1024)}, f32[768]{0:T(1024)S(1)}, u32[]{:S(2)}) copy-start(f32[768]{0:T(1024)S(1)} %get-tuple-element.124) | copy-start | bytes 9220
  49.1 18.4 %copy-start.102 = (f32[2,128]{1,0:T(2,128)}, f32[2,128]{1,0:T(2,128)S(1)}, u32[]{:S(2)}) copy-start(f32[2,128]{1,0:T(2,128)S(1)} %fusion.169) | copy-start | bytes 3076
  49.3 32.7 %copy-start.11 = (bf16[2,128,768]{2,1,0:T(8,128)(2,1)}, bf16[2,128,768]{2,1,0:T(8,128)(2,1)S(1)}, u32[]{:S(2)}) copy-start(bf16[2,128,768]{2,1,0:T(8,128)(2,1)S(1)} %fusion.171) | copy-start | bytes 1179652
  49.3 32.7 %copy-start.120 = (s32[2]{0:T(128)S(1)}, s32[2]{0:T(128)}, u32[]{:S(2)}) copy-start(s32[2]{0:T(128)} %param.19) | copy-start | bytes 28
  64.2 20.5 %copy-start.40 = (bf16[2,1024,192]{1,2,0:T(8,128)(2,1)}, bf16[2,1024,192]{1,2,0:T(8,128)(2,1)S(1)}, u32[]{:S(2)}) copy-start(bf16[2,1024,192]{1,2,0:T(8,128)(2,1)S(1)} %all_gather.12) | copy-start | bytes 2359300
  66.5 177.6 %copy-start.73 = (f32[128,32]{0,1:T(8,128)}, f32[128,32]{0,1:T(8,128)S(1)}, u32[]{:S(2)}) copy-start(f32[128,32]{0,1:T(8,128)S(1)} %get-tuple-element.197) | copy-start | bytes 49156
  85.7 46.0 %copy-start.57 = (bf16[2,128,3,64]{1,0,3,2:T(2,128)(2,1)}, bf16[2,128,3,64]{1,0,3,2:T(2,128)(2,1)S(1)}, u32[]{:S(2)}) copy-start(bf16[2,128,3,64]{1,0,3,2:T(2,128)(2,1)S(1)} %copy.341) | copy-start | bytes 294916
  87.9 50.8 %copy-start.95 = (s32[256,2]{0,1:T(2,128)}, s32[256,2]{0,1:T(2,128)S(1)}, u32[]{:S(2)}) copy-start(s32[256,2]{0,1:T(2,128)S(1)} %get-tuple-element.189) | copy-start | bytes 6148
  87.9 52.7 %copy-start.93 = (s32[256,2]{0,1:T(2,128)}, s32[256,2]{0,1:T(2,128)S(1)}, u32[]{:S(2)}) copy-start(s32[256,2]{0,1:T(2,128)S(1)} %get-tuple-element.190) | copy-start | bytes 6148
  88.8 85.1 %copy-start.17 = (s32[1024]{0:T(1024)}, s32[1024]{0:T(1024)S(1)}, u32[]{:S(2)}) copy-start(s32[1024]{0:T(1024)S(1)} %pad_clamp_fusion.1) | copy-start | bytes 12292
  129.2 21.9 %copy-start.114 = (f32[256]{0:T(256)}, f32[256]{0:T(256)S(1)}, u32[]{:S(2)}) copy-start(f32[256]{0:T(256)S(1)} %multiply_reduce_fusion.12) | copy-start | bytes 3076
  129.2 21.9 %copy-start.116 = (f32[256]{0:T(256)}, f32[256]{0:T(256)S(1)}, u32[]{:S(2)}) copy-start(f32[256]{0:T(256)S(1)} %fusion.302) | copy-start | bytes 3076
  130.4 33.8 %copy-start.15 = (bf16[256,768]{1,0:T(8,128)(2,1)}, bf16[256,768]{1,0:T(8,128)(2,1)S(1)}, u32[]{:S(2)}) copy-start(bf16[256,768]{1,0:T(8,128)(2,1)S(1)} %multiply_convert_fusion.26) | copy-start | bytes 1179652
  131.7 19.4 %all-to-all-start = ((bf16[16,32,768]{2,1,0:T(8,128)(2,1)}), bf16[16,32,768]{2,1,0:T(8,128)(2,1)S(1)}, u32[]{:S(2)}, u32[]{:S(2)}) async-start(bf16[16,32,768]{2,1,0:T(8,128)(2,1)} %convolution_convert_fusion.7), calls=%async_computation | async-start | bytes 1572864 | tf_op jit(solution)/shard_map/all_to_all | solution.py:519
  140.7 21.1 %copy-start.83 = (f32[256,2]{0,1:T(2,128)}, f32[256,2]{0,1:T(2,128)S(1)}, u32[]{:S(2)}) copy-start(f32[256,2]{0,1:T(2,128)S(1)} %select_reduce_fusion.3) | copy-start | bytes 6148
  140.7 21.1 %copy-start.97 = (f32[256]{0:T(256)}, f32[256]{0:T(256)S(1)}, u32[]{:S(2)}) copy-start(f32[256]{0:T(256)S(1)} %reduce_max.37) | copy-start | bytes 3076
  140.8 21.1 %copy-start.106 = (f32[256]{0:T(256)}, f32[256]{0:T(256)S(1)}, u32[]{:S(2)}) copy-start(f32[256]{0:T(256)S(1)} %fusion.299) | copy-start | bytes 3076
  157.0 16.6 %all-to-all-start.1 = ((bf16[2,256,768]{2,0,1:T(2,128)(2,1)}), bf16[2,256,768]{2,0,1:T(2,128)(2,1)S(1)}, u32[]{:S(2)}, u32[]{:S(2)}) async-start(bf16[2,256,768]{2,0,1:T(2,128)(2,1)} %copy.344), calls=%async_computation.1 | async-start | bytes 1572864 | tf_op jit(solution)/shard_map/all_to_all | solution.py:530
  161.4 62.3 %all-reduce.15.cloned.1.call-start = ((), (), s32[]{:S(2)}) async-start(), calls=%async_computation.13 | async-start | bytes 786432 | tf_op jit(solution)/shard_map/psum | solution.py:535
  178.8 44.9 %copy-start.33 = (bf16[256,768]{1,0:T(8,128)(2,1)S(1)}, bf16[256,768]{1,0:T(8,128)(2,1)}, u32[]{:S(2)}) copy-start(bf16[256,768]{1,0:T(8,128)(2,1)} %all-reduce.13.cloned.1.call-done) | copy-start | bytes 1179652
  184.4 119.2 %all-reduce.17.cloned.1.call-start = ((), (), s32[]{:S(2)}) async-start(), calls=%async_computation.14 | async-start | bytes 786432 | tf_op jit(solution)/shard_map/psum | solution.py:495
  223.6 19.9 %copy-start.48 = (bf16[192,768]{1,0:T(8,128)(2,1)S(1)}, bf16[192,768]{1,0:T(8,128)(2,1)}, u32[]{:S(2)}) copy-start(bf16[192,768]{1,0:T(8,128)(2,1)} %copy.348) | copy-start | bytes 884740
  223.6 20.2 %copy-start.49 = (bf16[192,768]{1,0:T(8,128)(2,1)S(1)}, bf16[192,768]{1,0:T(8,128)(2,1)}, u32[]{:S(2)}) copy-start(bf16[192,768]{1,0:T(8,128)(2,1)} %copy.349) | copy-start | bytes 884740
  224.9 32.7 %copy-start.111 = (f32[256]{0:T(256)}, f32[256]{0:T(256)S(1)}, u32[]{:S(2)}) copy-start(f32[256]{0:T(256)S(1)} %get-tuple-element.147) | copy-start | bytes 3076
  224.9 78.7 %copy-start.9 = (f32[256,768]{1,0:T(8,128)}, f32[256,768]{1,0:T(8,128)S(1)}, u32[]{:S(2)}) copy-start(f32[256,768]{1,0:T(8,128)S(1)} %get-tuple-element.148) | copy-start | bytes 2359300
  225.0 32.7 %copy-start.110 = (f32[256]{0:T(256)}, f32[256]{0:T(256)S(1)}, u32[]{:S(2)}) copy-start(f32[256]{0:T(256)S(1)} %fusion.303) | copy-start | bytes 3076
  225.1 32.5 %copy-start.13 = (bf16[256,768]{1,0:T(8,128)(2,1)}, bf16[256,768]{1,0:T(8,128)(2,1)S(1)}, u32[]{:S(2)}) copy-start(bf16[256,768]{1,0:T(8,128)(2,1)S(1)} %multiply_convert_fusion.25) | copy-start | bytes 1179652
  304.9 160.9 %copy-start.7 = (f32[256,768]{1,0:T(8,128)}, f32[256,768]{1,0:T(8,128)S(1)}, u32[]{:S(2)}) copy-start(f32[256,768]{1,0:T(8,128)S(1)} %get-tuple-element.146) | copy-start | bytes 2359300
  305.5 19.9 %copy-start.29 = (f32[512,768]{1,0:T(8,128)S(1)}, f32[512,768]{1,0:T(8,128)}, u32[]{:S(2)}) copy-start(f32[512,768]{1,0:T(8,128)} %mul.1000) | copy-start | bytes 4718596
  311.2 26.1 %all-to-all-start.2 = ((bf16[16,32,768]{2,1,0:T(8,128)(2,1)}), bf16[16,32,768]{2,1,0:T(8,128)(2,1)}, u32[]{:S(2)}, u32[]{:S(2)}) async-start(bf16[16,32,768]{2,1,0:T(8,128)(2,1)} %convolution_convert_fusion.6), calls=%async_computation.2 | async-start | bytes 1572864 | tf_op jit(solution)/shard_map/all_to_all | solution.py:519
  337.3 17.1 %all-to-all-start.4 = ((bf16[16,32,768]{2,1,0:T(8,128)(2,1)}), bf16[16,32,768]{2,1,0:T(8,128)(2,1)S(1)}, u32[]{:S(2)}, u32[]{:S(2)}) async-start(bf16[16,32,768]{2,1,0:T(8,128)(2,1)} %bitcast.87), calls=%async_computation.4 | async-start | bytes 1572864 | tf_op jit(solution)/shard_map/all_to_all | solution.py:629
  354.4 17.4 %all-to-all-start.3 = ((bf16[2,256,768]{2,0,1:T(2,128)(2,1)}), bf16[2,256,768]{2,0,1:T(2,128)(2,1)}, u32[]{:S(2)}, u32[]{:S(2)}) async-start(bf16[2,256,768]{2,0,1:T(2,128)(2,1)} %copy.353), calls=%async_computation.3 | async-start | bytes 1572864 | tf_op jit(solution)/shard_map/all_to_all | solution.py:530
  371.7 32.5 %all-to-all-start.5 = ((bf16[2,256,768]{2,0,1:T(2,128)(2,1)}), bf16[2,256,768]{2,0,1:T(2,128)(2,1)}, u32[]{:S(2)}, u32[]{:S(2)}) async-start(bf16[2,256,768]{2,0,1:T(2,128)(2,1)} %copy.360), calls=%async_computation.5 | async-start | bytes 1572864 | tf_op jit(solution)/shard_map/all_to_all | solution.py:643
  376.7 86.1 %all-reduce.19.cloned.1.call-start = ((), (), s32[]{:S(2)}) async-start(), calls=%async_computation.15 | async-start | bytes 786432 | tf_op jit(solution)/shard_map/psum | solution.py:648
  421.4 189.6 %reduce-scatter.13.cloned.1.call-start = ((), (), s32[]{:S(2)}) async-start(), calls=%async_computation.18 | async-start | bytes 884736
  480.4 150.6 %reduce-scatter.15.cloned.1.call-start = ((), (), s32[]{:S(2)}) async-start(), calls=%async_computation.19 | async-start | bytes 884736
  599.8 100.9 %all-reduce.21.cloned.1.call-start = ((), (), s32[]{:S(2)}) async-start(), calls=%async_computation.16 | async-start | bytes 786432 | tf_op jit(solution)/shard_map/psum | solution.py:736
  656.3 44.4 %copy-start.10 = (f32[256,768]{1,0:T(8,128)S(1)}, f32[256,768]{1,0:T(8,128)}, u32[]{:S(2)}) copy-start(f32[256,768]{1,0:T(8,128)} %copy-done.9) | copy-start | bytes 2359300
  721.7 20.8 %copy-start.26 = (f32[256,768]{1,0:T(8,128)S(1)}, f32[256,768]{1,0:T(8,128)}, u32[]{:S(2)}) copy-start(f32[256,768]{1,0:T(8,128)} %get-tuple-element.142) | copy-start | bytes 2359300
  730.2 26.8 %all-to-all-start.6 = ((bf16[16,32,768]{2,1,0:T(8,128)(2,1)}), bf16[16,32,768]{2,1,0:T(8,128)(2,1)}, u32[]{:S(2)}, u32[]{:S(2)}) async-start(bf16[16,32,768]{2,1,0:T(8,128)(2,1)} %bitcast.522), calls=%async_computation.6 | async-start | bytes 1572864 | tf_op jit(solution)/shard_map/all_to_all | solution.py:629
  758.2 94.7 %copy-start.126 = (bf16[2,2,768,512]{3,2,1,0:T(8,128)(2,1)S(1)}, bf16[2,2,768,512]{3,2,1,0:T(8,128)(2,1)}, u32[]{:S(2)}) copy-start(bf16[2,2,768,512]{3,2,1,0:T(8,128)(2,1)} %param.32) | copy-start | bytes 9437188
  873.7 33.7 %all-to-all-start.7 = ((bf16[2,256,768]{2,0,1:T(2,128)(2,1)}), bf16[2,256,768]{2,0,1:T(2,128)(2,1)S(1)}, u32[]{:S(2)}, u32[]{:S(2)}) async-start(bf16[2,256,768]{2,0,1:T(2,128)(2,1)} %copy.371), calls=%async_computation.7 | async-start | bytes 1572864 | tf_op jit(solution)/shard_map/all_to_all | solution.py:643
  879.6 76.6 %all-reduce.23.cloned.1.call-start = ((), (), s32[]{:S(2)}) async-start(), calls=%async_computation.17 | async-start | bytes 786432 | tf_op jit(solution)/shard_map/psum | solution.py:648
  917.4 38.8 %copy-start.6 = (bf16[2,128,768]{2,1,0:T(8,128)(2,1)S(1)}, bf16[2,128,768]{2,1,0:T(8,128)(2,1)}, u32[]{:S(2)}) copy-start(bf16[2,128,768]{2,1,0:T(8,128)(2,1)} %param.18) | copy-start | bytes 1179652
  917.4 38.8 %copy-start.34 = (bf16[256,768]{1,0:T(8,128)(2,1)S(1)}, bf16[256,768]{1,0:T(8,128)(2,1)}, u32[]{:S(2)}) copy-start(bf16[256,768]{1,0:T(8,128)(2,1)} %all-reduce.13.cloned.1.call-done) | copy-start | bytes 1179652
  917.4 38.8 %copy-start.90 = (f32[768]{0:T(1024)S(1)}, f32[768]{0:T(1024)}, u32[]{:S(2)}) copy-start(f32[768]{0:T(1024)} %copy-done.89) | copy-start | bytes 9220
  917.4 38.7 %copy-start.96 = (bf16[256,16]{0,1:T(8,128)(2,1)S(1)}, bf16[256,16]{0,1:T(8,128)(2,1)}, u32[]{:S(2)}) copy-start(bf16[256,16]{0,1:T(8,128)(2,1)} %select_reduce_fusion) | copy-start | bytes 24580
  917.4 38.7 %copy-start.117 = (f32[256]{0:T(256)S(1)}, f32[256]{0:T(256)}, u32[]{:S(2)}) copy-start(f32[256]{0:T(256)} %copy-done.116) | copy-start | bytes 3076
  917.4 41.0 %copy-start.115 = (f32[256]{0:T(256)S(1)}, f32[256]{0:T(256)}, u32[]{:S(2)}) copy-start(f32[256]{0:T(256)} %copy-done.114) | copy-start | bytes 3076
  917.4 41.0 %copy-start.27 = (f32[256,768]{1,0:T(8,128)S(1)}, f32[256,768]{1,0:T(8,128)}, u32[]{:S(2)}) copy-start(f32[256,768]{1,0:T(8,128)} %get-tuple-element.142) | copy-start | bytes 2359300
  917.4 184.2 %reduce-scatter.19.cloned.1.call-start = ((), (), s32[]{:S(2)}) async-start(), calls=%async_computation.21 | async-start | bytes 884736
  926.2 33.9 %copy-start.87 = (f32[2,3,128]{2,1,0:T(4,128)S(1)}, f32[2,3,128]{2,1,0:T(4,128)}, u32[]{:S(2)}) copy-start(f32[2,3,128]{2,1,0:T(4,128)} %log_add_fusion) | copy-start | bytes 9220
  1066.9 64.3 %reduce-scatter.17.cloned.1.call-start = ((), (), s32[]{:S(2)}) async-start(), calls=%async_computation.20 | async-start | bytes 884736
  1087.3 95.4 %all-reduce.25.cloned.1.call-start = ((), (), s32[]{:S(2)}) async-start(), calls=%async_computation.22 | async-start | bytes 1572864 | tf_op jit(solution)/shard_map/psum | solution.py:535
  1141.9 40.8 %copy-start.86 = (f32[768]{0:T(1024)S(1)}, f32[768]{0:T(1024)}, u32[]{:S(2)}) copy-start(f32[768]{0:T(1024)} %copy-done.85) | copy-start | bytes 9220
  1141.9 40.8 %copy-start.113 = (f32[256]{0:T(256)S(1)}, f32[256]{0:T(256)}, u32[]{:S(2)}) copy-start(f32[256]{0:T(256)} %bitcast_rsqrt_fusion) | copy-start | bytes 3076
  1145.7 38.6 %copy-start.43 = (bf16[768,46]{1,0:T(8,128)(2,1)S(1)}, bf16[768,46]{1,0:T(8,128)(2,1)}, u32[]{:S(2)}) copy-start(bf16[768,46]{1,0:T(8,128)(2,1)} %broadcast.606) | copy-start | bytes 211972
  1145.7 38.6 %copy-start.62 = (bf16[768,16]{1,0:T(8,128)(2,1)S(1)}, bf16[768,16]{1,0:T(8,128)(2,1)}, u32[]{:S(2)}) copy-start(bf16[768,16]{1,0:T(8,128)(2,1)} %copy.380) | copy-start | bytes 73732
  1186.3 40.2 %copy-start.8 = (f32[256,768]{1,0:T(8,128)S(1)}, f32[256,768]{1,0:T(8,128)}, u32[]{:S(2)}) copy-start(f32[256,768]{1,0:T(8,128)} %copy-done.7) | copy-start | bytes 2359300
  1186.3 40.2 %copy-start.75 = (bf16[256,768]{1,0:T(8,128)(2,1)S(1)}, bf16[256,768]{1,0:T(8,128)(2,1)}, u32[]{:S(2)}) copy-start(bf16[256,768]{1,0:T(8,128)(2,1)} %get-tuple-element.139) | copy-start | bytes 1179652
  1186.3 41.2 %copy-start.103 = (f32[2,128]{1,0:T(2,128)S(1)}, f32[2,128]{1,0:T(2,128)}, u32[]{:S(2)}) copy-start(f32[2,128]{1,0:T(2,128)} %copy-done.102) | copy-start | bytes 3076
  1186.3 41.2 %copy-start.44 = (bf16[256,768]{1,0:T(8,128)(2,1)S(1)}, bf16[256,768]{1,0:T(8,128)(2,1)}, u32[]{:S(2)}) copy-start(bf16[256,768]{1,0:T(8,128)(2,1)} %get-tuple-element.140) | copy-start | bytes 1179652
  (103 other events, 569.4 us)
Sparse Core Ops, SparseCore 0:
  87.9 39.9 all-reduce.12
  184.6 39.0 all-reduce.14
  263.6 39.9 all-reduce.16
  421.5 41.2 all-reduce.18
  480.5 31.0 reduce-scatter.12
  599.9 31.0 reduce-scatter.14
  658.6 41.9 all-reduce.20
  917.5 38.5 all-reduce.22
  1067.0 31.0 reduce-scatter.18
  1101.0 30.1 reduce-scatter.16
  1138.1 44.6 all-reduce.24

commit v2 on v1

v2 whole, which is shorter than its diff:
```python
import functools

import jax
import jax.numpy as jnp
from jax import lax
from jax.experimental import pallas as pl
from jax.experimental.pallas import tpu as pltpu
from jax.sharding import PartitionSpec as P

HD = 64
MESH = pl.DeviceIdType.MESH
BF = jnp.bfloat16
F32 = jnp.float32
WIDE = 2432
CHUNK = 48
VM = pl.BlockSpec(memory_space=pltpu.VMEM)


def place():
    y = lax.axis_index("dp")
    e = lax.axis_index("ep")
    z = lax.axis_index("tp")
    return y, e // 2, e % 2, z


def device(y, x, c, z):
    return (y, x * 2 + c, z)


def meet(givers, takers):
    barrier = pltpu.get_barrier_semaphore()
    for who in givers:
        pl.semaphore_signal(barrier, inc=1, device_id=who, device_id_type=MESH)
    pl.semaphore_wait(barrier, takers)


class Line:
    def __init__(self, send_sems, recv_sems):
        self.send_sems, self.recv_sems, self.used, self.open = send_sems, recv_sems, 0, []

    def start(self, src, dst, who):
        at = self.used
        self.used += 1
        copy = pltpu.make_async_remote_copy(
            src_ref=src,
            dst_ref=dst,
            send_sem=self.send_sems.at[at],
            recv_sem=self.recv_sems.at[at],
            device_id=who,
            device_id_type=MESH,
        )
        copy.start()
        self.open.append(copy)
        return copy

    def finish(self):
        for copy in self.open:
            copy.wait_send()


def gather_kernel(src, out, land, send_sems, recv_sems):
    y, x, c, z = place()

    def at(j, d, core=None):
        yy = (y + j * c + d * (1 - c) + 8) % 4
        xx = (x + j * (1 - c) + d * c + 8) % 4
        return yy, xx

    def who(j, d):
        yy, xx = at(j, d)
        return device(yy, xx, c, z)

    def slot(j, d):
        yy, xx = at(j, d)
        return yy * 8 + xx * 2 + c

    sibling = device(y, x, 1 - c, z)
    near = [who(1, 0), who(-1, 0), who(0, 1), who(0, -1), sibling]
    meet(near, 5)
    line = Line(send_sems, recv_sems)
    sib = []

    def spread(ref, j):
        plus = line.start(ref, land.at[slot(j, 0)], who(0, 1))
        minus = line.start(ref, land.at[slot(j, 0)], who(0, -1))
        sib.append(line.start(ref, land.at[slot(j, 0)], sibling))
        return plus, minus

    first_plus = line.start(src, land.at[slot(0, 0)], who(1, 0))
    first_minus = line.start(src, land.at[slot(0, 0)], who(-1, 0))
    second = {0: spread(src, 0)}
    land[slot(0, 0)] = src[...]
    first_plus.wait_recv()
    below = land.at[slot(-1, 0)]
    on_plus = line.start(below.at[pl.ds(0, 32)], below.at[pl.ds(0, 32)], who(1, 0))
    second[-1] = spread(below, -1)
    first_minus.wait_recv()
    above = land.at[slot(1, 0)]
    on_minus = line.start(above.at[pl.ds(32, 16)], above.at[pl.ds(32, 16)], who(-1, 0))
    second[1] = spread(above, 1)
    on_plus.wait_recv()
    on_minus.wait_recv()
    second[2] = spread(land.at[slot(2, 0)], 2)
    far = []
    for j in (0, -1, 1, 2):
        plus, minus = second[j]
        plus.wait_recv()
        got = land.at[slot(j, -1)]
        sib.append(line.start(got, got, sibling))
        if j in (0, -1):
            far.append((j, line.start(got, got, who(0, 1))))
        minus.wait_recv()
        got = land.at[slot(j, 1)]
        sib.append(line.start(got, got, sibling))
        if j in (1, 2):
            far.append((j, line.start(got, got, who(0, -1))))
    for j, copy in far:
        copy.wait_recv()
        got = land.at[slot(j, 2)]
        sib.append(line.start(got, got, sibling))
    for copy in sib:
        copy.wait_recv()
    line.finish()

    def unpack(p, carry):
        one = land[2 * p].astype(F32)
        two = land[2 * p + 1].astype(F32)
        rows = pl.ds(pl.multiple_of(p * CHUNK, CHUNK), CHUNK)
        out[0, rows] = jnp.concatenate([one[:24], two[:24]], axis=0).astype(BF)
        out[1, rows] = jnp.concatenate([one[24:], two[24:]], axis=0).astype(BF)
        return carry

    lax.fori_loop(0, 16, unpack, 0)


def gather_weights(src):
    return pl.pallas_call(
        gather_kernel,
        out_shape=jax.ShapeDtypeStruct((2, 768, WIDE), BF),
        in_specs=[VM],
        out_specs=VM,
        scratch_shapes=[
            pltpu.VMEM((32, CHUNK, WIDE), BF),
            pltpu.SemaphoreType.DMA((32,)),
            pltpu.SemaphoreType.DMA((32,)),
        ],
        compiler_params=pltpu.CompilerParams(
            collective_id=0, has_side_effects=True, vmem_limit_bytes=48 * 2**20
        ),
        name="gather_weights",
    )(src)


EPS = 1e-06
WIDTHS = (256, 640, 1024, 512)
SMALL = slice(128, 256)
ROUTER = 64
GAIN = 80
OUT = slice(0, 192)
QKV = slice(256, 896)
GATEUP = slice(896, 1920)
GATE = slice(896, 1408)
UP = slice(1408, 1920)
DOWN = slice(1920, 2432)


def mm(a, b):
    return lax.dot_general(a, b, (((1,), (0,)), ((), ())), preferred_element_type=F32)


def mm_t(a, b):
    return lax.dot_general(a, b, (((1,), (1,)), ((), ())), preferred_element_type=F32)


def t_mm(a, b):
    return lax.dot_general(a, b, (((0,), (0,)), ((), ())), preferred_element_type=F32)


def lanes(shape):
    return lax.broadcasted_iota(jnp.int32, shape, 1)


def gain_rows(weights):
    pick = (lanes((8, 128)) == lax.broadcasted_iota(jnp.int32, (8, 128), 0) + GAIN).astype(BF)
    return mm_t(pick, weights[:, SMALL])


def rms(values, gain):
    turn = lax.rsqrt(jnp.mean(values * values, axis=-1, keepdims=True) + EPS)
    return values * turn * gain


def rms_back(values, gain, grad):
    turn = lax.rsqrt(jnp.mean(values * values, axis=-1, keepdims=True) + EPS)
    scaled = grad * gain
    back = turn * scaled - values * (turn * turn * turn) * jnp.mean(values * scaled, axis=-1, keepdims=True)
    return back, jnp.sum(grad * values * turn, axis=0, keepdims=True)


def turned(values, cosine, sine):
    width = values.shape[1]
    front = lanes(values.shape) % HD < HD // 2
    other = jnp.where(front, pltpu.roll(values, width - HD // 2, 1), pltpu.roll(values, HD // 2, 1))
    return values * cosine + other * sine


def sigmoid(v):
    return 1.0 / (1.0 + jnp.exp(-v))


def swish_back(gate, up, grad):
    s = sigmoid(gate)
    return (grad * up * s * (1.0 + gate * (1.0 - s))).astype(BF), (grad * gate * s).astype(BF)


def two(values):
    return jnp.concatenate([values, values], axis=0)


def scatter_kernel(*refs):
    ins, gains, outs = refs[:8], refs[8:10], refs[10:14]
    chunks, sib_land, plus_far, minus_far, plus_near, minus_near, one_far, one_near, columns, send_sems, recv_sems = refs[14:]
    y, x, c, z = place()

    def at(j, d):
        yy = (y + j * c + d * (1 - c) + 8) % 4
        xx = (x + j * (1 - c) + d * c + 8) % 4
        return yy, xx

    def who(j, d):
        yy, xx = at(j, d)
        return device(yy, xx, c, z)

    def slot(j, d, core):
        yy, xx = at(j, d)
        return yy * 8 + xx * 2 + core

    sibling = device(y, x, 1 - c, z)
    meet([who(1, 0), who(-1, 0), who(0, 1), who(0, -1), sibling], 5)

    spot = lanes((8, 256)) == lax.broadcasted_iota(jnp.int32, (8, 256), 0) + 128 + GAIN

    def pack(p, carry):
        rows = pl.ds(pl.multiple_of(p * CHUNK, CHUNK), CHUNK)
        left = 0
        for part, width in enumerate(WIDTHS):
            one = ins[part][rows].astype(F32)
            two = ins[4 + part][rows].astype(F32)
            if part == 0:
                one += columns[0, rows]
                two += columns[1, rows]
            cols = slice(left, left + width)
            chunks[2 * p, :, cols] = jnp.concatenate([one[:24], two[:24]], axis=0).astype(BF)
            chunks[2 * p + 1, :, cols] = jnp.concatenate([one[24:], two[24:]], axis=0).astype(BF)
            left += width
        return carry

    for layer in range(2):
        columns[layer] = t_mm(gains[layer][...].astype(BF), spot.astype(BF))
    lax.fori_loop(0, 16, pack, 0)
    line = Line(send_sems, recv_sems)
    order = [(j, d) for d in (2, 1, -1, 0) for j in (0, -1, 1, 2)]
    swapped = {}
    for n, (j, d) in enumerate(order):
        yy = (y + j * (1 - c) + d * c + 8) % 4
        xx = (x + j * c + d * (1 - c) + 8) % 4
        swapped[j, d] = line.start(chunks.at[yy * 8 + xx * 2 + 1 - c], sib_land.at[n], sibling)

    def join(j, d):
        n = order.index((j, d))
        swapped[j, d].wait_recv()
        mine = slot(j, d, c)
        chunks[mine] = (chunks[mine].astype(F32) + sib_land[n].astype(F32)).astype(BF)
        return chunks.at[mine]

    plus_set, minus_set = (0, -1), (1, 2)
    far = {}
    for j in (0, -1, 1, 2):
        ref = join(j, 2)
        if j in plus_set:
            far[j] = line.start(ref, plus_far.at[plus_set.index(j)], who(0, 1))
        else:
            far[j] = line.start(ref, minus_far.at[minus_set.index(j)], who(0, -1))
    near = {}
    for j in (1, 2):
        near[j, 1] = line.start(join(j, 1), plus_near.at[j], who(0, 1))
    for j in (0, -1):
        near[j, -1] = line.start(join(j, -1), minus_near.at[j % 4], who(0, -1))
    for j in plus_set:
        ref = join(j, 1)
        far[j].wait_recv()
        ref[...] = (ref[...].astype(F32) + plus_far[plus_set.index(j)].astype(F32)).astype(BF)
        near[j, 1] = line.start(ref, plus_near.at[j % 4], who(0, 1))
    for j in minus_set:
        ref = join(j, -1)
        far[j].wait_recv()
        ref[...] = (ref[...].astype(F32) + minus_far[minus_set.index(j)].astype(F32)).astype(BF)
        near[j, -1] = line.start(ref, minus_near.at[j], who(0, -1))
    held = {}
    for j in (2, 1, -1, 0):
        ref = join(j, 0)
        near[j, 1].wait_recv()
        near[j, -1].wait_recv()
        total = ref[...].astype(F32) + plus_near[j % 4].astype(F32) + minus_near[j % 4].astype(F32)
        ref[...] = total.astype(BF)
        held[j] = ref
        if j == 2:
            a = line.start(ref.at[pl.ds(0, 32)], one_far.at[pl.ds(0, 32)], who(1, 0))
            b = line.start(ref.at[pl.ds(32, 16)], one_far.at[pl.ds(32, 16)], who(-1, 0))
    a.wait_recv()
    up = held[1].at[pl.ds(0, 32)]
    up[...] = (up[...].astype(F32) + one_far[:32].astype(F32)).astype(BF)
    last_plus = line.start(held[1], one_near.at[0], who(1, 0))
    b.wait_recv()
    down = held[-1].at[pl.ds(32, 16)]
    down[...] = (down[...].astype(F32) + one_far[32:].astype(F32)).astype(BF)
    last_minus = line.start(held[-1], one_near.at[1], who(-1, 0))
    last_plus.wait_recv()
    last_minus.wait_recv()
    left = 0
    for part, width in enumerate(WIDTHS):
        cols = slice(left, left + width)
        total = held[0][:, cols].astype(F32) + one_near[0, :, cols].astype(F32) + one_near[1, :, cols].astype(F32)
        outs[part][0] = total[:24]
        outs[part][1] = total[24:]
        left += width
    line.finish()


def scatter_grads(parts):
    chunk = lambda n: pltpu.VMEM((n, CHUNK, WIDE), BF)
    return pl.pallas_call(
        scatter_kernel,
        out_shape=[jax.ShapeDtypeStruct((2, 24, width), F32) for width in WIDTHS],
        in_specs=[VM] * 10,
        out_specs=[VM] * 4,
        scratch_shapes=[
            chunk(32),
            chunk(16),
            chunk(2),
            chunk(2),
            chunk(4),
            chunk(4),
            pltpu.VMEM((CHUNK, WIDE), BF),
            chunk(2),
            pltpu.VMEM((2, 768, 256), F32),
            pltpu.SemaphoreType.DMA((32,)),
            pltpu.SemaphoreType.DMA((32,)),
        ],
        compiler_params=pltpu.CompilerParams(
            collective_id=1, has_side_effects=True, vmem_limit_bytes=56 * 2**20
        ),
        name="scatter_grads",
    )(*parts)


def rows_kernel(a0, a1, b0, b1, o0, o1, o2, o3, send_sems, recv_sems):
    y, x, c, z = place()

    def along(dy, dz):
        return device((y + dy + 4) % 4, x, c, (z + dz + 4) % 4)

    meet([along(1, 0), along(-1, 0), along(0, 1), along(0, -1)], 4)
    line = Line(send_sems, recv_sems)

    def quarter(k, first, count):
        return pl.ds(pl.multiple_of(((z + k + 4) % 4) * 64 + first, 32), count)

    work = list(zip((a0, a1, b0, b1), (o0, o1, o2, o3)))
    near, half, full, spread = [], [], [], []
    for src, out in work:
        mine = src.at[0, quarter(0, 0, 64)]
        near.append(
            (
                line.start(mine, out.at[0, 1, quarter(0, 0, 64)], along(1, 0)),
                line.start(mine, out.at[0, 3, quarter(0, 0, 64)], along(-1, 0)),
            )
        )
        full.append(
            (
                line.start(src.at[1], out.at[1, 1], along(1, 0)),
                line.start(src.at[1], out.at[1, 3], along(-1, 0)),
            )
        )
    for (src, out), (plus, minus) in zip(work, near):
        plus.wait_recv()
        p = line.start(out.at[0, 1, quarter(0, 0, 32)], out.at[0, 2, quarter(0, 0, 32)], along(1, 0))
        minus.wait_recv()
        m = line.start(out.at[0, 3, quarter(0, 32, 32)], out.at[0, 2, quarter(0, 32, 32)], along(-1, 0))
        half.append((p, m))
    for (src, out), (plus, minus) in zip(work, half):
        plus.wait_recv()
        minus.wait_recv()
        got = out.at[0, pl.ds(1, 3), quarter(0, 0, 64)]
        spread.append((line.start(got, got, along(0, 1)), line.start(got, got, along(0, -1))))
    last = []
    for (src, out), (plus, minus) in zip(work, full):
        plus.wait_recv()
        p = line.start(out.at[1, 1, pl.ds(0, 128)], out.at[1, 2, pl.ds(0, 128)], along(1, 0))
        minus.wait_recv()
        m = line.start(out.at[1, 3, pl.ds(128, 128)], out.at[1, 2, pl.ds(128, 128)], along(-1, 0))
        last += [p, m]
    for (src, out), (plus, minus) in zip(work, spread):
        plus.wait_recv()
        got = out.at[0, pl.ds(1, 3), quarter(-1, 0, 32)]
        last.append(line.start(got, got, along(0, 1)))
        minus.wait_recv()
        got = out.at[0, pl.ds(1, 3), quarter(1, 32, 32)]
        last.append(line.start(got, got, along(0, -1)))
        out[:, 0] = src[...]
    for copy in last:
        copy.wait_recv()
    line.finish()


def gather_rows(arrays):
    shape = jax.ShapeDtypeStruct((2, 4, 256, 768), BF)
    return pl.pallas_call(
        rows_kernel,
        out_shape=[shape] * 4,
        in_specs=[VM] * 4,
        out_specs=[VM] * 4,
        scratch_shapes=[pltpu.SemaphoreType.DMA((48,)), pltpu.SemaphoreType.DMA((48,))],
        compiler_params=pltpu.CompilerParams(
            collective_id=2, has_side_effects=True, vmem_limit_bytes=48 * 2**20
        ),
        name="gather_rows",
    )(*arrays)


class Wires:
    def __init__(self, sends, recvs):
        self.sends, self.recvs, self.used, self.open = sends, recvs, 0, []

    def plan(self, src, dst, who, when=None):
        at = self.used
        self.used += 1
        copy = pltpu.make_async_remote_copy(
            src_ref=src,
            dst_ref=dst,
            send_sem=self.sends.at[at],
            recv_sem=self.recvs.at[at],
            device_id=who,
            device_id_type=MESH,
        )
        self.open.append((copy, when))
        return copy

    def go(self, src, dst, who):
        copy = self.plan(src, dst, who)
        copy.start()
        return copy

    def finish(self):
        for copy, when in self.open:
            if when is None:
                copy.wait_send()
            else:
                pl.when(when)(copy.wait_send)


def peers(y, e, z):
    row = [(y, (e + k) % 8, z) for k in range(1, 8)]
    return row, [(y, e, (z + k) % 4) for k in range(1, 4)]


def spread_rows(wires, held, y, e, z):
    sent = [wires.go(held.at[z], held.at[z], (y, e, (z + k) % 4)) for k in (2, 1, 3)]
    return lambda: [copy.wait_recv() for copy in sent]


def sum_rows(wires, parts, land, y, e, z):
    sent = []
    for k in (2, 1, 3):
        who = (z + k) % 4
        sent.append(wires.go(parts.at[who], land.at[k - 1], (y, e, who)))

    def total():
        for copy in sent:
            copy.wait_recv()
        return (
            parts[z].astype(F32) + land[0].astype(F32) + land[1].astype(F32) + land[2].astype(F32)
        )

    return total


def scatter_experts(wires, src, dst, y, e, z, i):
    rows = pl.ds(pl.multiple_of(e * 32, 32), 32)
    sent = []
    for k in (4, 3, 5, 2, 6, 1, 7):
        who = (e + k) % 8
        sent.append(wires.go(src.at[2 * who + i], dst.at[i, rows], (y, who, z)))
    dst[i, rows] = src[2 * e + i]
    return lambda: [copy.wait_recv() for copy in sent]


def return_experts(wires, src, dst, y, e, z, i):
    sent = []
    for k in (4, 3, 5, 2, 6, 1, 7):
        who = (e + k) % 8
        rows = pl.ds(pl.multiple_of(who * 32, 32), 32)
        sent.append(wires.go(src.at[i, rows], dst.at[2 * e + i], (y, who, z)))
    dst[2 * e + i] = src[i, pl.ds(pl.multiple_of(e * 32, 32), 32)]
    return lambda: [copy.wait_recv() for copy in sent]


def picks(route):
    slots = lanes((256, 512))
    return slots == route[:, 0:1], slots == route[:, 1:2]


def forward_kernel(
    layer, stream, own, lengths, route, cos, sin, w_all, eg_all, eu_all, ed_all,
    normed, queries, kv, probs, attended, middle, ffn_in, gud, gue, ret, shares, arrived, own_out, stream_out,
    w, eg, eu, ed, part, land, sent, made, local, sends, recvs,
):
    y, x, c, z = place()
    e = 2 * x + c
    row, column = peers(y, e, z)
    fetch = [
        pltpu.make_async_copy(src.at[layer], dst, local.at[n])
        for n, (src, dst) in enumerate(((w_all, w), (eg_all, eg), (eu_all, eu), (ed_all, ed)))
    ]
    for copy in fetch:
        copy.start()
    meet(row + column, 10)
    wires = Wires(sends, recvs)
    fetch[0].wait()
    gains = gain_rows(w)
    values = stream[...].reshape(256, 768).astype(F32)
    normed[...] = rms(values, gains[0:1]).astype(BF)
    lin = turned(mm(normed[...], w[:, QKV]), two(cos[...]), two(sin[...])).astype(BF)
    kv[e] = lin[:, :384]
    queries[...] = lin[:, 384:576]
    sibling = (y, e + 1 - 2 * c, z)
    first, second = [], []
    for k in (2, 3, 1):
        ahead, behind = x + k <= 3, x - k >= 0
        copy = wires.plan(kv.at[e], kv.at[e], (y, (e + 2 * k) % 8, z), ahead)
        pl.when(ahead)(copy.start)
        first.append((k, behind, copy))
    to_core = wires.plan(kv.at[e], kv.at[e], sibling, c == 0)
    pl.when(c == 0)(to_core.start)
    for j in range(8):

        @pl.when(j > e)
        def _():
            kv[j] = jnp.zeros((256, 384), BF)

    for k, behind, copy in reversed(first):
        slot = (e + 8 - 2 * k) % 8
        on = wires.plan(kv.at[slot], kv.at[slot], sibling, behind)

        @pl.when(behind)
        def _():
            copy.wait_recv()
            on.start()

        second.append((behind, on))
    pl.when(c == 1)(to_core.wait_recv)
    for behind, on in second:
        pl.when(behind)(on.wait_recv)
    at_key = lanes((128, 1024))
    at_query = lax.broadcasted_iota(jnp.int32, (128, 1024), 0) + e * 128
    for s in range(2):
        rows = slice(s * 128, s * 128 + 128)
        allowed = (at_key <= at_query) & (at_key < lengths[s : s + 1, 0:1])
        for h in range(3):
            keys = kv[:, rows, 64 * h : 64 * h + 64].reshape(1024, 64)
            vals = kv[:, rows, 192 + 64 * h : 256 + 64 * h].reshape(1024, 64)
            scores = jnp.where(allowed, mm_t(queries[rows, 64 * h : 64 * h + 64], keys) * HD**-0.5, -1e30)
            expd = jnp.exp(scores - jnp.max(scores, axis=-1, keepdims=True))
            low = (expd / jnp.sum(expd, axis=-1, keepdims=True)).astype(BF)
            probs[3 * s + h] = low
            attended[rows, 64 * h : 64 * h + 64] = mm(low, vals).astype(BF)
    part[0] = mm_t(attended[...], w[:, OUT]).astype(BF).reshape(4, 64, 768)
    total = sum_rows(wires, part.at[0], land.at[0], y, e, z)()
    middle[...] = own[...] + total
    ffn_in[z] = rms(middle[...], gains[1:2]).astype(BF)
    spread_rows(wires, ffn_in, y, e, z)()
    rows_in = ffn_in[...].reshape(256, 768)
    ids = route[...]
    pick0, pick1 = picks(ids)
    sent[...] = t_mm((pick0 | pick1).astype(BF), rows_in).astype(BF).reshape(16, 32, 768)
    coming = [scatter_experts(wires, sent, arrived, y, e, z, i) for i in range(2)]
    logits = mm(rows_in, w[:, SMALL])
    lane = lanes((256, 128))
    chosen = [
        jnp.sum(jnp.where(lane == ids[:, 2 + j : 3 + j] + ROUTER, logits, 0.0), axis=-1, keepdims=True)
        for j in range(2)
    ]
    top = jnp.maximum(chosen[0], chosen[1])
    expd = [jnp.exp(v - top) for v in chosen]
    share = [v / (expd[0] + expd[1]) for v in expd]
    shares[...] = jnp.where(lane == 0, share[0], jnp.where(lane == 1, share[1], 0.0))
    gud[...] = mm(rows_in, w[:, GATEUP])
    gate, up = gud[:, :512], gud[:, 512:]
    hidden = (gate * sigmoid(gate) * up).astype(BF)
    dense = mm_t(hidden, w[:, DOWN])
    for copy in fetch[1:]:
        copy.wait()
    back = []
    for i in range(2):
        coming[i]()
        gue[i, :, :512] = mm(arrived[i], eg[i])
        gue[i, :, 512:] = mm(arrived[i], eu[i])
        gate, up = gue[i, :, :512], gue[i, :, 512:]
        hidden = (gate * sigmoid(gate) * up).astype(BF)
        made[i] = mm(hidden, ed[i]).astype(BF)
        back.append(return_experts(wires, made, ret, y, e, z, i))
    for wait in back:
        wait()
    mix = (jnp.where(pick0, share[0], 0.0) + jnp.where(pick1, share[1], 0.0)).astype(BF)
    moe = mm(mix, ret[...].reshape(512, 768))
    part[1] = (dense + moe).astype(BF).reshape(4, 64, 768)
    total = sum_rows(wires, part.at[1], land.at[1], y, e, z)()
    result = middle[...] + total
    own_out[...] = result
    stream_out[z] = result.astype(BF)
    spread_rows(wires, stream_out, y, e, z)()
    wires.finish()


def backward_kernel(
    layer, incoming, grad_own, own, middle, normed, queries, kv, probs, attended, ffn_in, gud, gue, ret, shares, route, cos, sin,
    w_all, eg_all, eu_all, ed_all,
    grad_os, grad_qkv, grad_gu, grad_d, grad_gain, arrived, down_own, down_stream,
    w, eg, eu, ed, part_ffn, land_ffn, part, land, sent, made, sret, gathered, tail, dkv, sib_land, owner_land, lin,
    local, sends, recvs,
):
    y, x, c, z = place()
    e = 2 * x + c
    row, column = peers(y, e, z)
    fetch = [
        pltpu.make_async_copy(src.at[layer], dst, local.at[n])
        for n, (src, dst) in enumerate(((w_all, w), (eg_all, eg), (eu_all, eu), (ed_all, ed)))
    ]
    for copy in fetch:
        copy.start()
    meet(row + column, 10)
    wires = Wires(sends, recvs)
    mine = pl.ds(pl.multiple_of(z * 64, 64), 64)
    ffn_grad = incoming[...].reshape(256, 768)
    rows_in = ffn_in[...].reshape(256, 768)
    pick0, pick1 = picks(route[...])
    mix = (jnp.where(pick0, shares[:, 0:1], 0.0) + jnp.where(pick1, shares[:, 1:2], 0.0)).astype(BF)
    sent[...] = t_mm(mix, ffn_grad).astype(BF).reshape(16, 32, 768)
    coming = [scatter_experts(wires, sent, arrived, y, e, z, i) for i in range(2)]
    fetch[0].wait()
    gains = gain_rows(w)
    gate, up = gud[:, :512], gud[:, 512:]
    hidden_dense = (gate * sigmoid(gate) * up).astype(BF)
    gate_grad, up_grad = swish_back(gate, up, mm(ffn_grad, w[:, DOWN]))
    gu_grad = jnp.concatenate([gate_grad, up_grad], axis=1)
    dense = mm_t(gu_grad, w[:, GATEUP])
    match = mm_t(ffn_grad, ret[...].reshape(512, 768))
    share_grad = [
        jnp.sum(jnp.where(pick, match, 0.0), axis=-1, keepdims=True) for pick in (pick0, pick1)
    ]
    lane = lanes((256, 128))
    extra = jnp.where(lane == 0, share_grad[0], jnp.where(lane == 1, share_grad[1], 0.0))
    part_ffn[:, :, 768:] = extra.astype(BF).reshape(4, 64, 128)
    for copy in fetch[1:]:
        copy.wait()
    back = []
    for i in range(2):
        coming[i]()
        hidden_grad = mm_t(arrived[i], ed[i])
        gate_e, up_e = swish_back(gue[i, :, :512], gue[i, :, 512:], hidden_grad)
        made[i] = (mm_t(gate_e, eg[i]) + mm_t(up_e, eu[i])).astype(BF)
        back.append(return_experts(wires, made, sret, y, e, z, i))
    grad_gu[...] = t_mm(rows_in, gu_grad).astype(BF)
    grad_d[...] = t_mm(ffn_grad, hidden_dense).astype(BF)
    for wait in back:
        wait()
    dense += mm((pick0 | pick1).astype(BF), sret[...].reshape(512, 768))
    part_ffn[:, :, :768] = dense.astype(BF).reshape(4, 64, 768)
    total = sum_rows(wires, part_ffn, land_ffn, y, e, z)()
    input_sum = total[:, :768]
    share = shares[mine]
    ids = route[mine]
    weigh = share[:, 0:1] * total[:, 768:769] + share[:, 1:2] * total[:, 769:770]
    lane = lanes((64, 128))
    logit_grad = jnp.zeros((64, 128), F32)
    for j in range(2):
        chosen_grad = share[:, j : j + 1] * (total[:, 768 + j : 769 + j] - weigh)
        logit_grad += jnp.where(lane == ids[:, 2 + j : 3 + j] + ROUTER, chosen_grad, 0.0)
    logit_grad = logit_grad.astype(BF)
    back_norm, gain_two = rms_back(middle[...], gains[1:2], input_sum + mm_t(logit_grad, w[:, SMALL]))
    middle_grad = grad_own[...] + back_norm
    down_own[...] = middle_grad
    top = lax.broadcasted_iota(jnp.int32, (16, 768), 0) == 0
    gathered[z, :64, :768] = middle_grad.astype(BF)
    gathered[z, :64, 768:] = logit_grad
    gathered[z, 64:, :768] = jnp.where(top, gain_two, 0.0).astype(BF)
    gathered[z, 64:, 768:] = jnp.zeros((16, 128), BF)
    spread_rows(wires, gathered, y, e, z)()
    attn_grad = gathered[:, :64, :768].reshape(256, 768)
    attended_grad = mm(attn_grad, w[:, OUT]).astype(BF)
    for s in range(2):
        rows = slice(s * 128, s * 128 + 128)
        for h in range(3):
            cols = slice(64 * h, 64 * h + 64)
            late = slice(192 + 64 * h, 256 + 64 * h)
            keys = kv[:, rows, cols].reshape(1024, 64)
            vals = kv[:, rows, late].reshape(1024, 64)
            low = probs[3 * s + h]
            wide = low.astype(F32)
            grad_here = attended_grad[rows, cols]
            probs_grad = mm_t(grad_here, vals)
            kept = jnp.sum(wide * probs_grad, axis=-1, keepdims=True)
            score_grad = (wide * (probs_grad - kept)).astype(BF)
            lin[rows, 384 + 64 * h : 448 + 64 * h] = mm(score_grad, keys) * HD**-0.5
            keys_grad = t_mm(score_grad, queries[rows, cols]) * HD**-0.5
            dkv[:, rows, cols] = keys_grad.astype(BF).reshape(8, 128, 64)
            dkv[:, rows, late] = t_mm(low, grad_here).astype(BF).reshape(8, 128, 64)
    sibling = (y, e + 1 - 2 * c, z)
    swaps = []
    for k in range(4):
        gives = (x - k >= 0) & ((c == 1) if k == 0 else True)
        takes = (x - k >= 0) & ((c == 0) if k == 0 else True)
        copy = wires.plan(dkv.at[(2 * (x - k) + 1 - c + 8) % 8], sib_land.at[k], sibling, gives)
        pl.when(gives)(copy.start)
        swaps.append((takes, copy))
    far = []
    for k in (2, 3, 1):
        gives, takes = x - k >= 0, x + k <= 3
        block = (e - 2 * k + 8) % 8
        send = wires.plan(dkv.at[block], owner_land.at[k - 1], (y, block, z), gives)

        @pl.when(gives)
        def _():
            swaps[k][1].wait_recv()
            dkv[block] = (dkv[block].astype(F32) + sib_land[k].astype(F32)).astype(BF)
            send.start()

        far.append((k, takes, send))
    grad_os[:, :192] = t_mm(attn_grad, attended[...]).astype(BF)
    grad_os[:, 192:] = t_mm(rows_in, gathered[:, :64, 768:].reshape(256, 128)).astype(BF)[:, 64:]
    lin[:, :384] = dkv[e].astype(F32)
    lin[:, 576:] = jnp.zeros((256, 64), F32)

    @pl.when(swaps[0][0])
    def _():
        swaps[0][1].wait_recv()
        lin[:, :384] += sib_land[0].astype(F32)

    for k, takes, copy in reversed(far):

        @pl.when(takes)
        def _():
            copy.wait_recv()
            lin[:, :384] += owner_land[k - 1].astype(F32)

    lin_grad = turned(lin[...], two(cos[...]), -two(sin[...])).astype(BF)
    part[...] = mm_t(lin_grad, w[:, QKV]).astype(BF).reshape(4, 64, 768)
    summed = sum_rows(wires, part, land, y, e, z)
    grad_qkv[...] = t_mm(normed[...], lin_grad).astype(BF)
    back_norm, gain_one = rms_back(own[...], gains[0:1], summed())
    result = down_own[...] + back_norm
    down_own[...] = result
    tail[z, :64] = result.astype(BF)
    tail[z, 64:] = jnp.where(top, gain_one, 0.0).astype(BF)
    spread_rows(wires, tail, y, e, z)()
    down_stream[...] = tail[:, :64]
    one = jnp.sum(tail[:, 64:].astype(F32).reshape(64, 768), axis=0, keepdims=True)
    both = jnp.sum(gathered[:, 64:, :768].astype(F32).reshape(64, 768), axis=0, keepdims=True)
    at_row = lax.broadcasted_iota(jnp.int32, (8, 768), 0)
    grad_gain[...] = jnp.where(at_row == 0, one, jnp.where(at_row == 1, both, 0.0))
    wires.finish()


ANY = pl.BlockSpec(memory_space=pl.ANY)
WEIGHTS = [
    pltpu.VMEM((768, WIDE), BF),
    pltpu.VMEM((2, 768, 512), BF),
    pltpu.VMEM((2, 768, 512), BF),
    pltpu.VMEM((2, 512, 768), BF),
]
ROWS4 = (4, 64, 768)
SAVED = [
    ((256, 768), BF),
    ((256, 192), BF),
    ((8, 256, 384), BF),
    ((6, 128, 1024), BF),
    ((256, 192), BF),
    ((64, 768), F32),
    (ROWS4, BF),
    ((256, 1024), F32),
    ((2, 256, 1024), F32),
    ((16, 32, 768), BF),
    ((256, 128), F32),
]


def forward(layer, stream, own, lengths, route, cos, sin, w, eg, eu, ed):
    out = SAVED + [((2, 256, 768), BF), ((64, 768), F32), (ROWS4, BF)]
    return pl.pallas_call(
        functools.partial(forward_kernel, layer),
        out_shape=[jax.ShapeDtypeStruct(*one) for one in out],
        in_specs=[VM] * 6 + [ANY] * 4,
        out_specs=[VM] * len(out),
        scratch_shapes=WEIGHTS
        + [
            pltpu.VMEM((2, 4, 64, 768), BF),
            pltpu.VMEM((2, 3, 64, 768), BF),
            pltpu.VMEM((16, 32, 768), BF),
            pltpu.VMEM((2, 256, 768), BF),
            pltpu.SemaphoreType.DMA((4,)),
            pltpu.SemaphoreType.DMA((48,)),
            pltpu.SemaphoreType.DMA((48,)),
        ],
        compiler_params=pltpu.CompilerParams(
            collective_id=3 + layer, has_side_effects=True, vmem_limit_bytes=52 * 2**20
        ),
        name=f"block_forward_{layer}",
    )(stream, own, lengths, route, cos, sin, w, eg, eu, ed)


def backward(layer, incoming, grad_own, own, saved, route, cos, sin, w, eg, eu, ed):
    normed, queries, kv, probs, attended, middle, ffn_in, gud, gue, ret, shares = saved
    out = [((768, width), BF) for width in WIDTHS] + [
        ((8, 768), F32),
        ((2, 256, 768), BF),
        ((64, 768), F32),
        (ROWS4, BF),
    ]
    return pl.pallas_call(
        functools.partial(backward_kernel, layer),
        out_shape=[jax.ShapeDtypeStruct(*one) for one in out],
        in_specs=[VM] * 17 + [ANY] * 4,
        out_specs=[VM] * len(out),
        scratch_shapes=WEIGHTS
        + [
            pltpu.VMEM((4, 64, 896), BF),
            pltpu.VMEM((3, 64, 896), BF),
            pltpu.VMEM(ROWS4, BF),
            pltpu.VMEM((3, 64, 768), BF),
            pltpu.VMEM((16, 32, 768), BF),
            pltpu.VMEM((2, 256, 768), BF),
            pltpu.VMEM((16, 32, 768), BF),
            pltpu.VMEM((4, 80, 896), BF),
            pltpu.VMEM((4, 80, 768), BF),
            pltpu.VMEM((8, 256, 384), BF),
            pltpu.VMEM((4, 256, 384), BF),
            pltpu.VMEM((3, 256, 384), BF),
            pltpu.VMEM((256, 640), F32),
            pltpu.SemaphoreType.DMA((4,)),
            pltpu.SemaphoreType.DMA((56,)),
            pltpu.SemaphoreType.DMA((56,)),
        ],
        compiler_params=pltpu.CompilerParams(
            collective_id=5 + layer, has_side_effects=True, vmem_limit_bytes=56 * 2**20
        ),
        name=f"block_backward_{layer}",
    )(incoming, grad_own, own, middle, normed, queries, kv, probs, attended, ffn_in, gud, gue, ret, shares, route, cos, sin, w, eg, eu, ed)


def swish_product(gate, up):
    return jax.nn.silu(gate) * up


def rotation(span):
    half = HD // 2
    frequency = jnp.exp(-jnp.log(10000.0) * jnp.arange(half).astype(F32) / half)
    positions = (lax.axis_index("ep") * span + jnp.arange(span)).astype(F32)
    angles = positions[:, None] * frequency[None, :]
    cosine, sine = jnp.cos(angles), jnp.sin(angles)
    cosine = jnp.tile(jnp.concatenate([cosine, cosine], axis=1), (1, 3))
    sine = jnp.tile(jnp.concatenate([-sine, sine], axis=1), (1, 3))
    ones, none = jnp.ones((span, 192), F32), jnp.zeros((span, 192), F32)
    return (
        jnp.concatenate([cosine, ones, cosine, ones[:, :64]], axis=1),
        jnp.concatenate([sine, none, sine, none[:, :64]], axis=1),
    )


def shards(
    inputs, lengths, expert_ids, slot_ids, attn_gain, query_weight, key_weight, value_weight, out_weight, ffn_gain, router_weight,
    dense_gate, dense_up, dense_down, expert_gate, expert_up, expert_down, cotangent,
):
    filler = jnp.zeros((2, 24, 64), BF)
    small = jnp.concatenate(
        [router_weight, attn_gain[:, :, None], ffn_gain[:, :, None], filler[:, :, : 64 - 18]], axis=2
    )
    packed = jnp.concatenate(
        [out_weight, small, key_weight, value_weight, query_weight, filler, dense_gate, dense_up, dense_down],
        axis=2,
    )
    w = gather_weights(packed.reshape(CHUNK, WIDE))
    z = lax.axis_index("tp")
    cos, sin = rotation(128)
    used = jnp.broadcast_to(lengths[:, None], (2, 128))
    ids = expert_ids.reshape(2, 256, 2)
    slots = slot_ids.reshape(2, 256, 2)
    pairs = jnp.where(slots < 32, ids * 32 + slots, 512)
    routes = jnp.concatenate([pairs, ids], axis=2)

    def mine(rows):
        return lax.dynamic_slice_in_dim(rows.reshape(256, 768), z * 64, 64, 0).astype(F32)

    experts = (expert_gate, expert_up, expert_down)
    stream = inputs.reshape(ROWS4)
    own = mine(inputs)
    saved, owns, rows_at = [], [], []
    for layer in range(2):
        *kept, rows, after, stream = forward(layer, stream, own, used, routes[layer], cos, sin, w, *experts)
        saved.append(kept)
        owns.append(own)
        rows_at.append(rows)
        own = after
    outputs = stream
    grad = cotangent.reshape(ROWS4)
    grad_own = mine(cotangent)
    parts, gains, backs = [None, None], [None, None], [None, None]
    for layer in (1, 0):
        *parts[layer], gains[layer], backs[layer], grad_own, grad = backward(
            layer, grad, grad_own, owns[layer], saved[layer], routes[layer], cos, sin, w, *experts
        )
    first, second, third, g_down = scatter_grads(parts[0] + parts[1] + gains)
    rows0, rows1, back0, back1 = gather_rows(rows_at + backs)
    columns = ([], [], [])
    for layer, (all_rows, all_back) in enumerate(((rows0, back0), (rows1, back1))):
        all_rows = all_rows.reshape(2, 1024, 768)
        all_back = all_back.reshape(2, 1024, 768)
        gate = jnp.einsum("ecd,edf->ecf", all_rows, expert_gate[layer], preferred_element_type=F32)
        up = jnp.einsum("ecd,edf->ecf", all_rows, expert_up[layer], preferred_element_type=F32)
        hidden = swish_product(gate, up).astype(BF)
        hidden_grad = jnp.einsum("ecd,efd->ecf", all_back, expert_down[layer], preferred_element_type=F32)
        gate_grad, up_grad = jax.vjp(swish_product, gate, up)[1](hidden_grad)
        gate_grad, up_grad = gate_grad.astype(BF), up_grad.astype(BF)
        columns[0].append(jnp.einsum("ecd,ecf->edf", all_rows, gate_grad, preferred_element_type=F32))
        columns[1].append(jnp.einsum("ecd,ecf->edf", all_rows, up_grad, preferred_element_type=F32))
        columns[2].append(jnp.einsum("ecf,ecd->efd", hidden, all_back, preferred_element_type=F32))
    return (
        outputs.reshape(2, 128, 768).astype(F32),
        grad.reshape(2, 128, 768).astype(F32),
        first[:, :, 208],
        second[:, :, 384:576],
        second[:, :, 0:192],
        second[:, :, 192:384],
        first[:, :, 0:192],
        first[:, :, 209],
        first[:, :, 192:208],
        third[:, :, :512],
        third[:, :, 512:],
        g_down,
        *[jnp.stack(column) for column in columns],
    )


def solution(mesh):
    return jax.shard_map(
        shards,
        mesh=mesh,
        in_specs=(
            P("dp", "ep", None),
            P("dp"),
            P(None, "dp", "ep", None),
            P(None, "dp", "ep", None),
            P(None, ("dp", "ep")),
            P(None, ("dp", "ep"), "tp"),
            P(None, ("dp", "ep"), "tp"),
            P(None, ("dp", "ep"), "tp"),
            P(None, ("dp", "ep"), "tp"),
            P(None, ("dp", "ep")),
            P(None, ("dp", "ep"), None),
            P(None, ("dp", "ep"), "tp"),
            P(None, ("dp", "ep"), "tp"),
            P(None, ("dp", "ep"), "tp"),
            P(None, "ep", None, "tp"),
            P(None, "ep", None, "tp"),
            P(None, "ep", "tp", None),
            P("dp", "ep", None),
        ),
        out_specs=(
            P("dp", "ep", None),
            P("dp", "ep", None),
            P(None, ("dp", "ep")),
            P(None, ("dp", "ep"), "tp"),
            P(None, ("dp", "ep"), "tp"),
            P(None, ("dp", "ep"), "tp"),
            P(None, ("dp", "ep"), "tp"),
            P(None, ("dp", "ep")),
            P(None, ("dp", "ep"), None),
            P(None, ("dp", "ep"), "tp"),
            P(None, ("dp", "ep"), "tp"),
            P(None, ("dp", "ep"), "tp"),
            P(None, "ep", None, "tp"),
            P(None, "ep", None, "tp"),
            P(None, "ep", "tp", None),
        ),
        check_vma=False,
    )
```

time: 1250 us -> 566 us (0.45)
  local copies, waits for them, and re-layouts: 389 us -> 19.3 us
  Pallas kernels: 165 us -> 466 us
  waiting for transfers between devices: 287 us -> 0 us
  matrix products: 173 us -> 55.5 us
  blocking collectives: 73.5 us -> 0 us
  other arithmetic: 85.1 us -> 16.5 us
  starting transfers between devices: 50.6 us -> 0 us
  between operations: 16.5 us -> 1.31 us
    pallas_call x0 -> x4, Pallas kernels: none -> 308 us  [the longest x2 165 us: backward(): pl.pallas_call(functools.partial(backward_kernel, layer), out_shape=[jax....]
    unnamed x318 -> x66, local copies, waits for them, and re-layouts: 285 us -> 9.15 us
    psum x7 -> x0, waiting for transfers between devices: 242 us -> none  [the longest x2 71 us: shards(): lax.psum(attn_part.astype(jnp.bfloat16), 'tp').astype(jnp.float32)]
    dot_general x86 -> x12, matrix products: 173 us -> 55.5 us  [the longest x2 13 us: shards(): jnp.einsum('ecd,ecf->edf', all_rows, gate_grad, preferred_element_type=F32)]
    all_gather x4 -> x0, blocking collectives: 57.9 us -> none  [the longest x2 30.2 us: shards(): lax.all_gather(values_low, 'ep', axis=1, tiled=True)]
    all_to_all x8 -> x0, starting transfers between devices: 48.4 us -> none  [the longest x2 14.3 us: shards(): lax.all_to_all(sent, 'ep', split_axis=0, concat_axis=1, tiled=True)]
    reduce_sum x23 -> x0, other arithmetic: 29.6 us -> none  [the longest x2 6.04 us: shards(): share_part = jnp.sum(ffn_grad_wide[:, None, :] * picked_rows, axis=-1)]
    all_to_all x8 -> x0, waiting for transfers between devices: 26.2 us -> none  [the longest x2 10.4 us: shards(): lax.all_to_all(out_exp.astype(jnp.bfloat16), 'ep', split_axis=1, concat_a...]
  transfers between devices with their start and end apart: 19 -> 0, of which waited for: 13 -> 0; matrix products, arithmetic and copies ran while one was open for 27% -> 0% of each run, Pallas kernels for 0% -> 0%
where the time goes in v2:
time: 566 us; the launch traced here: 558 us
  Pallas kernels  466 us (82%)
  matrix products  55.5 us (10%)
  local copies, waits for them, and re-layouts  19.3 us (3%)
  other arithmetic  16.5 us (3%)
    pallas_call x2, Pallas kernels, backward(): pl.pallas_call(functools.partial(backward_kernel, layer), out_shape=[jax....  165 us
    pallas_call x2, Pallas kernels, forward(): pl.pallas_call(functools.partial(forward_kernel, layer), out_shape=[jax.S...  143 us
    pallas_call x1, Pallas kernels, gather_rows(): pl.pallas_call(rows_kernel, out_shape=[shape] * 4, in_specs=[VM] * 4, out...  87.7 us
    pallas_call x1, Pallas kernels, scatter_grads(): pl.pallas_call(scatter_kernel, out_shape=[jax.ShapeDtypeStruct((2, 24, wi...  36 us
    pallas_call x1, Pallas kernels, gather_weights(): pl.pallas_call(gather_kernel, out_shape=jax.ShapeDtypeStruct((2, 768, WID...  34.5 us
    dot_general x2, matrix products, shards(): jnp.einsum('ecd,ecf->edf', all_rows, gate_grad, preferred_element_type=F32)  13 us

profile of v2, /device:TPU:1, one launch (start us, length us, event | category | flops | bytes accessed | tf_op | source)
XLA Modules:
  0.0 558.3 jit_solution(14245804473108392253)
XLA Ops:
  0.7 0.7 broadcast_in_dim.11.lengths
  1.4 0.1 pad.7.clone
  1.5 0.1 pad.13.clone
  1.6 0.1 pad.9.clone
  1.6 0.1 pad.15.clone
  1.7 0.7 compare_select_fusion
  2.4 0.7 pad_add_fusion
  3.1 0.8 concatenate.55
  3.9 0.8 concatenate.56
  4.7 0.8 copy.68
  5.4 0.1 fusion.48
  5.6 0.1 copy.64
  5.7 0.1 copy.66
  5.8 0.1 copy.86
  6.0 0.0 copy-start.4
  6.0 0.1 copy.85
  6.2 1.1 concatenate.54.src
  7.3 0.0 copy-start
  7.3 0.0 copy-start.1
  7.3 1.8 dynamic-slice_convert_fusion
  9.2 34.5 %gather_weights.1.w_all = bf16[2,768,2432]{2,1,0:T(8,128)(2,1)} custom-call(bf16[48,2432]{1,0:T(8,128)(2,1)S(1)} %concatenate.54.src), custom_call_target="tpu_custom_call" | custom-call | tf_op jit(solution)/shard_map/gather_weights/pallas_call | solution.py:137
  43.6 68.6 %block_forward_0.1 = (bf16[256,768]{1,0:T(8,128)(2,1)}, bf16[256,192]{1,0:T(8,128)(2,1)S(1)}, bf16[8,256,384]{2,1,0:T(8,128)(2,1)}, bf16[6,128,1024]{2,1,0:T(8,1...) custom-call(bf16[4,64,768]{2,1,0:T(8,128)(2,1)} %bitcast.83, ...), custom_call_target="tpu_custom_call" | custom-call | tf_op jit(solution)/shard_map/block_forward_0/pallas_call | solution.py:799
  112.3 0.7 copy-done.10
  113.0 0.7 copy-done.12
  113.7 74.1 %block_forward_1.1 = (bf16[256,768]{1,0:T(8,128)(2,1)}, bf16[256,192]{1,0:T(8,128)(2,1)S(1)}, bf16[8,256,384]{2,1,0:T(8,128)(2,1)}, bf16[6,128,1024]{2,1,0:T(8,1...) custom-call(bf16[4,64,768]{2,1,0:T(8,128)(2,1)} %get-tuple-element.6, ...), custom_call_target="tpu_custom_call" | custom-call | tf_op jit(solution)/shard_map/block_forward_1/pallas_call | solution.py:799
  187.8 0.7 copy-done.11
  188.4 0.6 copy-done.15
  189.1 0.6 copy-done.17
  189.7 2.0 bitcast_convert_fusion.1
  191.7 88.1 %block_backward_1.1 = (bf16[768,256]{1,0:T(8,128)(2,1)}, bf16[768,640]{1,0:T(8,128)(2,1)}, bf16[768,1024]{1,0:T(8,128)(2,1)}, bf16[768,512]{1,0:T(8,128)(2,1)}, ...) custom-call(bf16[4,64,768]{2,1,0:T(8,128)(2,1)} %bitcast.85, ...), custom_call_target="tpu_custom_call" | custom-call | tf_op jit(solution)/shard_map/block_backward_1/pallas_call | solution.py:829
  279.8 76.8 %block_backward_0.1 = (bf16[768,256]{1,0:T(8,128)(2,1)}, bf16[768,640]{1,0:T(8,128)(2,1)}, bf16[768,1024]{1,0:T(8,128)(2,1)}, bf16[768,512]{1,0:T(8,128)(2,1)}, ...) custom-call(bf16[4,64,768]{2,1,0:T(8,128)(2,1)} %get-tuple-element.79.incoming, ...), custom_call_target="tpu_custom_call" | custom-call | tf_op jit(solution)/shard_map/block_backward_0/pallas_call | solution.py:829
  356.6 36.0 %scatter_grads.1 = (f32[2,24,256]{2,1,0:T(8,128)}, f32[2,24,640]{2,1,0:T(8,128)}, f32[2,24,1024]{2,1,0:T(8,128)}, f32[2,24,512]{2,1,0:T(8,128)}) custom-call(bf16[768,256]{1,0:T(8,128)(2,1)} %get-tuple-element.93.refs_0_, bf16[768,640]{1,0:T(8,128)(2,1)} %get-tuple-element.94.refs_1_, bf16[768,1024]{1,0:T(8,128)(2,1)} %get-tuple-element.95.refs_2_, ...), custom_call_target="tpu_custom_call" | custom-call | tf_op jit(solution)/shard_map/scatter_grads/pallas_call | solution.py:332
  392.7 1.5 slice_reduce_fusion
  394.2 1.4 slice.73
  395.6 1.4 copy.78
  397.0 1.8 fusion.57
  398.8 1.6 fusion.56
  400.4 0.9 bitcast_convert_fusion
  401.4 0.0 copy-done.7
  401.4 87.7 %gather_rows.1 = (bf16[2,4,256,768]{3,2,1,0:T(8,128)(2,1)}, bf16[2,4,256,768]{3,2,1,0:T(8,128)(2,1)}, bf16[2,4,256,768]{3,2,1,0:T(8,128)(2,1)}, bf16[2,4,256,768]{3,2,1,0:T(8,128)(2,1)}) custom-call(bf16[2,256,768]{2,1,0:T(8,128)(2,1)S(1)} %copy-done.6, bf16[2,256,768]{2,1,0:T(8,128)(2,1)S(1)} %copy-done.7, bf16[2,256,768]{2,1,0:T(8,128)(2,1)S(1)} %copy-done.9, ...), custom_call_target="tpu_custom_call" | custom-call | tf_op jit(solution)/shard_map/gather_rows/pallas_call | solution.py:418
  489.0 3.8 fusion.32
  492.9 0.0 copy-start.29
  492.9 0.0 copy-start.20
  492.9 3.8 fusion.26
  496.7 0.3 copy-done.20
  497.1 1.6 copy-done.26
  498.6 3.8 fusion.36
  502.5 4.3 fusion.25
  506.8 0.0 copy-done.29
  506.9 3.8 fusion.34
  510.6 7.1 %fusion.16 = f32[1,2,768,512]{3,2,1,0:T(8,128)S(1)} fusion(bf16[2,1024,768]{2,1,0:T(8,128)(2,1)S(1)} %bitcast.111, f32[2,1024,512]{2,1,0:T(8,128)} %copy-done.29, f32[2,1024,512]{2,1,0:T(8,128)} %fusion.36, f32[2,1024,512]{2,1,0:T(8,128)} %fusion.34), kind=kOutput, calls=%fused_computation.25 | convolution fusion | flops 1622147072 | bytes 18874368 | tf_op jit(solution)/shard_map/ecd,ecf->edf/dot_general | solution.py:933
  517.7 6.3 %fusion.23 = f32[1,2,512,768]{3,2,1,0:T(8,128)S(1)} fusion(bf16[2,1024,768]{2,1,0:T(8,128)(2,1)S(1)} %bitcast.107, f32[2,1024,512]{2,1,0:T(8,128)} %fusion.34, f32[2,1024,512]{2,1,0:T(8,128)} %copy-done.29), kind=kOutput, calls=%fused_computation.28 | convolution fusion | flops 1616904192 | bytes 14680064 | tf_op jit(solution)/shard_map/ecf,ecd->efd/dot_general | solution.py:935
  524.1 0.0 copy-start.28
  524.1 3.8 fusion.28
  527.9 0.1 copy-done.28
  528.0 4.8 fusion.22
  532.9 3.2 pad_maximum_fusion.2
  536.1 3.8 fusion.30
  539.9 5.9 %fusion.19 = f32[1,2,768,512]{3,2,1,0:T(8,128)S(1)} fusion(bf16[2,1024,768]{2,1,0:T(8,128)(2,1)S(1)} %bitcast.102, f32[2,1024,512]{2,1,0:T(8,128)S(1)} %copy-done.28, f32[2,1024,512]{2,1,0:T(8,128)} %fusion.30, f32[2,1024,512]{2,1,0:T(8,128)} %fusion.28), kind=kOutput, calls=%fused_computation.26 | convolution fusion | flops 1622147072 | bytes 18874368 | tf_op jit(solution)/shard_map/ecd,ecf->edf/dot_general | solution.py:933
  545.8 4.1 fusion.24
  550.0 3.5 pad_maximum_fusion.1
  553.4 3.4 pad_maximum_fusion
  556.9 0.6 copy.89
  557.5 0.6 copy.90
  (57 shorter events, 0.2 us)
Async XLA Ops:
  6.0 107.7 %copy-start.4 = (s32[1,256,4]{2,1,0:T(8,128)}, s32[1,256,4]{2,1,0:T(8,128)S(1)}, u32[]{:S(2)}) copy-start(s32[1,256,4]{2,1,0:T(8,128)S(1)} %copy.86) | copy-start | bytes 12292
  6.1 37.5 %copy-start.3 = (s32[1,256,4]{2,1,0:T(8,128)}, s32[1,256,4]{2,1,0:T(8,128)S(1)}, u32[]{:S(2)}) copy-start(s32[1,256,4]{2,1,0:T(8,128)S(1)} %copy.85) | copy-start | bytes 12292
  7.3 106.4 %copy-start = (f32[128,640]{1,0:T(8,128)}, f32[128,640]{1,0:T(8,128)S(1)}, u32[]{:S(2)}) copy-start(f32[128,640]{1,0:T(8,128)S(1)} %maximum_maximum_fusion.1.sin) | copy-start | bytes 983044
  7.3 106.3 %copy-start.1 = (f32[128,640]{1,0:T(8,128)}, f32[128,640]{1,0:T(8,128)S(1)}, u32[]{:S(2)}) copy-start(f32[128,640]{1,0:T(8,128)S(1)} %maximum_maximum_fusion.cos) | copy-start | bytes 983044
  9.2 103.1 %copy-start.2 = (f32[64,768]{1,0:T(8,128)}, f32[64,768]{1,0:T(8,128)S(1)}, u32[]{:S(2)}) copy-start(f32[64,768]{1,0:T(8,128)S(1)} %get-tuple-element.173.own) | copy-start | bytes 589828
  112.3 0.7 copy-start.10
  113.0 0.7 copy-start.12
  113.6 74.1 %copy-start.5 = (f32[64,768]{1,0:T(8,128)}, f32[64,768]{1,0:T(8,128)S(1)}, u32[]{:S(2)}) copy-start(f32[64,768]{1,0:T(8,128)S(1)} %get-tuple-element.66.own) | copy-start | bytes 589828
  113.6 74.1 %copy-start.13 = (bf16[256,192]{1,0:T(8,128)(2,1)}, bf16[256,192]{1,0:T(8,128)(2,1)S(1)}, u32[]{:S(2)}) copy-start(bf16[256,192]{1,0:T(8,128)(2,1)S(1)} %get-tuple-element.86.attended) | copy-start | bytes 294916
  113.6 74.1 %copy-start.14 = (f32[256,128]{1,0:T(8,128)}, f32[256,128]{1,0:T(8,128)S(1)}, u32[]{:S(2)}) copy-start(f32[256,128]{1,0:T(8,128)S(1)} %get-tuple-element.91.shares) | copy-start | bytes 393220
  187.8 0.7 copy-start.11
  188.4 0.6 copy-start.15
  189.1 0.7 copy-start.17
  189.7 2.0 copy-start.16
  356.6 43.8 %copy-start.21 = (bf16[4,64,768]{2,1,0:T(8,128)(2,1)S(1)}, bf16[4,64,768]{2,1,0:T(8,128)(2,1)}, u32[]{:S(2)}) copy-start(bf16[4,64,768]{2,1,0:T(8,128)(2,1)} %get-tuple-element.92) | copy-start | bytes 1179652
  356.6 44.8 %copy-start.6 = (bf16[2,256,768]{2,1,0:T(8,128)(2,1)S(1)}, bf16[2,256,768]{2,1,0:T(8,128)(2,1)}, u32[]{:S(2)}) copy-start(bf16[2,256,768]{2,1,0:T(8,128)(2,1)} %get-tuple-element.107.a0) | copy-start | bytes 2359300
  356.6 44.8 %copy-start.7 = (bf16[2,256,768]{2,1,0:T(8,128)(2,1)S(1)}, bf16[2,256,768]{2,1,0:T(8,128)(2,1)}, u32[]{:S(2)}) copy-start(bf16[2,256,768]{2,1,0:T(8,128)(2,1)} %get-tuple-element.108.a1) | copy-start | bytes 2359300
  356.6 44.8 %copy-start.8 = (bf16[2,256,768]{2,1,0:T(8,128)(2,1)S(1)}, bf16[2,256,768]{2,1,0:T(8,128)(2,1)}, u32[]{:S(2)}) copy-start(bf16[2,256,768]{2,1,0:T(8,128)(2,1)} %get-tuple-element.110.b1) | copy-start | bytes 2359300
  356.6 44.8 %copy-start.9 = (bf16[2,256,768]{2,1,0:T(8,128)(2,1)S(1)}, bf16[2,256,768]{2,1,0:T(8,128)(2,1)}, u32[]{:S(2)}) copy-start(bf16[2,256,768]{2,1,0:T(8,128)(2,1)} %get-tuple-element.109.b0) | copy-start | bytes 2359300
  397.0 92.0 %copy-start.18 = (bf16[2,2,768,512]{3,2,1,0:T(8,128)(2,1)S(1)}, bf16[2,2,768,512]{3,2,1,0:T(8,128)(2,1)}, u32[]{:S(2)}) copy-start(bf16[2,2,768,512]{3,2,1,0:T(8,128)(2,1)} %eg_all.7) | copy-start | bytes 9437188
  489.0 3.8 copy-start.24
  492.9 14.0 %copy-start.29 = (f32[2,1024,512]{2,1,0:T(8,128)}, f32[2,1024,512]{2,1,0:T(8,128)S(1)}, u32[]{:S(2)}) copy-start(f32[2,1024,512]{2,1,0:T(8,128)S(1)} %fusion.32) | copy-start | bytes 12582916
  492.9 4.2 copy-start.20
  492.9 5.7 %copy-start.26 = (bf16[2,4,256,768]{3,2,1,0:T(8,128)(2,1)S(1)}, bf16[2,4,256,768]{3,2,1,0:T(8,128)(2,1)}, u32[]{:S(2)}) copy-start(bf16[2,4,256,768]{3,2,1,0:T(8,128)(2,1)} %get-tuple-element.112) | copy-start | bytes 9437188
  498.6 3.8 copy-start.27
  502.5 4.4 copy-start.19
  524.1 3.8 copy-start.25
  524.1 3.9 copy-start.28
  553.4 3.4 copy-start.22
  553.4 4.0 copy-start.23

commit v3 on v2

--- a/solution.py
+++ b/solution.py
@@ -152,7 +152,6 @@
 
 
 EPS = 1e-06
-WIDTHS = (256, 640, 1024, 512)
 SMALL = slice(128, 256)
 ROUTER = 64
 GAIN = 80
@@ -217,224 +216,14 @@
     return jnp.concatenate([values, values], axis=0)
 
 
-def scatter_kernel(*refs):
-    ins, gains, outs = refs[:8], refs[8:10], refs[10:14]
-    chunks, sib_land, plus_far, minus_far, plus_near, minus_near, one_far, one_near, columns, send_sems, recv_sems = refs[14:]
-    y, x, c, z = place()
-
-    def at(j, d):
-        yy = (y + j * c + d * (1 - c) + 8) % 4
-        xx = (x + j * (1 - c) + d * c + 8) % 4
-        return yy, xx
-
-    def who(j, d):
-        yy, xx = at(j, d)
-        return device(yy, xx, c, z)
-
-    def slot(j, d, core):
-        yy, xx = at(j, d)
-        return yy * 8 + xx * 2 + core
-
-    sibling = device(y, x, 1 - c, z)
-    meet([who(1, 0), who(-1, 0), who(0, 1), who(0, -1), sibling], 5)
-
-    spot = lanes((8, 256)) == lax.broadcasted_iota(jnp.int32, (8, 256), 0) + 128 + GAIN
-
-    def pack(p, carry):
-        rows = pl.ds(pl.multiple_of(p * CHUNK, CHUNK), CHUNK)
-        left = 0
-        for part, width in enumerate(WIDTHS):
-            one = ins[part][rows].astype(F32)
-            two = ins[4 + part][rows].astype(F32)
-            if part == 0:
-                one += columns[0, rows]
-                two += columns[1, rows]
-            cols = slice(left, left + width)
-            chunks[2 * p, :, cols] = jnp.concatenate([one[:24], two[:24]], axis=0).astype(BF)
-            chunks[2 * p + 1, :, cols] = jnp.concatenate([one[24:], two[24:]], axis=0).astype(BF)
-            left += width
-        return carry
-
-    for layer in range(2):
-        columns[layer] = t_mm(gains[layer][...].astype(BF), spot.astype(BF))
-    lax.fori_loop(0, 16, pack, 0)
-    line = Line(send_sems, recv_sems)
-    order = [(j, d) for d in (2, 1, -1, 0) for j in (0, -1, 1, 2)]
-    swapped = {}
-    for n, (j, d) in enumerate(order):
-        yy = (y + j * (1 - c) + d * c + 8) % 4
-        xx = (x + j * c + d * (1 - c) + 8) % 4
-        swapped[j, d] = line.start(chunks.at[yy * 8 + xx * 2 + 1 - c], sib_land.at[n], sibling)
-
-    def join(j, d):
-        n = order.index((j, d))
-        swapped[j, d].wait_recv()
-        mine = slot(j, d, c)
-        chunks[mine] = (chunks[mine].astype(F32) + sib_land[n].astype(F32)).astype(BF)
-        return chunks.at[mine]
-
-    plus_set, minus_set = (0, -1), (1, 2)
-    far = {}
-    for j in (0, -1, 1, 2):
-        ref = join(j, 2)
-        if j in plus_set:
-            far[j] = line.start(ref, plus_far.at[plus_set.index(j)], who(0, 1))
-        else:
-            far[j] = line.start(ref, minus_far.at[minus_set.index(j)], who(0, -1))
-    near = {}
-    for j in (1, 2):
-        near[j, 1] = line.start(join(j, 1), plus_near.at[j], who(0, 1))
-    for j in (0, -1):
-        near[j, -1] = line.start(join(j, -1), minus_near.at[j % 4], who(0, -1))
-    for j in plus_set:
-        ref = join(j, 1)
-        far[j].wait_recv()
-        ref[...] = (ref[...].astype(F32) + plus_far[plus_set.index(j)].astype(F32)).astype(BF)
-        near[j, 1] = line.start(ref, plus_near.at[j % 4], who(0, 1))
-    for j in minus_set:
-        ref = join(j, -1)
-        far[j].wait_recv()
-        ref[...] = (ref[...].astype(F32) + minus_far[minus_set.index(j)].astype(F32)).astype(BF)
-        near[j, -1] = line.start(ref, minus_near.at[j], who(0, -1))
-    held = {}
-    for j in (2, 1, -1, 0):
-        ref = join(j, 0)
-        near[j, 1].wait_recv()
-        near[j, -1].wait_recv()
-        total = ref[...].astype(F32) + plus_near[j % 4].astype(F32) + minus_near[j % 4].astype(F32)
-        ref[...] = total.astype(BF)
-        held[j] = ref
-        if j == 2:
-            a = line.start(ref.at[pl.ds(0, 32)], one_far.at[pl.ds(0, 32)], who(1, 0))
-            b = line.start(ref.at[pl.ds(32, 16)], one_far.at[pl.ds(32, 16)], who(-1, 0))
-    a.wait_recv()
-    up = held[1].at[pl.ds(0, 32)]
-    up[...] = (up[...].astype(F32) + one_far[:32].astype(F32)).astype(BF)
-    last_plus = line.start(held[1], one_near.at[0], who(1, 0))
-    b.wait_recv()
-    down = held[-1].at[pl.ds(32, 16)]
-    down[...] = (down[...].astype(F32) + one_far[32:].astype(F32)).astype(BF)
-    last_minus = line.start(held[-1], one_near.at[1], who(-1, 0))
-    last_plus.wait_recv()
-    last_minus.wait_recv()
-    left = 0
-    for part, width in enumerate(WIDTHS):
-        cols = slice(left, left + width)
-        total = held[0][:, cols].astype(F32) + one_near[0, :, cols].astype(F32) + one_near[1, :, cols].astype(F32)
-        outs[part][0] = total[:24]
-        outs[part][1] = total[24:]
-        left += width
-    line.finish()
-
-
-def scatter_grads(parts):
-    chunk = lambda n: pltpu.VMEM((n, CHUNK, WIDE), BF)
-    return pl.pallas_call(
-        scatter_kernel,
-        out_shape=[jax.ShapeDtypeStruct((2, 24, width), F32) for width in WIDTHS],
-        in_specs=[VM] * 10,
-        out_specs=[VM] * 4,
-        scratch_shapes=[
-            chunk(32),
-            chunk(16),
-            chunk(2),
-            chunk(2),
-            chunk(4),
-            chunk(4),
-            pltpu.VMEM((CHUNK, WIDE), BF),
-            chunk(2),
-            pltpu.VMEM((2, 768, 256), F32),
-            pltpu.SemaphoreType.DMA((32,)),
-            pltpu.SemaphoreType.DMA((32,)),
-        ],
-        compiler_params=pltpu.CompilerParams(
-            collective_id=1, has_side_effects=True, vmem_limit_bytes=56 * 2**20
-        ),
-        name="scatter_grads",
-    )(*parts)
-
-
-def rows_kernel(a0, a1, b0, b1, o0, o1, o2, o3, send_sems, recv_sems):
-    y, x, c, z = place()
-
-    def along(dy, dz):
-        return device((y + dy + 4) % 4, x, c, (z + dz + 4) % 4)
-
-    meet([along(1, 0), along(-1, 0), along(0, 1), along(0, -1)], 4)
-    line = Line(send_sems, recv_sems)
-
-    def quarter(k, first, count):
-        return pl.ds(pl.multiple_of(((z + k + 4) % 4) * 64 + first, 32), count)
-
-    work = list(zip((a0, a1, b0, b1), (o0, o1, o2, o3)))
-    near, half, full, spread = [], [], [], []
-    for src, out in work:
-        mine = src.at[0, quarter(0, 0, 64)]
-        near.append(
-            (
-                line.start(mine, out.at[0, 1, quarter(0, 0, 64)], along(1, 0)),
-                line.start(mine, out.at[0, 3, quarter(0, 0, 64)], along(-1, 0)),
-            )
-        )
-        full.append(
-            (
-                line.start(src.at[1], out.at[1, 1], along(1, 0)),
-                line.start(src.at[1], out.at[1, 3], along(-1, 0)),
-            )
-        )
-    for (src, out), (plus, minus) in zip(work, near):
-        plus.wait_recv()
-        p = line.start(out.at[0, 1, quarter(0, 0, 32)], out.at[0, 2, quarter(0, 0, 32)], along(1, 0))
-        minus.wait_recv()
-        m = line.start(out.at[0, 3, quarter(0, 32, 32)], out.at[0, 2, quarter(0, 32, 32)], along(-1, 0))
-        half.append((p, m))
-    for (src, out), (plus, minus) in zip(work, half):
-        plus.wait_recv()
-        minus.wait_recv()
-        got = out.at[0, pl.ds(1, 3), quarter(0, 0, 64)]
-        spread.append((line.start(got, got, along(0, 1)), line.start(got, got, along(0, -1))))
-    last = []
-    for (src, out), (plus, minus) in zip(work, full):
-        plus.wait_recv()
-        p = line.start(out.at[1, 1, pl.ds(0, 128)], out.at[1, 2, pl.ds(0, 128)], along(1, 0))
-        minus.wait_recv()
-        m = line.start(out.at[1, 3, pl.ds(128, 128)], out.at[1, 2, pl.ds(128, 128)], along(-1, 0))
-        last += [p, m]
-    for (src, out), (plus, minus) in zip(work, spread):
-        plus.wait_recv()
-        got = out.at[0, pl.ds(1, 3), quarter(-1, 0, 32)]
-        last.append(line.start(got, got, along(0, 1)))
-        minus.wait_recv()
-        got = out.at[0, pl.ds(1, 3), quarter(1, 32, 32)]
-        last.append(line.start(got, got, along(0, -1)))
-        out[:, 0] = src[...]
-    for copy in last:
-        copy.wait_recv()
-    line.finish()
-
-
-def gather_rows(arrays):
-    shape = jax.ShapeDtypeStruct((2, 4, 256, 768), BF)
-    return pl.pallas_call(
-        rows_kernel,
-        out_shape=[shape] * 4,
-        in_specs=[VM] * 4,
-        out_specs=[VM] * 4,
-        scratch_shapes=[pltpu.SemaphoreType.DMA((48,)), pltpu.SemaphoreType.DMA((48,))],
-        compiler_params=pltpu.CompilerParams(
-            collective_id=2, has_side_effects=True, vmem_limit_bytes=48 * 2**20
-        ),
-        name="gather_rows",
-    )(*arrays)
-
-
 class Wires:
     def __init__(self, sends, recvs):
         self.sends, self.recvs, self.used, self.open = sends, recvs, 0, []
 
-    def plan(self, src, dst, who, when=None):
-        at = self.used
-        self.used += 1
+    def plan(self, src, dst, who, when=None, at=None):
+        if at is None:
+            at = self.used
+            self.used += 1
         copy = pltpu.make_async_remote_copy(
             src_ref=src,
             dst_ref=dst,
@@ -452,6 +241,7 @@
         return copy
 
     def finish(self):
+        assert self.used <= self.sends.shape[0]
         for copy, when in self.open:
             if when is None:
                 copy.wait_send()
@@ -461,7 +251,7 @@
 
 def peers(y, e, z):
     row = [(y, (e + k) % 8, z) for k in range(1, 8)]
-    return row, [(y, e, (z + k) % 4) for k in range(1, 4)]
+    return row + [(y, e, (z + k) % 4) for k in range(1, 4)] + [((y + 1) % 4, e, z), ((y + 3) % 4, e, z)]
 
 
 def spread_rows(wires, held, y, e, z):
@@ -490,8 +280,8 @@
     sent = []
     for k in (4, 3, 5, 2, 6, 1, 7):
         who = (e + k) % 8
-        sent.append(wires.go(src.at[2 * who + i], dst.at[i, rows], (y, who, z)))
-    dst[i, rows] = src[2 * e + i]
+        sent.append(wires.go(src.at[2 * who + i], dst.at[i, 0, rows], (y, who, z)))
+    dst[i, 0, rows] = src[2 * e + i]
     return lambda: [copy.wait_recv() for copy in sent]
 
 
@@ -505,6 +295,33 @@
     return lambda: [copy.wait_recv() for copy in sent]
 
 
+class RowWalk:
+    def __init__(self, wires, rows, y, e, z):
+        self.wires, self.rows = wires, rows
+        self.up, self.down = ((y + 1) % 4, e, z), ((y + 3) % 4, e, z)
+        self.near, self.far = [], []
+
+    def start(self, i):
+        rows = self.rows
+        self.near.append(
+            (
+                self.wires.go(rows.at[i, 0], rows.at[i, 1], self.up),
+                self.wires.go(rows.at[i, 0], rows.at[i, 3], self.down),
+            )
+        )
+
+    def pass_on(self, i):
+        self.near[i][i].wait_recv()
+        slot, who = ((1, self.up), (3, self.down))[i]
+        self.far.append(self.wires.go(self.rows.at[i, slot], self.rows.at[i, 2], who))
+
+    def finish(self):
+        self.near[0][1].wait_recv()
+        self.near[1][0].wait_recv()
+        for copy in self.far:
+            copy.wait_recv()
+
+
 def picks(route):
     slots = lanes((256, 512))
     return slots == route[:, 0:1], slots == route[:, 1:2]
@@ -517,14 +334,13 @@
 ):
     y, x, c, z = place()
     e = 2 * x + c
-    row, column = peers(y, e, z)
     fetch = [
         pltpu.make_async_copy(src.at[layer], dst, local.at[n])
         for n, (src, dst) in enumerate(((w_all, w), (eg_all, eg), (eu_all, eu), (ed_all, ed)))
     ]
     for copy in fetch:
         copy.start()
-    meet(row + column, 10)
+    meet(peers(y, e, z), 12)
     wires = Wires(sends, recvs)
     fetch[0].wait()
     gains = gain_rows(w)
@@ -600,47 +416,56 @@
     dense = mm_t(hidden, w[:, DOWN])
     for copy in fetch[1:]:
         copy.wait()
+    walk = RowWalk(wires, arrived, y, e, z)
     back = []
     for i in range(2):
         coming[i]()
-        gue[i, :, :512] = mm(arrived[i], eg[i])
-        gue[i, :, 512:] = mm(arrived[i], eu[i])
+        walk.start(i)
+        gue[i, :, :512] = mm(arrived[i, 0], eg[i])
+        gue[i, :, 512:] = mm(arrived[i, 0], eu[i])
         gate, up = gue[i, :, :512], gue[i, :, 512:]
         hidden = (gate * sigmoid(gate) * up).astype(BF)
         made[i] = mm(hidden, ed[i]).astype(BF)
         back.append(return_experts(wires, made, ret, y, e, z, i))
     for wait in back:
         wait()
+    walk.pass_on(0)
     mix = (jnp.where(pick0, share[0], 0.0) + jnp.where(pick1, share[1], 0.0)).astype(BF)
     moe = mm(mix, ret[...].reshape(512, 768))
     part[1] = (dense + moe).astype(BF).reshape(4, 64, 768)
     total = sum_rows(wires, part.at[1], land.at[1], y, e, z)()
+    walk.pass_on(1)
     result = middle[...] + total
     own_out[...] = result
     stream_out[z] = result.astype(BF)
-    spread_rows(wires, stream_out, y, e, z)()
+    wait = spread_rows(wires, stream_out, y, e, z)
+    wait()
+    walk.finish()
     wires.finish()
 
 
 def backward_kernel(
     layer, incoming, grad_own, own, middle, normed, queries, kv, probs, attended, ffn_in, gud, gue, ret, shares, route, cos, sin,
     w_all, eg_all, eu_all, ed_all,
-    grad_os, grad_qkv, grad_gu, grad_d, grad_gain, arrived, down_own, down_stream,
+    grads, arrived, down_own, down_stream,
     w, eg, eu, ed, part_ffn, land_ffn, part, land, sent, made, sret, gathered, tail, dkv, sib_land, owner_land, lin,
     local, sends, recvs,
 ):
     y, x, c, z = place()
     e = 2 * x + c
-    row, column = peers(y, e, z)
     fetch = [
         pltpu.make_async_copy(src.at[layer], dst, local.at[n])
         for n, (src, dst) in enumerate(((w_all, w), (eg_all, eg), (eu_all, eu), (ed_all, ed)))
     ]
     for copy in fetch:
         copy.start()
-    meet(row + column, 10)
+    meet(peers(y, e, z), 12)
     wires = Wires(sends, recvs)
     mine = pl.ds(pl.multiple_of(z * 64, 64), 64)
+
+    def keep(columns, values):
+        grads[:, :, columns] = values.astype(BF).reshape(16, CHUNK, values.shape[1])
+
     ffn_grad = incoming[...].reshape(256, 768)
     rows_in = ffn_in[...].reshape(256, 768)
     pick0, pick1 = picks(route[...])
@@ -663,15 +488,17 @@
     part_ffn[:, :, 768:] = extra.astype(BF).reshape(4, 64, 128)
     for copy in fetch[1:]:
         copy.wait()
+    walk = RowWalk(wires, arrived, y, e, z)
     back = []
     for i in range(2):
         coming[i]()
-        hidden_grad = mm_t(arrived[i], ed[i])
+        walk.start(i)
+        hidden_grad = mm_t(arrived[i, 0], ed[i])
         gate_e, up_e = swish_back(gue[i, :, :512], gue[i, :, 512:], hidden_grad)
         made[i] = (mm_t(gate_e, eg[i]) + mm_t(up_e, eu[i])).astype(BF)
         back.append(return_experts(wires, made, sret, y, e, z, i))
-    grad_gu[...] = t_mm(rows_in, gu_grad).astype(BF)
-    grad_d[...] = t_mm(ffn_grad, hidden_dense).astype(BF)
+    keep(GATEUP, t_mm(rows_in, gu_grad))
+    keep(DOWN, t_mm(ffn_grad, hidden_dense))
     for wait in back:
         wait()
     dense += mm((pick0 | pick1).astype(BF), sret[...].reshape(512, 768))
@@ -696,6 +523,8 @@
     gathered[z, 64:, :768] = jnp.where(top, gain_two, 0.0).astype(BF)
     gathered[z, 64:, 768:] = jnp.zeros((16, 128), BF)
     spread_rows(wires, gathered, y, e, z)()
+    walk.pass_on(0)
+    walk.pass_on(1)
     attn_grad = gathered[:, :64, :768].reshape(256, 768)
     attended_grad = mm(attn_grad, w[:, OUT]).astype(BF)
     for s in range(2):
@@ -736,8 +565,8 @@
             send.start()
 
         far.append((k, takes, send))
-    grad_os[:, :192] = t_mm(attn_grad, attended[...]).astype(BF)
-    grad_os[:, 192:] = t_mm(rows_in, gathered[:, :64, 768:].reshape(256, 128)).astype(BF)[:, 64:]
+    keep(OUT, t_mm(attn_grad, attended[...]))
+    router_grad = t_mm(rows_in, gathered[:, :64, 768:].reshape(256, 128))
     lin[:, :384] = dkv[e].astype(F32)
     lin[:, 576:] = jnp.zeros((256, 64), F32)
 
@@ -756,7 +585,7 @@
     lin_grad = turned(lin[...], two(cos[...]), -two(sin[...])).astype(BF)
     part[...] = mm_t(lin_grad, w[:, QKV]).astype(BF).reshape(4, 64, 768)
     summed = sum_rows(wires, part, land, y, e, z)
-    grad_qkv[...] = t_mm(normed[...], lin_grad).astype(BF)
+    keep(QKV, t_mm(normed[...], lin_grad))
     back_norm, gain_one = rms_back(own[...], gains[0:1], summed())
     result = down_own[...] + back_norm
     down_own[...] = result
@@ -766,8 +595,11 @@
     down_stream[...] = tail[:, :64]
     one = jnp.sum(tail[:, 64:].astype(F32).reshape(64, 768), axis=0, keepdims=True)
     both = jnp.sum(gathered[:, 64:, :768].astype(F32).reshape(64, 768), axis=0, keepdims=True)
-    at_row = lax.broadcasted_iota(jnp.int32, (8, 768), 0)
-    grad_gain[...] = jnp.where(at_row == 0, one, jnp.where(at_row == 1, both, 0.0))
+    at_row = lax.broadcasted_iota(jnp.int32, (16, 768), 0)
+    gain_grads = jnp.where(at_row == 0, one, jnp.where(at_row == 1, both, 0.0)).astype(BF)
+    spot = (lanes((16, 128)) == lax.broadcasted_iota(jnp.int32, (16, 128), 0) + GAIN).astype(BF)
+    keep(slice(192, 256), (router_grad + t_mm(gain_grads, spot))[:, 64:])
+    walk.finish()
     wires.finish()
 
 
@@ -794,8 +626,184 @@
 ]
 
 
+def scatter_kernel(
+    grads0, grads1, o_q, o_k, o_v, o_o, o_small, o_gate, o_up, o_down,
+    acc, sib_land, plus_far, minus_far, plus_near, minus_near, one_far, one_near, total, other, local, sends, recvs,
+):
+    y, x, c, z = place()
+
+    def at(j, d, core):
+        yy = (y + j * core + d * (1 - core) + 8) % 4
+        xx = (x + j * (1 - core) + d * core + 8) % 4
+        return yy, xx
+
+    def who(j, d):
+        yy, xx = at(j, d, c)
+        return device(yy, xx, c, z)
+
+    def chip(j, d, core):
+        yy, xx = at(j, d, core)
+        return yy * 4 + xx
+
+    sibling = device(y, x, 1 - c, z)
+    mine = [pltpu.make_async_copy(grads, acc, local) for grads in (grads0, grads1)]
+    for core in range(2):
+        pl.when(c == core)(mine[core].start)
+    meet([who(1, 0), who(-1, 0), who(0, 1), who(0, -1), sibling], 5)
+    wires = Wires(sends, recvs)
+    order = [(j, d) for d in (2, 1, -1, 0) for j in (0, -1, 1, 2)]
+    swapped = {}
+    for n, (j, d) in enumerate(order):
+        block = chip(j, d, 1 - c)
+        at_sem = wires.used
+        wires.used += 1
+        for core, grads in enumerate((grads1, grads0)):
+            copy = wires.plan(grads.at[block], sib_land.at[n], sibling, c == core, at_sem)
+            pl.when(c == core)(copy.start)
+        swapped[j, d] = copy
+    for core in range(2):
+        pl.when(c == core)(mine[core].wait)
+
+    def join(j, d):
+        n = order.index((j, d))
+        swapped[j, d].wait_recv()
+        block = chip(j, d, c)
+        acc[block] = (acc[block].astype(F32) + sib_land[n].astype(F32)).astype(BF)
+        return acc.at[block]
+
+    plus_set, minus_set = (0, -1), (1, 2)
+    far, near, held = {}, {}, {}
+    for j in (0, 1, -1, 2):
+        ref = join(j, 2)
+        if j in plus_set:
+            far[j] = wires.go(ref, plus_far.at[plus_set.index(j)], who(0, 1))
+        else:
+            far[j] = wires.go(ref, minus_far.at[minus_set.index(j)], who(0, -1))
+    for j, k in ((1, 0), (2, -1)):
+        near[j, 1] = wires.go(join(j, 1), plus_near.at[j], who(0, 1))
+        near[k, -1] = wires.go(join(k, -1), minus_near.at[k % 4], who(0, -1))
+    for j, k in zip(plus_set, minus_set):
+        ref = join(j, 1)
+        far[j].wait_recv()
+        ref[...] = (ref[...].astype(F32) + plus_far[plus_set.index(j)].astype(F32)).astype(BF)
+        near[j, 1] = wires.go(ref, plus_near.at[j % 4], who(0, 1))
+        ref = join(k, -1)
+        far[k].wait_recv()
+        ref[...] = (ref[...].astype(F32) + minus_far[minus_set.index(k)].astype(F32)).astype(BF)
+        near[k, -1] = wires.go(ref, minus_near.at[k], who(0, -1))
+    for j in (2, 1, -1, 0):
+        held[j] = join(j, 0)
+    for j in (2, 1, -1, 0):
+        ref = held[j]
+        near[j, 1].wait_recv()
+        near[j, -1].wait_recv()
+        ref[...] = (ref[...].astype(F32) + plus_near[j % 4].astype(F32) + minus_near[j % 4].astype(F32)).astype(BF)
+        if j == 2:
+            a = wires.go(ref.at[pl.ds(0, 32)], one_far.at[pl.ds(0, 32)], who(1, 0))
+            b = wires.go(ref.at[pl.ds(32, 16)], one_far.at[pl.ds(32, 16)], who(-1, 0))
+    a.wait_recv()
+    up = held[1].at[pl.ds(0, 32)]
+    up[...] = (up[...].astype(F32) + one_far[:32].astype(F32)).astype(BF)
+    last_plus = wires.go(held[1], one_near.at[0], who(1, 0))
+    b.wait_recv()
+    down = held[-1].at[pl.ds(32, 16)]
+    down[...] = (down[...].astype(F32) + one_far[32:].astype(F32)).astype(BF)
+    last_minus = wires.go(held[-1], one_near.at[1], who(-1, 0))
+    last_plus.wait_recv()
+    last_minus.wait_recv()
+    total[...] = held[0][...].astype(F32) + one_near[0].astype(F32) + one_near[1].astype(F32)
+    trade = wires.go(total.at[pl.ds(pl.multiple_of(24 - 24 * c, 8), 24)], other, sibling)
+    spots = (
+        (o_o, OUT), (o_small, slice(128, 256)), (o_k, slice(256, 448)), (o_v, slice(448, 640)), (o_q, slice(640, 832)),
+        (o_gate, GATE), (o_up, UP), (o_down, DOWN),
+    )
+    own = total[pl.ds(pl.multiple_of(24 * c, 8), 24)]
+    for ref, columns in spots:
+        ref[c] = own[:, columns]
+    trade.wait_recv()
+    for ref, columns in spots:
+        ref[1 - c] = other[:, columns]
+    wires.finish()
+
+
+def scatter_grads(grads):
+    chunk = lambda n: pltpu.VMEM((n, CHUNK, WIDE), BF)
+    widths = (192, 192, 192, 192, 128, 512, 512, 512)
+    return pl.pallas_call(
+        scatter_kernel,
+        out_shape=[jax.ShapeDtypeStruct((2, 24, width), F32) for width in widths],
+        in_specs=[ANY] * 2,
+        out_specs=[VM] * 8,
+        scratch_shapes=[
+            chunk(16),
+            chunk(16),
+            chunk(2),
+            chunk(2),
+            chunk(4),
+            chunk(4),
+            pltpu.VMEM((CHUNK, WIDE), BF),
+            chunk(2),
+            pltpu.VMEM((CHUNK, WIDE), F32),
+            pltpu.VMEM((24, WIDE), F32),
+            pltpu.SemaphoreType.DMA,
+            pltpu.SemaphoreType.DMA((40,)),
+            pltpu.SemaphoreType.DMA((40,)),
+        ],
+        compiler_params=pltpu.CompilerParams(
+            collective_id=1, has_side_effects=True, vmem_limit_bytes=48 * 2**20
+        ),
+        name="scatter_grads",
+    )(*grads)
+
+
+def expert_kernel(rows, grads, eg, eu, ed, *rest):
+    g_gate, g_up, g_down, hidden, gu = rest[-5:]
+    weights = jnp.concatenate([eg[...], eu[...]], axis=1)
+
+    def piece(n, carry):
+        some = pl.ds(pl.multiple_of(n * 256, 256), 256)
+        both = mm(rows[n], weights)
+        gate, up = both[:, :256], both[:, 256:]
+        hidden_grad = mm_t(grads[n], ed[...])
+        s = sigmoid(gate)
+        silu = gate * s
+        hidden[some] = (silu * up).astype(BF)
+        gu[some, :256] = (hidden_grad * up * (s * (1.0 + gate * (1.0 - s)))).astype(BF)
+        gu[some, 256:] = (hidden_grad * silu).astype(BF)
+        return carry
+
+    lax.fori_loop(0, 4, piece, 0)
+    both = t_mm(rows[...].reshape(1024, 768), gu[...])
+    g_gate[...] = both[:, :256]
+    g_up[...] = both[:, 256:]
+    g_down[...] = t_mm(hidden[...], grads[...].reshape(1024, 768))
+
+
+def expert_grads(layer, rows, grads, eg, eu, ed, before=None):
+    whole = pl.BlockSpec((None, 4, 256, 768), lambda i, f: (i, 0, 0, 0))
+    wide = pl.BlockSpec((None, None, 768, 256), lambda i, f: (layer, i, 0, f))
+    tall = pl.BlockSpec((None, None, 256, 768), lambda i, f: (layer, i, f, 0))
+    before = [] if before is None else list(before)
+    return pl.pallas_call(
+        expert_kernel,
+        grid=(2, 2),
+        out_shape=[
+            jax.ShapeDtypeStruct((2, 2, 768, 512), F32),
+            jax.ShapeDtypeStruct((2, 2, 768, 512), F32),
+            jax.ShapeDtypeStruct((2, 2, 512, 768), F32),
+        ],
+        in_specs=[whole, whole, wide, wide, tall] + [ANY] * len(before),
+        out_specs=[wide, wide, tall],
+        scratch_shapes=[pltpu.VMEM((1024, 256), BF), pltpu.VMEM((1024, 512), BF)],
+        input_output_aliases={5 + n: n for n in range(len(before))},
+        compiler_params=pltpu.CompilerParams(vmem_limit_bytes=40 * 2**20),
+        cost_estimate=pl.CostEstimate(flops=9_700_000_000, bytes_accessed=20_000_000, transcendentals=2_000_000),
+        name=f"expert_grads_{layer}",
+    )(rows, grads, eg, eu, ed, *before)
+
+
 def forward(layer, stream, own, lengths, route, cos, sin, w, eg, eu, ed):
-    out = SAVED + [((2, 256, 768), BF), ((64, 768), F32), (ROWS4, BF)]
+    out = SAVED + [((2, 4, 256, 768), BF), ((64, 768), F32), (ROWS4, BF)]
     return pl.pallas_call(
         functools.partial(forward_kernel, layer),
         out_shape=[jax.ShapeDtypeStruct(*one) for one in out],
@@ -808,8 +816,8 @@
             pltpu.VMEM((16, 32, 768), BF),
             pltpu.VMEM((2, 256, 768), BF),
             pltpu.SemaphoreType.DMA((4,)),
-            pltpu.SemaphoreType.DMA((48,)),
-            pltpu.SemaphoreType.DMA((48,)),
+            pltpu.SemaphoreType.DMA((64,)),
+            pltpu.SemaphoreType.DMA((64,)),
         ],
         compiler_params=pltpu.CompilerParams(
             collective_id=3 + layer, has_side_effects=True, vmem_limit_bytes=52 * 2**20
@@ -820,9 +828,9 @@
 
 def backward(layer, incoming, grad_own, own, saved, route, cos, sin, w, eg, eu, ed):
     normed, queries, kv, probs, attended, middle, ffn_in, gud, gue, ret, shares = saved
-    out = [((768, width), BF) for width in WIDTHS] + [
-        ((8, 768), F32),
-        ((2, 256, 768), BF),
+    out = [
+        ((16, CHUNK, WIDE), BF),
+        ((2, 4, 256, 768), BF),
         ((64, 768), F32),
         (ROWS4, BF),
     ]
@@ -847,18 +855,14 @@
             pltpu.VMEM((3, 256, 384), BF),
             pltpu.VMEM((256, 640), F32),
             pltpu.SemaphoreType.DMA((4,)),
-            pltpu.SemaphoreType.DMA((56,)),
-            pltpu.SemaphoreType.DMA((56,)),
+            pltpu.SemaphoreType.DMA((64,)),
+            pltpu.SemaphoreType.DMA((64,)),
         ],
         compiler_params=pltpu.CompilerParams(
             collective_id=5 + layer, has_side_effects=True, vmem_limit_bytes=56 * 2**20
         ),
         name=f"block_backward_{layer}",
     )(incoming, grad_own, own, middle, normed, queries, kv, probs, attended, ffn_in, gud, gue, ret, shares, route, cos, sin, w, eg, eu, ed)
-
-
-def swish_product(gate, up):
-    return jax.nn.silu(gate) * up
 
 
 def rotation(span):
@@ -913,40 +917,27 @@
     outputs = stream
     grad = cotangent.reshape(ROWS4)
     grad_own = mine(cotangent)
-    parts, gains, backs = [None, None], [None, None], [None, None]
+    parts, results = [None, None], None
     for layer in (1, 0):
-        *parts[layer], gains[layer], backs[layer], grad_own, grad = backward(
+        parts[layer], back, grad_own, grad = backward(
             layer, grad, grad_own, owns[layer], saved[layer], routes[layer], cos, sin, w, *experts
         )
-    first, second, third, g_down = scatter_grads(parts[0] + parts[1] + gains)
-    rows0, rows1, back0, back1 = gather_rows(rows_at + backs)
-    columns = ([], [], [])
-    for layer, (all_rows, all_back) in enumerate(((rows0, back0), (rows1, back1))):
-        all_rows = all_rows.reshape(2, 1024, 768)
-        all_back = all_back.reshape(2, 1024, 768)
-        gate = jnp.einsum("ecd,edf->ecf", all_rows, expert_gate[layer], preferred_element_type=F32)
-        up = jnp.einsum("ecd,edf->ecf", all_rows, expert_up[layer], preferred_element_type=F32)
-        hidden = swish_product(gate, up).astype(BF)
-        hidden_grad = jnp.einsum("ecd,efd->ecf", all_back, expert_down[layer], preferred_element_type=F32)
-        gate_grad, up_grad = jax.vjp(swish_product, gate, up)[1](hidden_grad)
-        gate_grad, up_grad = gate_grad.astype(BF), up_grad.astype(BF)
-        columns[0].append(jnp.einsum("ecd,ecf->edf", all_rows, gate_grad, preferred_element_type=F32))
-        columns[1].append(jnp.einsum("ecd,ecf->edf", all_rows, up_grad, preferred_element_type=F32))
-        columns[2].append(jnp.einsum("ecf,ecd->efd", hidden, all_back, preferred_element_type=F32))
+        results = expert_grads(layer, rows_at[layer], back, *experts, before=results)
+    g_q, g_k, g_v, g_o, g_small, g_gate, g_up, g_down = scatter_grads(parts)
     return (
         outputs.reshape(2, 128, 768).astype(F32),
         grad.reshape(2, 128, 768).astype(F32),
-        first[:, :, 208],
-        second[:, :, 384:576],
-        second[:, :, 0:192],
-        second[:, :, 192:384],
-        first[:, :, 0:192],
-        first[:, :, 209],
-        first[:, :, 192:208],
-        third[:, :, :512],
-        third[:, :, 512:],
+        g_small[:, :, GAIN],
+        g_q,
+        g_k,
+        g_v,
+        g_o,
+        g_small[:, :, GAIN + 1],
+        g_small[:, :, ROUTER : ROUTER + 16],
+        g_gate,
+        g_up,
         g_down,
-        *[jnp.stack(column) for column in columns],
+        *results,
     )
 
 

time: 566 us -> 459 us (0.81)
  matrix products: 55.5 us -> 0 us
  Pallas kernels: 466 us -> 423 us
  other arithmetic: 16.5 us -> 7.37 us
    dot_general x12 -> x0, matrix products: 55.5 us -> none  [the longest x2 13 us: shards(): jnp.einsum('ecd,ecf->edf', all_rows, gate_grad, preferred_element_type=F32)]
    pallas_call x1 -> x2, Pallas kernels: 87.7 us -> 32.6 us  [expert_grads(): pl.pallas_call(expert_kernel, grid=(2, 2), out_shape=[jax.ShapeDtypeStruc...]
    another operation x3 -> x0, other arithmetic: 10.1 us -> none  [shards(): jnp.stack(column)]
    unnamed x66 -> x61, local copies, waits for them, and re-layouts: 9.15 us -> 19.2 us
    pallas_call x2, Pallas kernels: 143 us -> 152 us  [forward(): pl.pallas_call(functools.partial(forward_kernel, layer), out_shape=[jax.S...]
    pallas_call x2, Pallas kernels: 165 us -> 172 us  [backward(): pl.pallas_call(functools.partial(backward_kernel, layer), out_shape=[jax....]
where the time goes in v3:
time: 459 us; the launch traced here: 456 us
  Pallas kernels  423 us (92%)
  local copies, waits for them, and re-layouts  24.4 us (5%)
  other arithmetic  7.37 us (2%)
    pallas_call x2, Pallas kernels, backward(): pl.pallas_call(functools.partial(backward_kernel, layer), out_shape=[jax....  172 us
    pallas_call x2, Pallas kernels, forward(): pl.pallas_call(functools.partial(forward_kernel, layer), out_shape=[jax.S...  152 us
    pallas_call x1, Pallas kernels, gather_weights(): pl.pallas_call(gather_kernel, out_shape=jax.ShapeDtypeStruct((2, 768, WID...  34.5 us
    pallas_call x2, Pallas kernels, expert_grads(): pl.pallas_call(expert_kernel, grid=(2, 2), out_shape=[jax.ShapeDtypeStruc...  32.6 us
    pallas_call x1, Pallas kernels, scatter_grads(): pl.pallas_call(scatter_kernel, out_shape=[jax.ShapeDtypeStruct((2, 24, wi...  31.9 us
    unnamed x61, local copies, waits for them, and re-layouts  19.2 us

profile of v3, /device:TPU:1, one launch (start us, length us, event | category | flops | bytes accessed | tf_op | source)
XLA Modules:
  0.0 456.0 jit_solution(4370710334726805057)
XLA Ops:
  0.7 0.7 broadcast_in_dim.11.lengths
  1.4 0.1 pad.1.clone
  1.5 0.1 pad.7.clone
  1.6 0.1 pad.3.clone
  1.6 0.1 pad.9.clone
  1.7 0.7 compare_select_fusion
  2.4 0.7 pad_add_fusion
  3.1 0.8 concatenate.55
  3.9 0.8 concatenate.56
  4.7 0.8 copy.59
  5.4 0.1 fusion
  5.6 0.1 copy.55
  5.7 0.1 copy.57
  5.8 0.1 copy.65
  6.0 0.0 copy-start.7
  6.0 0.1 copy.64
  6.1 0.0 copy-start.6
  6.2 1.1 concatenate.54.src
  7.3 0.0 copy-start.2
  7.3 0.0 copy-start.3
  7.3 1.8 dynamic-slice_convert_fusion
  9.2 34.5 %gather_weights.1.w_all = bf16[2,768,2432]{2,1,0:T(8,128)(2,1)} custom-call(bf16[48,2432]{1,0:T(8,128)(2,1)S(1)} %concatenate.54.src), custom_call_target="tpu_custom_call" | custom-call | tf_op jit(solution)/shard_map/gather_weights/pallas_call | solution.py:137
  43.6 0.0 copy-done.6
  43.7 0.0 copy-done.5
  43.7 74.9 %block_forward_0.1 = (bf16[256,768]{1,0:T(8,128)(2,1)}, bf16[256,192]{1,0:T(8,128)(2,1)S(1)}, bf16[8,256,384]{2,1,0:T(8,128)(2,1)}, bf16[6,128,1024]{2,1,0:T(8,1...) custom-call(bf16[4,64,768]{2,1,0:T(8,128)(2,1)} %bitcast.36, ...), custom_call_target="tpu_custom_call" | custom-call | tf_op jit(solution)/shard_map/block_forward_0/pallas_call | solution.py:807
  118.6 0.0 copy-start.9
  118.6 0.7 copy-done.9
  119.3 0.7 copy-done.11
  119.9 0.0 copy-done.7
  120.0 0.0 copy-done.2
  120.0 0.0 copy-done.3
  120.0 77.2 %block_forward_1.1 = (bf16[256,768]{1,0:T(8,128)(2,1)}, bf16[256,192]{1,0:T(8,128)(2,1)S(1)}, bf16[8,256,384]{2,1,0:T(8,128)(2,1)}, bf16[6,128,1024]{2,1,0:T(8,1...) custom-call(bf16[4,64,768]{2,1,0:T(8,128)(2,1)} %get-tuple-element.6, ...), custom_call_target="tpu_custom_call" | custom-call | tf_op jit(solution)/shard_map/block_forward_1/pallas_call | solution.py:807
  197.2 0.0 copy-done.8
  197.3 0.7 copy-done.10
  197.9 0.7 copy-done.14
  198.6 0.7 copy-done.16
  199.2 2.0 bitcast_convert_fusion.1
  201.2 0.0 copy-done.15
  201.2 91.9 %block_backward_1.1 = (bf16[16,48,2432]{2,1,0:T(8,128)(2,1)}, bf16[2,4,256,768]{3,2,1,0:T(8,128)(2,1)}, f32[64,768]{1,0:T(8,128)}, bf16[4,64,768]{2,1,0:T(8,128)(2,1)}) custom-call(bf16[4,64,768]{2,1,0:T(8,128)(2,1)} %bitcast.38, f32[64,768]{1,0:T(8,128)} %get-tuple-element.163.grad_own, f32[64,768]{1,0:T(8,128)} %copy-done.8, f32[64,768]{1,0:T(8,128)} %copy-done.10, ...), custom_call_target="tpu_custom_call" | custom-call | tf_op jit(solution)/shard_map/block_backward_1/pallas_call | solution.py:837
  293.1 80.0 %block_backward_0.1 = (bf16[16,48,2432]{2,1,0:T(8,128)(2,1)}, bf16[2,4,256,768]{3,2,1,0:T(8,128)(2,1)}, f32[64,768]{1,0:T(8,128)}, bf16[4,64,768]{2,1,0:T(8,128)(2,1)}) custom-call(bf16[4,64,768]{2,1,0:T(8,128)(2,1)} %get-tuple-element.77.incoming, f32[64,768]{1,0:T(8,128)} %get-tuple-element.78.grad_own, f32[64,768]{1,0:T(8,128)} %copy-done.5, ...), custom_call_target="tpu_custom_call" | custom-call | tf_op jit(solution)/shard_map/block_backward_0/pallas_call | solution.py:837
  373.1 0.0 copy-start.4
  373.1 2.0 copy-done.4
  375.2 31.9 %scatter_grads.1 = (f32[2,24,192]{2,1,0:T(8,128)S(1)}, f32[2,24,192]{2,1,0:T(8,128)S(1)}, f32[2,24,192]{2,1,0:T(8,128)S(1)}, f32[2,24,192]{2,1,0:T(8,128)S(1)}, ...) custom-call(bf16[16,48,2432]{2,1,0:T(8,128)(2,1)S(1)} %copy-done.4, ...), custom_call_target="tpu_custom_call" | custom-call | tf_op jit(solution)/shard_map/scatter_grads/pallas_call | solution.py:732
  407.1 0.0 copy-start.17
  407.1 0.6 copy-done.17
  407.7 0.6 copy-done.19
  408.4 0.7 slice_reduce_fusion
  409.1 0.7 slice.33
  409.8 1.4 copy.63
  411.2 1.9 bitcast_convert_fusion
  413.1 1.9 copy-done.1
  415.0 1.9 copy-done.22
  416.9 1.9 copy-done.23
  418.8 16.3 %expert_grads_1.1 = (f32[2,2,768,512]{3,2,1,0:T(8,128)}, f32[2,2,768,512]{3,2,1,0:T(8,128)}, f32[2,2,512,768]{3,2,1,0:T(8,128)}) custom-call(bf16[2,4,256,768]{3,2,1,0:T(8,128)(2,1)S(1)} %copy-done.22, bf16[2,4,256,768]{3,2,1,0:T(8,128)(2,1)S(1)} %copy-done.23, bf16[2,2,768,512]{3,2,1,0:T(8,128)(2,1)S(1)} %copy-done, bf16[2,2,768,512]{3,2,1,0:T(8,128)(2,1)S(1)} %copy-done.1, ...), custom_call_target="tpu_custom_call" | custom-call | flops 9699999744 | bytes 20000000 | tf_op jit(solution)/shard_map/expert_grads_1/pallas_call | solution.py:787
  435.1 0.0 copy-start.18
  435.2 16.2 %expert_grads_0.1 = (f32[2,2,768,512]{3,2,1,0:T(8,128)}, f32[2,2,768,512]{3,2,1,0:T(8,128)}, f32[2,2,512,768]{3,2,1,0:T(8,128)}) custom-call(bf16[2,4,256,768]{3,2,1,0:T(8,128)(2,1)S(1)} %copy-done.21, bf16[2,4,256,768]{3,2,1,0:T(8,128)(2,1)S(1)} %copy-done.24, ...), custom_call_target="tpu_custom_call", output_to_operand_aliasing={{0}: (5, {}), {1}: (6, {}), {2}: (7, {})} | custom-call | flops 9699999744 | bytes 20000000 | tf_op jit(solution)/shard_map/expert_grads_0/pallas_call | solution.py:787
  451.4 0.0 copy-done.20
  451.4 0.6 copy.76
  452.0 0.6 copy.77
  452.6 0.6 copy.78
  453.2 0.6 copy.79
  453.9 0.6 copy.80
  454.5 0.6 copy.81
  455.1 0.6 copy.82
  (36 shorter events, 0.2 us)
Async XLA Ops:
  6.0 114.0 %copy-start.7 = (s32[1,256,4]{2,1,0:T(8,128)}, s32[1,256,4]{2,1,0:T(8,128)S(1)}, u32[]{:S(2)}) copy-start(s32[1,256,4]{2,1,0:T(8,128)S(1)} %copy.65) | copy-start | bytes 12292
  6.1 37.5 %copy-start.6 = (s32[1,256,4]{2,1,0:T(8,128)}, s32[1,256,4]{2,1,0:T(8,128)S(1)}, u32[]{:S(2)}) copy-start(s32[1,256,4]{2,1,0:T(8,128)S(1)} %copy.64) | copy-start | bytes 12292
  7.3 112.7 %copy-start.2 = (f32[128,640]{1,0:T(8,128)}, f32[128,640]{1,0:T(8,128)S(1)}, u32[]{:S(2)}) copy-start(f32[128,640]{1,0:T(8,128)S(1)} %maximum_maximum_fusion.1.sin) | copy-start | bytes 983044
  7.3 112.7 %copy-start.3 = (f32[128,640]{1,0:T(8,128)}, f32[128,640]{1,0:T(8,128)S(1)}, u32[]{:S(2)}) copy-start(f32[128,640]{1,0:T(8,128)S(1)} %maximum_maximum_fusion.cos) | copy-start | bytes 983044
  9.2 34.5 %copy-start.5 = (f32[64,768]{1,0:T(8,128)}, f32[64,768]{1,0:T(8,128)S(1)}, u32[]{:S(2)}) copy-start(f32[64,768]{1,0:T(8,128)S(1)} %get-tuple-element.164.own) | copy-start | bytes 589828
  118.6 0.7 copy-start.9
  119.3 0.7 copy-start.11
  119.9 77.3 %copy-start.8 = (f32[64,768]{1,0:T(8,128)}, f32[64,768]{1,0:T(8,128)S(1)}, u32[]{:S(2)}) copy-start(f32[64,768]{1,0:T(8,128)S(1)} %get-tuple-element.64.own) | copy-start | bytes 589828
  119.9 77.3 %copy-start.12 = (bf16[256,192]{1,0:T(8,128)(2,1)}, bf16[256,192]{1,0:T(8,128)(2,1)S(1)}, u32[]{:S(2)}) copy-start(bf16[256,192]{1,0:T(8,128)(2,1)S(1)} %get-tuple-element.84.attended) | copy-start | bytes 294916
  119.9 77.3 %copy-start.13 = (f32[256,128]{1,0:T(8,128)}, f32[256,128]{1,0:T(8,128)S(1)}, u32[]{:S(2)}) copy-start(f32[256,128]{1,0:T(8,128)S(1)} %get-tuple-element.89.shares) | copy-start | bytes 393220
  197.3 0.7 copy-start.10
  197.9 0.7 copy-start.14
  198.6 0.7 copy-start.16
  199.2 2.0 copy-start.15
  373.1 2.1 copy-start.4
  375.2 37.9 %copy-start = (bf16[2,2,768,512]{3,2,1,0:T(8,128)(2,1)S(1)}, bf16[2,2,768,512]{3,2,1,0:T(8,128)(2,1)}, u32[]{:S(2)}) copy-start(bf16[2,2,768,512]{3,2,1,0:T(8,128)(2,1)} %eg.3) | copy-start | bytes 9437188
  407.1 0.6 copy-start.17
  407.7 0.6 copy-start.19
  413.1 1.9 copy-start.1
  415.0 1.9 copy-start.22
  416.9 1.9 copy-start.23
  418.8 16.3 %copy-start.21 = (bf16[2,4,256,768]{3,2,1,0:T(8,128)(2,1)S(1)}, bf16[2,4,256,768]{3,2,1,0:T(8,128)(2,1)}, u32[]{:S(2)}) copy-start(bf16[2,4,256,768]{3,2,1,0:T(8,128)(2,1)} %get-tuple-element.101.rows) | copy-start | bytes 9437188
  418.8 16.3 %copy-start.24 = (bf16[2,4,256,768]{3,2,1,0:T(8,128)(2,1)S(1)}, bf16[2,4,256,768]{3,2,1,0:T(8,128)(2,1)}, u32[]{:S(2)}) copy-start(bf16[2,4,256,768]{3,2,1,0:T(8,128)(2,1)} %get-tuple-element.102.grads) | copy-start | bytes 9437188
  435.1 16.2 %copy-start.20 = (f32[2,24,192]{2,1,0:T(8,128)S(1)}, f32[2,24,192]{2,1,0:T(8,128)}, u32[]{:S(2)}) copy-start(f32[2,24,192]{2,1,0:T(8,128)} %copy-done.19) | copy-start | bytes 110596
  435.1 16.9 %copy-start.18 = (f32[2,24,192]{2,1,0:T(8,128)S(1)}, f32[2,24,192]{2,1,0:T(8,128)}, u32[]{:S(2)}) copy-start(f32[2,24,192]{2,1,0:T(8,128)} %copy-done.17) | copy-start | bytes 110596
